TPU v7x, 32 devices: a whole 2x2x4 slice. The times are simulated.
32 devices in a mesh: modes: 16 (over z, y, core), dom: 2 (over x).
Axes of the slice: x: 2, y: 2, z: 4, core: 2. Of those that a mesh axis runs over, the one named last changes fastest.
Arguments:
- velocity: float32 [3, 256, 81, 256], P(None, 'modes', None, 'dom'), may hold values from -6 to 6
- slot_of_cell: int32 [2, 128], P('dom'), may hold values from 0 to 127, each once within a row
- elem_mats: float32 [4, 81, 81], replicated, may hold values from -0.625 to 0.625
- geometry: float32 [4, 256], P(None, 'dom'), may hold values from 0.5 to 2
Outputs:
- result: float32 [3, 256, 81, 256], P(None, 'modes', None, 'dom')
Inputs may be any that keep to these rules, and one draw needn't show every extreme that they name: `slot_of_cell`: each row is a permutation of the slots 0 to 127.
All inputs are finite; a program needn't handle non-finite values.
Results may differ from a plain program's by a relative error of at most 0.0003.
Values sent between devices are 32-bit elements; how exact they have to be, the bound alone decides.
No kernel may reach another device: no remote copies, remote signals or barrier semaphores. Data moves between devices by JAX's collectives and lax.ppermute only.
A program may use at most 128 MiB of HBM per device.

v0:
```python
import math

import jax
import jax.numpy as jnp
from jax import lax
from jax.sharding import PartitionSpec as P

EX = 16
EY = 8


def padded(block, sides, width):
    for axis, dim in sides:
        count = lax.axis_size(axis)
        forward = [(i, i + 1) for i in range(count - 1)]
        forward.append((count - 1, 0))
        backward = [(target, source) for source, target in forward]
        low = lax.ppermute(
            lax.slice_in_dim(block, block.shape[dim] - width, None, axis=dim), axis, forward
        )
        high = lax.ppermute(lax.slice_in_dim(block, 0, width, axis=dim), axis, backward)
        block = jnp.concatenate([low, block, high], axis=dim)
    return block


def tables(length):
    indices = jnp.arange(length, dtype=jnp.int32)
    halfway = length // 2
    wavenum = jnp.where(indices <= halfway, indices, indices - halfway)
    phases = wavenum[:, None] * indices[None, :] % length
    angles = phases.astype(jnp.float32) * jnp.float32(2.0 * math.pi / length)
    forward = jnp.where((indices <= halfway)[:, None], jnp.cos(angles), jnp.sin(angles))
    weights = jnp.where(
        (indices == 0) | (indices == halfway), jnp.float32(1.0 / length), jnp.float32(2.0 / length)
    )
    inverse = (forward * weights[:, None]).T
    helm_shift = 1.0 + (8.0 * wavenum.astype(jnp.float32) / length) ** 2
    return (forward, inverse, helm_shift)


def assemble(values, slot_of_cell):
    depth = values.shape[1]
    per_part = values.shape[3]
    order = slot_of_cell[0]
    picked = jnp.take(values, order, axis=3)
    cells_grid = picked.reshape(3, depth, 9, 9, EX, EY)
    left_face = cells_grid[:, :, 0, :, 0]
    right_face = cells_grid[:, :, 8, :, EX - 1]
    extended = padded(jnp.stack([left_face, right_face]), (("dom", 0),), 1)
    interior = cells_grid[:, :, 8, :, :-1] + cells_grid[:, :, 0, :, 1:]
    right_sum = right_face + extended[3]
    left_sum = left_face + extended[0]
    cells_grid = cells_grid.at[:, :, 8].set(
        jnp.concatenate([interior, right_sum[:, :, :, None]], axis=3)
    )
    cells_grid = cells_grid.at[:, :, 0].set(
        jnp.concatenate([left_sum[:, :, :, None], interior], axis=3)
    )
    across = cells_grid[:, :, :, 8, :, :-1] + cells_grid[:, :, :, 0, :, 1:]
    cells_grid = cells_grid.at[:, :, :, 8, :, :-1].set(across).at[:, :, :, 0, :, 1:].set(across)
    flat = cells_grid.reshape(3, depth, 81, per_part)
    inverse_slot = jnp.zeros_like(order).at[order].set(jnp.arange(per_part, dtype=jnp.int32))
    return jnp.take(flat, inverse_slot, axis=3)


def to_pencil(products):
    return lax.all_to_all(products, "modes", split_axis=3, concat_axis=1, tiled=True)


def to_planes(physical):
    return lax.all_to_all(physical, "modes", split_axis=1, concat_axis=3, tiled=True)


def local(velocity, slot_of_cell, elem_mats, geometry):
    products = velocity * jnp.roll(velocity, -1, axis=0)
    pencil = to_pencil(products)
    length = pencil.shape[1]
    narrow = pencil.shape[3]
    forward, inverse, helm_shift = tables(length)
    flat = pencil.reshape(3, length, 81 * narrow)
    spectra = jnp.einsum("mp,cpx->cmx", forward, flat, precision=lax.Precision.HIGHEST)
    block_geo = lax.dynamic_slice_in_dim(geometry, lax.axis_index("modes") * narrow, narrow, 1)
    identity = jnp.eye(narrow, dtype=jnp.float32)
    stiff_kron = jnp.einsum(
        "tij,te,ef->iejf", elem_mats[:3], block_geo[:3], identity, precision=lax.Precision.HIGHEST
    ).reshape(81 * narrow, 81 * narrow)
    mass_kron = jnp.einsum(
        "ij,e,ef->iejf", elem_mats[3], block_geo[3], identity, precision=lax.Precision.HIGHEST
    ).reshape(81 * narrow, 81 * narrow)
    stiff_part = jnp.einsum("xy,cmy->cmx", stiff_kron, spectra, precision=lax.Precision.HIGHEST)
    mass_part = jnp.einsum("xy,cmy->cmx", mass_kron, spectra, precision=lax.Precision.HIGHEST)
    applied = stiff_part + helm_shift[:, None] * mass_part
    physical = jnp.einsum("pm,cmx->cpx", inverse, applied, precision=lax.Precision.HIGHEST)
    planes = to_planes(physical.reshape(3, length, 81, narrow))
    return assemble(planes, slot_of_cell)


def solution(mesh):
    in_specs = (P(None, "modes", None, "dom"), P("dom", None), P(), P(None, "dom"))
    out_specs = P(None, "modes", None, "dom")
    return jax.shard_map(local, mesh=mesh, in_specs=in_specs, out_specs=out_specs, check_vma=False)
```

profile of v0, /device:TPU:16, one launch (start us, length us, event | category | flops | bytes accessed | tf_op | source)
XLA Modules:
  0.0 290.7 jit_solution(12288134338118866685)
XLA Ops:
  0.0 2.4 copy.32
  2.4 0.3 slice.212
  2.8 0.1 slice.213
  2.8 2.2 maximum_multiply_fusion
  5.1 6.3 %all-to-all-start = ((f32[3,16,81,128]{2,1,0,3:T(8,128)}), f32[3,16,81,128]{2,1,0,3:T(8,128)S(1)}, u32[]{:S(2)}, u32[]{:S(2)}) async-start(f32[3,16,81,128]{2,1,0,3:T(8,128)} %maximum_multiply_fusion), calls=%async_computation | async-start | bytes 6291456 | tf_op jit(solution)/shard_map/all_to_all | solution.py:67
  11.6 11.6 %multiply_bitcast_fusion = f32[81,8,81,8]{3,2,1,0:T(8,128)} fusion(f32[81,81]{1,0:T(8,128)S(1)} %bitcast.115, f32[8,8]{1,0:T(8,128)S(1)} %fusion.29), kind=kLoop, calls=%fused_computation.3 | loop fusion | flops 419904 | bytes 1706116 | tf_op jit(solution)/shard_map/ij,e,ef->iejf/transpose | solution.py:87
  23.2 17.3 %reshape.349 = f32[648,648,1]{1,0,2:T(8,128)} reshape(f32[81,8,81,8]{3,2,1,0:T(8,128)} %multiply_bitcast_fusion) | data formatting | bytes 3359232 | tf_op jit(solution)/shard_map/reshape | solution.py:89
  40.4 0.5 fusion.25
  40.9 10.3 %multiply_bitcast_fusion.1 = f32[81,8,81,8]{3,2,1,0:T(8,128)} fusion(f32[8,8]{1,0:T(8,128)S(1)} %fusion.30, f32[8,81,81]{2,0,1:T(8,128)S(1)} %fusion.25), kind=kLoop, calls=%fused_computation.4 | loop fusion | flops 419904 | bytes 1889824 | tf_op jit(solution)/shard_map/tij,te,ef->iejf/transpose | solution.py:84
  51.3 17.2 %reshape.348 = f32[648,648,1]{1,0,2:T(8,128)} reshape(f32[81,8,81,8]{3,2,1,0:T(8,128)} %multiply_bitcast_fusion.1) | data formatting | bytes 3359232 | tf_op jit(solution)/shard_map/reshape | solution.py:86
  68.6 12.9 %all-to-all-done = f32[3,16,81,128]{2,1,0,3:T(8,128)S(1)} async-done(((f32[3,16,81,128]{2,1,0,3:T(8,128)}), f32[3,16,81,128]{2,1,0,3:T(8,128)S(1)}, u32[]{:S(2)}, u32[]{:S(2)}) %all-to-all-start) | async-done | bytes 1990688 | tf_op jit(solution)/shard_map/all_to_all | solution.py:67
  81.5 9.5 %copy.34 = f32[3,16,16,81,8]{2,1,4,3,0:T(8,128)} copy(f32[3,16,16,81,8]{3,2,0,4,1:T(8,128)S(1)} %bitcast.112) | data formatting | bytes 3981312 | tf_op jit(solution)/shard_map/all_to_all | solution.py:67
  91.0 11.0 %reshape.306 = f32[3,256,648]{1,2,0:T(8,128)S(1)} reshape(f32[3,16,16,81,8]{2,1,4,3,0:T(8,128)} %copy.34) | data formatting | bytes 3981312 | tf_op jit(solution)/shard_map/reshape | solution.py:80
  102.0 2.9 fusion.19
  104.9 5.3 %fusion = f32[3,256,648]{1,2,0:T(8,128)S(1)} fusion(f32[648,648,1]{1,0,2:T(8,128)S(1)} %copy-done.2, f32[3,648,256]{2,1,0:T(8,128)S(1)} %fusion.19), kind=kOutput, calls=%fused_computation.9 | convolution fusion | flops 3869835264 | bytes 5660928 | tf_op jit(solution)/shard_map/xy,cmy->cmx/dot_general | solution.py:91
  110.2 5.6 %fusion.2 = f32[3,256,648]{1,2,0:T(8,128)S(1)} fusion(f32[648,648,1]{1,0,2:T(8,128)S(1)} %copy-done.3, f32[3,648,256]{2,1,0:T(8,128)S(1)} %fusion.19), kind=kOutput, calls=%fused_computation.11 | convolution fusion | flops 3869835264 | bytes 5660928 | tf_op jit(solution)/shard_map/xy,cmy->cmx/dot_general | solution.py:90
  115.8 2.9 %fusion.11 = f32[3,256,81,8]{1,3,2,0:T(8,128)S(1)} fusion(f32[3,256,648]{1,2,0:T(8,128)S(1)} %fusion.2, f32[3,256,648]{1,2,0:T(8,128)S(1)} %fusion, f32[256]{0:T(256)S(1)} %get-tuple-element.59, f32[256]{0:T(256)S(1)} %get-tuple-element.58, s32[256]{0:T(256)S(1)} %add_select_fusion.1, pred[256]{0:T(512)(128)(4,1)S(1)} %iota_compare_fusion.1), kind=kOutput, calls=%fused_computation.26 | convolution fusion | flops 1530867712 | bytes 5975296 | tf_op jit(solution)/shard_map/pm,cmx->cpx/dot_general | solution.py:93
  118.8 2.3 copy.36
  121.1 4.8 %all-to-all-start.1 = ((f32[3,256,81,8]{2,3,0,1:T(8,128)}), f32[3,256,81,8]{2,3,0,1:T(8,128)S(1)}, u32[]{:S(2)}, u32[]{:S(2)}) async-start(f32[3,256,81,8]{2,3,0,1:T(8,128)} %copy.36), calls=%async_computation.1 | async-start | bytes 6291456 | tf_op jit(solution)/shard_map/all_to_all | solution.py:71
  125.9 0.6 slice.207
  126.5 1.0 scatter_custom_fusion
  127.5 0.8 concatenate.23
  128.3 0.7 and_reduce_fusion
  129.0 67.0 %all-to-all-done.1 = f32[3,256,81,8]{2,3,0,1:T(8,128)S(1)} async-done(((f32[3,256,81,8]{2,3,0,1:T(8,128)}), f32[3,256,81,8]{2,3,0,1:T(8,128)S(1)}, u32[]{:S(2)}, u32[]{:S(2)}) %all-to-all-start.1) | async-done | bytes 1990688 | tf_op jit(solution)/shard_map/all_to_all | solution.py:71
  196.0 0.4 copy.59
  196.4 1.8 copy.39
  198.2 2.4 gather_fusion
  200.6 2.2 select_bitcast_fusion.1
  202.8 9.8 %copy.40 = f32[3,16,81,128]{1,3,2,0:T(8,128)} copy(f32[3,16,81,128]{2,1,0,3:T(8,128)S(1)} %select_bitcast_fusion.1) | data formatting | bytes 3981312 | tf_op jit(solution)/shard_map/jit(_take)/select_n | solution.py:45
  212.6 1.0 slice_bitcast_fusion.3
  213.6 1.6 collective-permute-start
  215.1 2.1 fusion.10
  217.2 0.6 collective-permute-start.1
  217.8 0.5 collective-permute-done
  218.4 0.9 bitcast_add_fusion.1
  219.3 2.7 collective-permute-done.1
  222.1 0.9 fusion.28
  223.0 1.5 fusion.7
  224.4 1.4 fusion.8
  225.9 11.3 %copy.63 = f32[3,16,9,9,16,8]{1,5,4,3,2,0:T(8,128)} copy(f32[3,16,9,9,16,8]{1,5,4,3,2,0:T(8,128)} %fusion.8) | data formatting | bytes 3981312
  237.2 2.3 slice_add_fusion
  239.5 14.5 %scatter.24 = f32[3,16,9,9,16,8]{1,5,4,3,2,0:T(8,128)} dynamic-update-slice(f32[3,16,9,9,16,8]{1,5,4,3,2,0:T(8,128)} %copy.63, f32[3,16,9,1,16,7]{1,5,4,3,2,0:T(8,128)S(1)} %slice_add_fusion, s32[]{:T(128)} %constant.151.clone.1, s32[]{:T(128)} %constant.151.clone.1, s32[]{:T(128)} %constant.151.clone.1, s32[]{:T(128)} %constant.157.clone.1, s32[]{:T(128)} %constant.151.clone.1, s32[]{:T(128)} %constant.151.clone.1) | dynamic-update-slice | bytes 387076 | tf_op jit(solution)/shard_map/scatter | solution.py:60
  254.0 4.4 %dynamic-slice_select_fusion = f32[3,16,9,1,16,7]{1,5,4,3,2,0:T(8,128)S(1)} fusion(f32[3,16,9,9,16,8]{1,5,4,3,2,0:T(8,128)} %scatter.24, s32[]{:T(128)S(1)} %bitcast.117, s32[]{:T(128)} %bitcast.35, pred[]{:T(512)} %and_reduce_fusion, f32[3,16,9,9,16,8]{1,5,4,3,2,0:T(8,128)} %fusion.8), kind=kLoop, calls=%fused_computation.21 | loop fusion | flops 96768 | bytes 774153 | tf_op jit(solution)/shard_map/select.7
  258.4 15.2 %scatter.30 = f32[3,16,9,9,16,8]{1,5,4,3,2,0:T(8,128)} dynamic-update-slice(f32[3,16,9,9,16,8]{1,5,4,3,2,0:T(8,128)} %scatter.24, f32[3,16,9,1,16,7]{1,5,4,3,2,0:T(8,128)S(1)} %dynamic-slice_select_fusion, s32[]{:T(128)} %constant.151.clone.1, s32[]{:T(128)} %constant.151.clone.1, s32[]{:T(128)} %constant.151.clone.1, s32[]{:T(128)S(1)} %bitcast.118, s32[]{:T(128)} %constant.151.clone.1, s32[]{:T(128)} %bitcast.35) | dynamic-update-slice | bytes 387076 | tf_op jit(solution)/shard_map/scatter | solution.py:60
  273.6 10.4 %copy.48 = f32[3,16,81,128]{2,1,3,0:T(8,128)S(1)} copy(f32[3,16,81,128]{1,3,2,0:T(8,128)} %bitcast.111) | data formatting | bytes 3981312 | tf_op jit(solution)/shard_map/reshape | solution.py:61
  284.0 2.4 gather_fusion.1
  286.3 2.2 select_bitcast_fusion
  288.5 2.2 copy.49
  (32 shorter events, 0.3 us)
Async XLA Ops:
  0.0 11.4 %copy-start = (f32[4,128]{1,0:T(4,128)S(1)}, f32[4,128]{1,0:T(4,128)}, u32[]{:S(2)}) copy-start(f32[4,128]{1,0:T(4,128)} %param.17) | copy-start | bytes 6148
  5.0 6.5 %copy-start.4 = (f32[4,81,81]{2,0,1:T(4,128)S(1)}, f32[4,81,81]{2,0,1:T(4,128)}, u32[]{:S(2)}) copy-start(f32[4,81,81]{2,0,1:T(4,128)} %param.16) | copy-start | bytes 314932
  5.1 76.4 %all-to-all-start = ((f32[3,16,81,128]{2,1,0,3:T(8,128)}), f32[3,16,81,128]{2,1,0,3:T(8,128)S(1)}, u32[]{:S(2)}, u32[]{:S(2)}) async-start(f32[3,16,81,128]{2,1,0,3:T(8,128)} %maximum_multiply_fusion), calls=%async_computation | async-start | bytes 6291456 | tf_op jit(solution)/shard_map/all_to_all | solution.py:67
  102.0 2.9 copy-start.2
  104.9 5.3 %copy-start.3 = (f32[648,648,1]{1,0,2:T(8,128)S(1)}, f32[648,648,1]{1,0,2:T(8,128)}, u32[]{:S(2)}) copy-start(f32[648,648,1]{1,0,2:T(8,128)} %reshape.348) | copy-start | bytes 5038852
  121.1 5.4 %copy-start.5 = (s32[1,128]{1,0:T(1,128)S(1)}, s32[1,128]{1,0:T(1,128)}, u32[]{:S(2)}) copy-start(s32[1,128]{1,0:T(1,128)} %param.15) | copy-start | bytes 1540
  121.1 7.2 %copy-start.6 = (s32[6]{0:T(128)S(1)}, s32[6]{0:T(128)}, u32[]{:S(2)}) copy-start(s32[6]{0:T(128)} %constant.164.clone.1) | copy-start | bytes 76
  121.1 74.9 %all-to-all-start.1 = ((f32[3,256,81,8]{2,3,0,1:T(8,128)}), f32[3,256,81,8]{2,3,0,1:T(8,128)S(1)}, u32[]{:S(2)}, u32[]{:S(2)}) async-start(f32[3,256,81,8]{2,3,0,1:T(8,128)} %copy.36), calls=%async_computation.1 | async-start | bytes 6291456 | tf_op jit(solution)/shard_map/all_to_all | solution.py:71
  213.6 4.8 %collective-permute-start = (f32[1,3,16,9,8]{2,4,3,1,0:T(8,128)S(1)}, f32[1,3,16,9,8]{2,4,3,1,0:T(8,128)S(1)}, u32[]{:S(2)}, u32[]{:S(2)}) collective-permute-start(f32[1,3,16,9,8]{2,4,3,1,0:T(8,128)S(1)} %get-tuple-element.55), channel_id=1, source_target_pairs={{1,0},{0,1},{3,2},{2,3},{5,4},{4,5},{7,6},{6,7},{9,8},{8,9},{11,10... | collective-permute-start | bytes 41480 | tf_op jit(solution)/shard_map/ppermute | solution.py:21
  217.2 4.8 %collective-permute-start.1 = (f32[1,3,16,9,8]{2,4,3,1,0:T(8,128)S(1)}, f32[1,3,16,9,8]{2,4,3,1,0:T(8,128)S(1)}, u32[]{:S(2)}, u32[]{:S(2)}) collective-permute-start(f32[1,3,16,9,8]{2,4,3,1,0:T(8,128)S(1)} %get-tuple-element.54), channel_id=1, source_target_pairs={{0,1},{1,0},{2,3},{3,2},{4,5},{5,4},{6,7},{7,6},{8,9},{9,8},{10,11... | collective-permute-start | bytes 41480 | tf_op jit(solution)/shard_map/ppermute | solution.py:18
  286.3 4.4 %copy-start.1 = (f32[4,128]{1,0:T(4,128)S(1)}, f32[4,128]{1,0:T(4,128)}, u32[]{:S(2)}) copy-start(f32[4,128]{1,0:T(4,128)} %param.17) | copy-start | bytes 6148
where the time goes:
time: 293 us; the launch traced here: 291 us
  local copies, waits for them, and re-layouts  134 us (46%)
  waiting for transfers between devices  83.2 us (28%)
  other arithmetic  42.9 us (15%)
  matrix products  17.2 us (6%)
  starting transfers between devices  13.3 us (5%)
    all_to_all x1, waiting for transfers between devices, to_planes(): lax.all_to_all(physical, 'modes', split_axis=1, concat_axis=3, tiled=True)  67 us
    scatter x2, local copies, waits for them, and re-layouts, assemble(): cells_grid.at[:, :, :, 8, :, :-1].set(across).at[:, :, :, 0, :, 1:]  29.7 us
    reshape x1, local copies, waits for them, and re-layouts, local(): mass_kron = jnp.einsum('ij,e,ef->iejf', elem_mats[3], block_geo[3], ident...  17.3 us
    reshape x1, local copies, waits for them, and re-layouts, local(): stiff_kron = jnp.einsum('tij,te,ef->iejf', elem_mats[:3], block_geo[:3],...  17.2 us
    unnamed x17, local copies, waits for them, and re-layouts  13.8 us
    all_to_all x1, waiting for transfers between devices, to_pencil(): lax.all_to_all(products, 'modes', split_axis=3, concat_axis=1, tiled=True)  12.9 us
    transpose x1, other arithmetic, local(): jnp.einsum('ij,e,ef->iejf', elem_mats[3], block_geo[3], identity, precisi...  11.6 us
    reshape x1, local copies, waits for them, and re-layouts, local(): flat = pencil.reshape(3, length, 81 * narrow)  11 us
  transfers between devices with their start and end apart: 4, of which 4 were waited for; matrix products, arithmetic and copies ran while one was open for 22% of the time, Pallas kernels for 0%

commit v1 on v0

v1 whole, which is shorter than its diff:
```python
import functools

import jax
import jax.numpy as jnp
import numpy as np
from jax import lax
from jax.experimental import pallas as pl
from jax.experimental.pallas import tpu as pltpu
from jax.sharding import PartitionSpec as P

EX = 16
EY = 8
NODES = 81
INNER = 64
ROWS = INNER + 3
ACROSS, RIGHT, LEFT = INNER, INNER + 1, INNER + 2
VMEM = 48 * 1024 * 1024

f32 = jnp.float32
bf16 = jnp.bfloat16


def split(values):
    high = values.astype(bf16)
    return high, (values - high.astype(f32)).astype(bf16)


def operator(length):
    half = length // 2
    waves = np.arange(half + 1)
    weights = np.where((waves == 0) | (waves == half), 1.0, 2.0) / length
    sigma = 1.0 + (8.0 * waves / length) ** 2
    distance = np.arange(length)
    phases = (distance[:, None] * waves[None, :]) % length
    row = (np.cos(phases * (2.0 * np.pi / length)) * (weights * sigma)).sum(1)
    full = row[(distance[:, None] - distance[None, :]) % length].astype(np.float32)
    high = full.astype(jnp.bfloat16)
    low = (full - high.astype(np.float32)).astype(jnp.bfloat16)
    return high, low


def selector(slots):
    slot = lax.broadcasted_iota(jnp.int32, (EX * EY, EX * EY), 0)
    return jnp.where(slot == slots, 1.0, 0.0).astype(f32)


def lane_index(shape):
    return lax.broadcasted_iota(jnp.int32, shape, len(shape) - 1)


def element_kernel(terms, vel_ref, slots_ref, mats_ref, geo_ref, out_ref, left_ref, nodes_ref):
    depth = vel_ref.shape[1]
    count = len(terms)
    select = selector(slots_ref[...])
    geo = jnp.dot(geo_ref[...], select, precision=lax.Precision.HIGHEST, preferred_element_type=f32)
    select = select.astype(bf16)
    left_ref[...] = jnp.zeros_like(left_ref)
    for place, term in enumerate(terms):
        high, low = split(mats_ref[term])
        left_ref[place, :NODES, 0:NODES] = high
        left_ref[place, :NODES, 128 : 128 + NODES] = high
        left_ref[place, :NODES, 256 : 256 + NODES] = low
    left = left_ref[...].reshape(count * 96, 384)
    lane = lane_index((depth, EX * EY))
    across = lane % EY
    pad_rows = jnp.zeros((96 - NODES, EX * EY), f32)
    pad_deep = jnp.zeros((32, 2 * EX * EY), bf16)
    for c in range(3):
        for pair in range(depth // 2):
            parts = []
            for p in (2 * pair, 2 * pair + 1):
                product = vel_ref[c, p] * vel_ref[(c + 1) % 3, p]
                high, low = split(jnp.concatenate([product, pad_rows], axis=0))
                cells = jnp.dot(
                    jnp.concatenate([high, low], axis=0), select, preferred_element_type=f32
                )
                parts.append(cells.astype(bf16))
            both = jnp.concatenate(parts, axis=1)
            high = jnp.concatenate([both[:96], pad_deep], axis=0)
            low = jnp.concatenate([both[96:], pad_deep], axis=0)
            right = jnp.concatenate([high, low, high], axis=0)
            images = jnp.dot(left, right, preferred_element_type=f32)
            for place, p in enumerate((2 * pair, 2 * pair + 1)):
                total = 0.0
                for t, term in enumerate(terms):
                    total = total + (
                        images[96 * t : 96 * t + 88, 128 * place : 128 * place + 128]
                        * geo[term : term + 1]
                    )
                nodes_ref[c, pl.ds(p, 88, stride=depth), :] = total
        node = lambda i, j: nodes_ref[c, (9 * i + j) * depth : (9 * i + j + 1) * depth, :]

        def first(j):
            return node(0, j) + jnp.where(lane >= EY, pltpu.roll(node(8, j), EY, 1), 0.0)

        def store(row, value):
            out_ref[c * ROWS + row] = value

        def join(low, high):
            return low + jnp.where(across > 0, pltpu.roll(high, 1, 1), 0.0)

        end = jnp.zeros((depth, EX * EY), f32)
        for i in range(8):
            column = [first(j) if i == 0 else node(i, j) for j in range(9)]
            store(8 * i, join(column[0], column[8]))
            for j in range(1, 8):
                store(8 * i + j, column[j])
            shift = (i + 1 - EY) % (EX * EY)
            ended = column[8] if shift == 0 else pltpu.roll(column[8], shift, 1)
            end = jnp.where(across == i, ended, end)
        store(ACROSS, end)
        for row, i, origin in ((RIGHT, 8, (EX - 1) * EY), (LEFT, 0, 0)):
            last = node(i, 8)
            face = jnp.where(lane == INNER, pltpu.roll(last, (INNER - origin - EY + 1) % (EX * EY), 1), 0.0)
            for j in range(8):
                value = join(node(i, 0), last) if j == 0 else node(i, j)
                shift = (8 * j - origin) % (EX * EY)
                moved = value if shift == 0 else pltpu.roll(value, shift, 1)
                face = jnp.where(lane // EY == j, moved, face)
            store(row, face)


def elements(terms, velocity, slot_of_cell, elem_mats, geometry, rows):
    depth = velocity.shape[1]
    step = 8
    lanes = EX * EY
    return pl.pallas_call(
        functools.partial(element_kernel, terms),
        grid=(depth // step,),
        in_specs=[
            pl.BlockSpec((3, step, NODES, lanes), lambda k: (0, k, 0, 0)),
            pl.BlockSpec((1, lanes), lambda k: (0, 0)),
            pl.BlockSpec((4, NODES, NODES), lambda k: (0, 0, 0)),
            pl.BlockSpec((4, lanes), lambda k: (0, 0)),
        ],
        out_specs=pl.BlockSpec((rows, step, lanes), lambda k: (0, k, 0)),
        out_shape=jax.ShapeDtypeStruct((rows, depth, lanes), f32),
        scratch_shapes=[
            pltpu.VMEM((len(terms), 96, 384), bf16),
            pltpu.VMEM((3, 88 * step, lanes), f32),
        ],
        compiler_params=pltpu.CompilerParams(vmem_limit_bytes=VMEM),
        cost_estimate=pl.CostEstimate(
            flops=2 * 3 * depth * len(terms) * 96 * 384 * 128,
            bytes_accessed=4 * 3 * depth * 128 * (88 + 67),
            transcendentals=0,
        ),
        name="element_terms" if len(terms) > 1 else "element_mass",
    )(velocity, slot_of_cell, elem_mats, geometry)


def spanwise_kernel(x_ref, high_ref, low_ref, y_ref):
    parts, rows, depth, lanes = x_ref.shape
    length = parts * depth
    high, low = high_ref[...], low_ref[...]
    for r in range(0, rows, 2):
        width = min(2, rows - r)
        x = [x_ref[:, r + k].reshape(length, lanes) for k in range(width)]
        x = x[0] if width == 1 else jnp.concatenate(x, axis=1)
        x_high, x_low = split(x)
        y = jnp.dot(high, x_high, preferred_element_type=f32)
        y += jnp.dot(low, x_high, preferred_element_type=f32)
        y += jnp.dot(high, x_low, preferred_element_type=f32)
        for k in range(width):
            y_ref[:, r + k] = y[:, lanes * k : lanes * k + lanes].reshape(parts, depth, lanes)


def spanwise(values):
    parts, rows, depth, lanes = values.shape
    length = parts * depth
    high, low = operator(length)
    return pl.pallas_call(
        spanwise_kernel,
        out_shape=jax.ShapeDtypeStruct(values.shape, f32),
        compiler_params=pltpu.CompilerParams(vmem_limit_bytes=VMEM),
        cost_estimate=pl.CostEstimate(
            flops=6 * length * length * rows * lanes,
            bytes_accessed=8 * length * rows * lanes,
            transcendentals=0,
        ),
        name="spanwise",
    )(values, high, low)


def expand_kernel(u_ref, y_ref, faces_ref, slots_ref, out_ref, nodes_ref):
    depth, lanes = u_ref.shape[1:]
    select = selector(slots_ref[...]).astype(bf16)
    select = jnp.concatenate([select, select], axis=1)
    lane = lane_index((depth, lanes))
    across = lane % EY
    row = lambda q: u_ref[q] + y_ref[q]
    before, after = faces_ref[0, 0], faces_ref[1, 0]

    def put(i, j, value):
        high, low = split(value)
        nodes_ref[pl.ds((9 * i + j) * depth, depth), :] = jnp.concatenate([high, low], axis=1)

    end = row(ACROSS) + jnp.where(lane == 0, pltpu.roll(before, lanes - INNER, 1), 0.0)
    face = row(RIGHT) + after
    for i in range(8):
        for j in range(8):
            value = row(8 * i + j)
            if i == 0:
                moved = before if j == 0 else pltpu.roll(before, lanes - 8 * j, 1)
                value = value + jnp.where(lane < EY, moved, 0.0)
                moved = pltpu.roll(face, (lanes - EY - 8 * j) % lanes, 1) if j < 15 else face
                beyond = jnp.where(lane >= lanes - EY, moved, pltpu.roll(value, lanes - EY, 1))
                put(8, j, beyond)
                if j == 0:
                    corner = pltpu.roll(beyond, lanes - 1, 1)
            put(i, j, value)
            if j == 0:
                moved = end if i == 7 else pltpu.roll(end, EY - 1 - i, 1)
                last = jnp.where(across == EY - 1, moved, pltpu.roll(value, lanes - 1, 1))
                put(i, 8, last)
    corner = jnp.where(across == EY - 1, pltpu.roll(end, lanes - 1, 1), corner)
    corner = jnp.where(lane == lanes - 1, pltpu.roll(face, lanes - 1 - INNER, 1), corner)
    put(8, 8, corner)
    slots = lax.dot_general(
        nodes_ref[...], select, (((1,), (1,)), ((), ())), preferred_element_type=f32
    )
    result_ref = out_ref
    slots = slots.reshape(NODES, depth, lanes)
    for p in range(depth):
        result_ref[0, p] = slots[:, p, :]


def expand(u, y, faces, slot_of_cell):
    depth, lanes = u.shape[1:]
    return pl.pallas_call(
        expand_kernel,
        grid=(3,),
        in_specs=[
            pl.BlockSpec((ROWS, depth, lanes), lambda c: (c, 0, 0)),
            pl.BlockSpec((ROWS, depth, lanes), lambda c: (c, 0, 0)),
            pl.BlockSpec((2, 1, depth, lanes), lambda c: (0, c, 0, 0)),
            pl.BlockSpec((1, lanes), lambda c: (0, 0)),
        ],
        out_specs=pl.BlockSpec((1, depth, NODES, lanes), lambda c: (c, 0, 0, 0)),
        out_shape=jax.ShapeDtypeStruct((3, depth, NODES, lanes), f32),
        scratch_shapes=[pltpu.VMEM((NODES * depth, 2 * lanes), bf16)],
        compiler_params=pltpu.CompilerParams(vmem_limit_bytes=VMEM),
        cost_estimate=pl.CostEstimate(
            flops=2 * 3 * NODES * depth * 256 * 128,
            bytes_accessed=4 * 3 * depth * lanes * 222,
            transcendentals=0,
        ),
        name="expand",
    )(u, y, faces, slot_of_cell)


def swap(values):
    return lax.all_to_all(values, "modes", split_axis=0, concat_axis=0, tiled=True)


def local(velocity, slot_of_cell, elem_mats, geometry):
    depth = velocity.shape[1]
    lanes = velocity.shape[3]
    parts = lax.axis_size("modes")
    share = -(-3 * ROWS // parts)
    rows = share * parts
    z = elements((3,), velocity, slot_of_cell, elem_mats, geometry, rows)
    pencil = swap(z.reshape(parts, share * depth, lanes))
    u = elements((0, 1, 2), velocity, slot_of_cell, elem_mats, geometry, rows)
    y = spanwise(pencil.reshape(parts, share, depth, lanes))
    y = swap(y.reshape(parts, share * depth, lanes)).reshape(rows, depth, lanes)
    count = lax.axis_size("dom")
    forward = [(k, (k + 1) % count) for k in range(count)]
    backward = [(k, (k - 1) % count) for k in range(count)]

    def face(row):
        pick = lambda a: a[: 3 * ROWS].reshape(3, ROWS, depth, lanes)[:, row]
        return pick(u) + pick(y)

    before = lax.ppermute(face(RIGHT), "dom", forward)
    after = lax.ppermute(face(LEFT), "dom", backward)
    return expand(u, y, jnp.stack([before, after]), slot_of_cell)


def solution(mesh):
    in_specs = (P(None, "modes", None, "dom"), P("dom", None), P(), P(None, "dom"))
    out_specs = P(None, "modes", None, "dom")
    return jax.shard_map(local, mesh=mesh, in_specs=in_specs, out_specs=out_specs, check_vma=False)
```

time: 293 us -> 109 us (0.37)
  local copies, waits for them, and re-layouts: 134 us -> 8.82 us
  waiting for transfers between devices: 83.2 us -> 33.5 us
  blocking collectives: 0 us -> 45.3 us
  other arithmetic: 42.9 us -> 0.78 us
  matrix products: 17.2 us -> 0 us
  Pallas kernels: 0 us -> 12.6 us
  starting transfers between devices: 13.3 us -> 7.26 us
    reshape x5 -> x0, local copies, waits for them, and re-layouts: 58.1 us -> none  [the longest x1 17.3 us: local(): mass_kron = jnp.einsum('ij,e,ef->iejf', elem_mats[3], block_geo[3], ident...]
    all_to_all x2 -> x1, waiting for transfers between devices: 79.9 us -> 30.2 us  [swap(): lax.all_to_all(values, 'modes', split_axis=0, concat_axis=0, tiled=True)]
    all_to_all x0 -> x1, blocking collectives: none -> 45.3 us  [swap(): lax.all_to_all(values, 'modes', split_axis=0, concat_axis=0, tiled=True)]
    scatter x3 -> x0, local copies, waits for them, and re-layouts: 30.7 us -> none  [the longest x2 29.7 us: assemble(): cells_grid.at[:, :, :, 8, :, :-1].set(across).at[:, :, :, 0, :, 1:]]
    transpose x2 -> x0, other arithmetic: 21.9 us -> none  [the longest x1 11.6 us: local(): jnp.einsum('ij,e,ef->iejf', elem_mats[3], block_geo[3], identity, precisi...]
    dot_general x5 -> x0, matrix products: 17.2 us -> none  [the longest x1 5.55 us: local(): jnp.einsum('xy,cmy->cmx', stiff_kron, spectra, precision=lax.Precision.HI...]
    pallas_call x0 -> x4, Pallas kernels: none -> 12.6 us  [the longest x2 9.07 us: elements(): pl.pallas_call(functools.partial(element_kernel, terms), grid=(depth // s...]
    select_n x2 -> x0, local copies, waits for them, and re-layouts: 12 us -> none  [the longest x1 9.82 us: assemble(): picked = jnp.take(values, order, axis=3)]
  transfers between devices with their start and end apart: 4 -> 3, of which waited for: 4 -> 3; matrix products, arithmetic and copies ran while one was open for 22% -> 1% of each run, Pallas kernels for 0% -> 5%
where the time goes in v1:
time: 109 us; the launch traced here: 108 us
  blocking collectives  45.3 us (42%)
  waiting for transfers between devices  33.5 us (31%)
  Pallas kernels  12.6 us (12%)
  local copies, waits for them, and re-layouts  8.82 us (8%)
  starting transfers between devices  7.26 us (7%)
    all_to_all x1, blocking collectives, swap(): lax.all_to_all(values, 'modes', split_axis=0, concat_axis=0, tiled=True)  45.3 us
    all_to_all x1, waiting for transfers between devices, swap(): lax.all_to_all(values, 'modes', split_axis=0, concat_axis=0, tiled=True)  30.2 us
    pallas_call x2, Pallas kernels, elements(): pl.pallas_call(functools.partial(element_kernel, terms), grid=(depth // s...  9.07 us
    unnamed x18, local copies, waits for them, and re-layouts  5.77 us
    all_to_all x1, starting transfers between devices, swap(): lax.all_to_all(values, 'modes', split_axis=0, concat_axis=0, tiled=True)  5.19 us
  transfers between devices with their start and end apart: 3, of which 3 were waited for; matrix products, arithmetic and copies ran while one was open for 1% of the time, Pallas kernels for 5%

profile of v1, /device:TPU:16, one launch (start us, length us, event | category | flops | bytes accessed | tf_op | source)
XLA Modules:
  0.0 108.3 jit_solution(13591792364082011419)
XLA Ops:
  0.0 0.9 copy.13.mats_ref
  0.9 0.0 copy-start.2
  0.9 0.0 copy-start.6
  1.0 0.0 copy-start.7
  1.0 2.3 %copy.12.vel_ref = f32[3,16,81,128]{3,2,1,0:T(8,128)S(1)} copy(f32[3,16,81,128]{3,1,2,0:T(8,128)} %param.6) | data formatting | bytes 3981312 | tf_op args[0]
  3.3 0.0 copy-done.2
  3.3 0.0 copy-done.6
  3.3 0.0 copy-done.7
  3.3 0.0 copy-start
  3.3 3.9 %element_mass.1 = f32[208,16,128]{2,1,0:T(8,128)S(1)} custom-call(f32[3,16,81,128]{3,2,1,0:T(8,128)S(1)} %copy.12.vel_ref, s32[1,128]{1,0:T(1,128)S(1)} %copy-done.7, f32[4,81,81]{2,1,0:T(8,128)S(1)} %copy.13.mats_ref, f32[4,128]{1,0:T(4,128)S(1)} %copy-done.6), custom_call_target="tpu_custom_call" | custom-call | flops 452984832 | bytes 3809280 | tf_op jit(solution)/shard_map/element_mass/pallas_call | solution.py:127
  7.2 0.0 copy-done
  7.2 0.0 copy-start.4
  7.2 0.0 copy-start.5
  7.3 45.3 %all_to_all.10 = f32[16,208,128]{2,1,0:T(8,128)S(1)} all-to-all(f32[16,208,128]{2,1,0:T(8,128)S(1)} %bitcast.35), channel_id=1, replica_groups=mesh['modes'=16,'dom'=2] {'modes'}, dimensions={0} | all-to-all | bytes 3407872 | tf_op jit(solution)/shard_map/all_to_all | solution.py:253
  52.5 0.0 copy-done.4
  52.5 0.0 copy-done.5
  52.5 2.1 %spanwise.1 = f32[16,13,16,128]{3,2,1,0:T(8,128)} custom-call(f32[16,13,16,128]{3,2,1,0:T(8,128)S(1)} %bitcast.34, bf16[256,256]{1,0:T(8,128)(2,1)S(1)} %copy-done.5, bf16[256,256]{1,0:T(8,128)(2,1)S(1)} %copy-done.4), custom_call_target="tpu_custom_call" | custom-call | flops 654311424 | bytes 3407872 | tf_op jit(solution)/shard_map/spanwise/pallas_call | solution.py:172
  54.6 5.2 %all-to-all-start.1 = ((f32[16,208,128]{2,1,0:T(8,128)}), f32[16,208,128]{2,1,0:T(8,128)S(1)}, u32[]{:S(2)}, u32[]{:S(2)}) async-start(f32[16,208,128]{2,1,0:T(8,128)} %bitcast.2), calls=%async_computation.1 | async-start | bytes 3407872 | tf_op jit(solution)/shard_map/all_to_all | solution.py:253
  59.8 0.0 copy-start.1
  59.8 1.6 %copy-done.1 = f32[3,16,81,128]{3,2,1,0:T(8,128)S(1)} copy-done((f32[3,16,81,128]{3,2,1,0:T(8,128)S(1)}, f32[3,16,81,128]{3,2,1,0:T(8,128)}, u32[]{:S(2)}) %copy-start.1) | copy-done | bytes 1990680
  61.4 0.0 copy-start.3
  61.4 0.9 copy-done.3
  62.3 5.1 %element_terms.1.u_ref = f32[208,16,128]{2,1,0:T(8,128)S(1)} custom-call(f32[3,16,81,128]{3,2,1,0:T(8,128)S(1)} %copy-done.1, s32[1,128]{1,0:T(1,128)S(1)} %copy-done.7, f32[4,81,81]{2,1,0:T(8,128)S(1)} %copy-done.3, f32[4,128]{1,0:T(4,128)S(1)} %copy-done.6), custom_call_target="tpu_custom_call" | custom-call | flops 1358954496 | bytes 3809280 | tf_op jit(solution)/shard_map/element_terms/pallas_call | solution.py:127
  67.5 1.3 %slice.26 = f32[201,16,128]{2,1,0:T(8,128)} slice(f32[208,16,128]{2,1,0:T(8,128)S(1)} %element_terms.1.u_ref), slice={[0:201], [0:16], [0:128]} | slice | bytes 3293184 | tf_op jit(solution)/shard_map/slice | solution.py:272
  68.8 30.2 %all-to-all-done.1 = f32[16,208,128]{2,1,0:T(8,128)S(1)} async-done(((f32[16,208,128]{2,1,0:T(8,128)}), f32[16,208,128]{2,1,0:T(8,128)S(1)}, u32[]{:S(2)}, u32[]{:S(2)}) %all-to-all-start.1) | async-done | bytes 1703968 | tf_op jit(solution)/shard_map/all_to_all | solution.py:253
  99.0 0.1 slice.28
  99.1 0.8 fusion.3
  99.9 1.5 %collective-permute-start = (f32[3,16,128]{2,1,0:T(8,128)S(1)}, f32[3,16,128]{2,1,0:T(8,128)S(1)}, u32[]{:S(2)}, u32[]{:S(2)}) collective-permute-start(f32[3,16,128]{2,1,0:T(8,128)S(1)} %get-tuple-element.5), channel_id=1, source_target_pairs={{0,1},{1,0},{2,3},{3,2},{4,5},{5,4},{6,7},{7,6},{8,9},{9,8},{10,11... | collective-permute-start | bytes 73736 | tf_op jit(solution)/shard_map/ppermute | solution.py:275
  101.4 0.5 collective-permute-start.1
  102.0 1.9 %collective-permute-done = f32[3,16,128]{2,1,0:T(8,128)S(1)} collective-permute-done((f32[3,16,128]{2,1,0:T(8,128)S(1)}, f32[3,16,128]{2,1,0:T(8,128)S(1)}, u32[]{:S(2)}, u32[]{:S(2)}) %collective-permute-start) | collective-permute-done | bytes 24608 | tf_op jit(solution)/shard_map/ppermute | solution.py:275
  103.9 1.3 %collective-permute-done.1 = f32[3,16,128]{2,1,0:T(8,128)S(1)} collective-permute-done((f32[3,16,128]{2,1,0:T(8,128)S(1)}, f32[3,16,128]{2,1,0:T(8,128)S(1)}, u32[]{:S(2)}, u32[]{:S(2)}) %collective-permute-start.1) | collective-permute-done | bytes 24608 | tf_op jit(solution)/shard_map/ppermute | solution.py:276
  105.3 1.4 %expand.1 = f32[3,16,81,128]{3,2,1,0:T(8,128)S(1)} custom-call(f32[208,16,128]{2,1,0:T(8,128)S(1)} %element_terms.1.u_ref, f32[208,16,128]{2,1,0:T(8,128)S(1)} %bitcast.33, f32[2,3,16,128]{3,2,1,0:T(8,128)S(1)} %pad_maximum_fusion.faces_ref, s32[1,128]{1,0:T(1,128)S(1)} %copy-done.7), custom_call_target="tpu_custom_call" | custom-call | flops 254803968 | bytes 5455872 | tf_op jit(solution)/shard_map/expand/pallas_call | solution.py:230
  106.7 1.6 %copy.20 = f32[3,16,81,128]{3,1,2,0:T(8,128)} copy(f32[3,16,81,128]{3,2,1,0:T(8,128)S(1)} %expand.1) | data formatting | bytes 3981312 | tf_op jit(solution)/shard_map/expand/pallas_call | solution.py:230
  (1 shorter events, 0.0 us)
Async XLA Ops:
  0.9 2.3 %copy-start.2 = (f32[4,81,81]{2,1,0:T(8,128)}, f32[4,81,81]{2,1,0:T(8,128)S(1)}, u32[]{:S(2)}) copy-start(f32[4,81,81]{2,1,0:T(8,128)S(1)} %copy.13.mats_ref) | copy-start | bytes 314932
  0.9 2.3 %copy-start.6 = (f32[4,128]{1,0:T(4,128)S(1)}, f32[4,128]{1,0:T(4,128)}, u32[]{:S(2)}) copy-start(f32[4,128]{1,0:T(4,128)} %geo_ref.3) | copy-start | bytes 6148
  1.0 2.3 %copy-start.7 = (s32[1,128]{1,0:T(1,128)S(1)}, s32[1,128]{1,0:T(1,128)}, u32[]{:S(2)}) copy-start(s32[1,128]{1,0:T(1,128)} %slots_ref.5) | copy-start | bytes 1540
  3.3 3.9 %copy-start = (f32[3,16,81,128]{3,2,1,0:T(8,128)}, f32[3,16,81,128]{3,2,1,0:T(8,128)S(1)}, u32[]{:S(2)}) copy-start(f32[3,16,81,128]{3,2,1,0:T(8,128)S(1)} %copy.12.vel_ref) | copy-start | bytes 5971972
  7.2 45.3 %copy-start.4 = (bf16[256,256]{1,0:T(8,128)(2,1)S(1)}, bf16[256,256]{1,0:T(8,128)(2,1)}, u32[]{:S(2)}) copy-start(bf16[256,256]{1,0:T(8,128)(2,1)} %constant.5.clone.low_ref) | copy-start | bytes 393220
  7.2 45.3 %copy-start.5 = (bf16[256,256]{1,0:T(8,128)(2,1)S(1)}, bf16[256,256]{1,0:T(8,128)(2,1)}, u32[]{:S(2)}) copy-start(bf16[256,256]{1,0:T(8,128)(2,1)} %constant.4.clone.high_ref) | copy-start | bytes 393220
  54.6 44.4 %all-to-all-start.1 = ((f32[16,208,128]{2,1,0:T(8,128)}), f32[16,208,128]{2,1,0:T(8,128)S(1)}, u32[]{:S(2)}, u32[]{:S(2)}) async-start(f32[16,208,128]{2,1,0:T(8,128)} %bitcast.2), calls=%async_computation.1 | async-start | bytes 3407872 | tf_op jit(solution)/shard_map/all_to_all | solution.py:253
  59.8 1.6 %copy-start.1 = (f32[3,16,81,128]{3,2,1,0:T(8,128)S(1)}, f32[3,16,81,128]{3,2,1,0:T(8,128)}, u32[]{:S(2)}) copy-start(f32[3,16,81,128]{3,2,1,0:T(8,128)} %copy-done) | copy-start | bytes 5971972
  61.4 0.9 copy-start.3
  99.9 4.0 %collective-permute-start = (f32[3,16,128]{2,1,0:T(8,128)S(1)}, f32[3,16,128]{2,1,0:T(8,128)S(1)}, u32[]{:S(2)}, u32[]{:S(2)}) collective-permute-start(f32[3,16,128]{2,1,0:T(8,128)S(1)} %get-tuple-element.5), channel_id=1, source_target_pairs={{0,1},{1,0},{2,3},{3,2},{4,5},{5,4},{6,7},{7,6},{8,9},{9,8},{10,11... | collective-permute-start | bytes 73736 | tf_op jit(solution)/shard_map/ppermute | solution.py:275
  101.4 3.8 %collective-permute-start.1 = (f32[3,16,128]{2,1,0:T(8,128)S(1)}, f32[3,16,128]{2,1,0:T(8,128)S(1)}, u32[]{:S(2)}, u32[]{:S(2)}) collective-permute-start(f32[3,16,128]{2,1,0:T(8,128)S(1)} %get-tuple-element.6), channel_id=1, source_target_pairs={{0,1},{1,0},{2,3},{3,2},{4,5},{5,4},{6,7},{7,6},{8,9},{9,8},{10,11... | collective-permute-start | bytes 73736 | tf_op jit(solution)/shard_map/ppermute | solution.py:276

commit v2 on v0

v2 whole, which is shorter than its diff:
```python
import functools
import math

import jax
import jax.numpy as jnp
import numpy as np
from jax import lax
from jax.experimental import pallas as pl
from jax.experimental.pallas import tpu as pltpu
from jax.sharding import PartitionSpec as P

EX = 16
EY = 8
LANES = EX * EY
NODES = 81
SIDE = 8
INNER = SIDE * (SIDE - 1)
FACE = SIDE * EY
ACROSS, RIGHT, LEFT, EXTRA = SIDE, SIDE + 1, SIDE + 2, SIDE + 3
DEEP = 96
VMEM = 48 * 1024 * 1024
WIDE = 60 * 1024 * 1024

f32 = jnp.float32
bf16 = jnp.bfloat16


def split(values):
    high = values.astype(bf16)
    return high, (values - high.astype(f32)).astype(bf16)


class Layout:

    def __init__(self, parts):
        self.outer = max(d for d in range(1, math.isqrt(parts) + 1) if parts % d == 0)
        self.inner = parts // self.outer
        assert self.inner & (self.inner - 1) == 0
        self.late = [0, self.outer // 2]
        self.early = [k for k in range(1, self.outer) if k not in self.late]
        self.blocks = [(k, s) for k in range(self.outer) for s in range(self.inner)]

    def place(self, k, s):
        me = lax.axis_index("modes")
        out = lax.rem(me // self.inner + (k + self.outer), self.outer)
        return out * self.inner + jnp.bitwise_xor(lax.rem(me, self.inner), s)

    def sent(self, k, s, early, late):
        if k in self.late:
            return late[s].at[self.late.index(k)]
        return early[self.early.index(k)].at[s]

    def shapes(self, share):
        early = [(self.inner,) + share] * len(self.early)
        return early + [(len(self.late),) + share] * self.inner

    def divide(self, arrays):
        return arrays[: len(self.early)], arrays[len(self.early) :]

    def got(self, refs):
        inner = self.inner
        late, middle, early = refs[:inner], refs[inner], refs[inner + 1 :]
        found = {(0, s): late[s].at[0] for s in range(inner)}
        found.update({(self.late[1], s): middle.at[s] for s in range(inner)})
        for at, k in enumerate(self.early):
            found.update({(k, s): early[s].at[at] for s in range(inner)})
        return found

    def swap(self, early, late):
        parts = self.outer * self.inner

        def onward(value, k):
            steps = [(d, (d + k * self.inner) % parts) for d in range(parts)]
            return lax.ppermute(value, "modes", steps)

        def across(values):
            pairs = lambda s: [(d, d ^ s) for d in range(parts)]
            return values[:1] + [
                lax.ppermute(value, "modes", pairs(s)) for s, value in enumerate(values) if s
            ]

        early = [onward(value, k) for k, value in zip(self.early, early)]
        late = across(list(late))
        middle = onward(jnp.stack([value[1] for value in late]), self.late[1])
        early = across([jnp.stack([value[s] for value in early]) for s in range(self.inner)])
        return late + [middle] + early


def operator(layout, depth):
    outer, inner = layout.outer, layout.inner
    length = outer * inner * depth
    half = length // 2
    waves = np.arange(half + 1)
    weights = np.where((waves == 0) | (waves == half), 1.0, 2.0) / length
    sigma = 1.0 + (8.0 * waves / length) ** 2
    phases = (np.arange(length)[:, None] * waves[None, :]) % length
    row = (np.cos(phases * (2.0 * np.pi / length)) * (weights * sigma)).sum(1)
    step, slot, plane = np.meshgrid(np.arange(outer), np.arange(inner), np.arange(depth), indexing="ij")
    step, slot, plane = step.ravel(), slot.ravel(), plane.ravel()
    place = np.arange(inner)[:, None]
    sent = (step * inner + (place ^ slot)) * depth + plane
    got = (-step * inner + (place ^ slot)) * depth + plane
    full = row[(sent[:, :, None] - got[:, None, :]) % length].astype(np.float32)
    high = full.astype(jnp.bfloat16)
    low = (full - high.astype(np.float32)).astype(jnp.bfloat16)
    return np.concatenate([high, low], axis=1)


def selector(slots):
    slot = lax.broadcasted_iota(jnp.int32, (LANES, LANES), 0)
    return jnp.where(slot == slots, 1.0, 0.0).astype(f32)


def lane_index(depth):
    return lax.broadcasted_iota(jnp.int32, (depth, LANES), 1)


def roll(value, shift):
    shift = shift % LANES
    return value if shift == 0 else pltpu.roll(value, shift, 1)


def gather_face(column, origin):
    lane = lane_index(column[0].shape[0])
    face = jnp.where(lane == FACE, roll(column[SIDE], FACE - origin - EY + 1), 0.0)
    for j in range(SIDE):
        face = jnp.where(lane // EY == j, roll(column[j], EY * j - origin), face)
    return face


def prepare(terms, slots_ref, mats_ref, geo_ref, left_ref, cells_ref):
    select = selector(slots_ref[...])
    geo = jnp.dot(geo_ref[...], select, precision=lax.Precision.HIGHEST, preferred_element_type=f32)
    left_ref[...] = jnp.zeros_like(left_ref)
    for place, term in enumerate(terms):
        high, low = split(mats_ref[:, term, :])
        left_ref[place, :NODES, 0:NODES] = high
        left_ref[place, :NODES, DEEP : DEEP + NODES] = high
        left_ref[place, :NODES, 2 * DEEP : 2 * DEEP + NODES] = low
    depth = cells_ref.shape[1] // DEEP
    cells_ref[:, NODES * depth :, :] = jnp.zeros((2, (DEEP - NODES) * depth, LANES), f32)
    return select.astype(bf16), geo


def component(terms, first, second, select, geo, left, cells_ref, nodes_ref, inner, extra):
    depth = first.shape[1]
    product = (first[...] * second[...]).reshape(NODES * depth, LANES)
    for place, part in enumerate(split(product)):
        cells_ref[place, : NODES * depth, :] = jnp.dot(part, select, preferred_element_type=f32)
    for pair in range(depth // 2):
        parts = [
            jnp.concatenate(
                [cells_ref[k, pl.ds(2 * pair + p, DEEP, stride=depth), :] for p in (0, 1)], axis=1
            ).astype(bf16)
            for k in (0, 1)
        ]
        right = jnp.concatenate([parts[0], parts[1], parts[0]], axis=0)
        images = jnp.dot(left, right, preferred_element_type=f32)
        for p in (0, 1):
            total = 0.0
            for t, term in enumerate(terms):
                total = total + (
                    images[DEEP * t : DEEP * t + 88, LANES * p : LANES * p + LANES]
                    * geo[term : term + 1]
                )
            nodes_ref[pl.ds(2 * pair + p, 88, stride=depth), :] = total
    lane = lane_index(depth)
    across = lane % EY

    def node(i, j):
        value = nodes_ref[(9 * i + j) * depth : (9 * i + j + 1) * depth, :]
        if i > 0:
            return value
        return value + jnp.where(lane >= EY, roll(node(8, j), EY), 0.0)

    def join(low, high):
        return low + jnp.where(across > 0, roll(high, 1), 0.0)

    end = jnp.zeros((depth, LANES), f32)
    for i in range(SIDE + 1):
        column = [node(i, j) for j in range(SIDE + 1)]
        column[0] = join(column[0], column[SIDE])
        if i < SIDE:
            for j in range(SIDE):
                inner(SIDE * (i - 1) + j, column[j]) if i else extra(j, column[j])
            end = jnp.where(across == i, roll(column[SIDE], i + 1 - EY), end)
        if i in (0, SIDE):
            extra(RIGHT if i else LEFT, gather_face(column, LANES - EY if i else 0))
    extra(ACROSS, end)


def element_kernel(terms, layout, count, *refs):
    vel_hbm, slots_hbm, mats_hbm, geo_hbm = refs[:4]
    outs, scratch = refs[4 : 4 + count], refs[4 + count :]
    vel_ref, slots_ref, mats_ref, geo_ref, left_ref, cells_ref, nodes_ref, sems = scratch[:8]
    out_ref = scratch[8] if layout else outs[0]
    pairs = [(slots_hbm, slots_ref), (geo_hbm, geo_ref), (mats_hbm, mats_ref)]
    pairs += [(vel_hbm.at[c], vel_ref.at[c]) for c in range(3)]
    copies = [pltpu.make_async_copy(*pair, sems.at[k]) for k, pair in enumerate(pairs)]
    for copy in copies:
        copy.start()
    for copy in copies[:3]:
        copy.wait()
    select, geo = prepare(terms, slots_ref, mats_ref, geo_ref, left_ref, cells_ref)
    left = left_ref[...].reshape(len(terms) * DEEP, 3 * DEEP)

    def put(first, row, value):
        out_ref[first + row] = value

    copies[3].wait()
    for c in range(3):
        if c < 2:
            copies[4 + c].wait()
        component(
            terms,
            vel_ref.at[c],
            vel_ref.at[(c + 1) % 3],
            select,
            geo,
            left,
            cells_ref,
            nodes_ref,
            functools.partial(put, c * INNER),
            functools.partial(put, 3 * INNER + c * EXTRA),
        )
    for row in range(3 * (INNER + EXTRA), out_ref.shape[0]):
        out_ref[row] = jnp.zeros(out_ref.shape[1:], f32)
    if layout:
        send_sems = scratch[9]
        share = out_ref.shape[0] // len(layout.blocks)
        early, late = layout.divide(outs)
        copies = [
            pltpu.make_async_copy(
                out_ref.at[pl.ds(layout.place(k, s) * share, share)],
                layout.sent(k, s, early, late),
                send_sems.at[at],
            )
            for at, (k, s) in enumerate(layout.blocks)
        ]
        for copy in copies:
            copy.start()
        for copy in copies:
            copy.wait()


def elements(name, terms, layout, rows, args):
    depth = args[0].shape[2]
    scratch = [
        *(pltpu.VMEM(a.shape, a.dtype) for a in args),
        pltpu.VMEM((len(terms), DEEP, 3 * DEEP), bf16),
        pltpu.VMEM((2, DEEP * depth, LANES), f32),
        pltpu.VMEM((88 * depth, LANES), f32),
        pltpu.SemaphoreType.DMA((6,)),
    ]
    shapes = [(rows, depth, LANES)]
    if layout:
        scratch += [pltpu.VMEM(shapes[0], f32), pltpu.SemaphoreType.DMA((len(layout.blocks),))]
        shapes = layout.shapes((rows // len(layout.blocks), depth, LANES))
    anywhere = pl.BlockSpec(memory_space=pl.ANY)
    return pl.pallas_call(
        functools.partial(element_kernel, terms, layout, len(shapes)),
        in_specs=[anywhere] * len(args),
        out_specs=[anywhere if layout else pl.BlockSpec(memory_space=pltpu.VMEM)] * len(shapes),
        out_shape=[jax.ShapeDtypeStruct(shape, f32) for shape in shapes],
        scratch_shapes=scratch,
        compiler_params=pltpu.CompilerParams(vmem_limit_bytes=WIDE if layout else VMEM),
        cost_estimate=pl.CostEstimate(
            flops=2 * 3 * depth * len(terms) * DEEP * 3 * DEEP * LANES,
            bytes_accessed=4 * 3 * depth * LANES * 150,
            transcendentals=0,
        ),
        name=name,
    )(*args)


def spanwise_kernel(layout, count, *refs):
    got = layout.got(refs[:count])
    table_ref, early, late = refs[count], *layout.divide(refs[count + 1 :])
    share, depth, lanes = late[0].shape[1:]
    length = len(layout.blocks) * depth
    table = table_ref[...]
    for r in range(0, share, 2):
        width = min(2, share - r)
        x = [
            jnp.concatenate([got[block][r + k] for block in layout.blocks], axis=0)
            for k in range(width)
        ]
        x = x[0] if width == 1 else jnp.concatenate(x, axis=1)
        x_high, x_low = split(x)
        y = jnp.dot(table, x_high, preferred_element_type=f32)
        y = y[:length] + y[length:]
        y += jnp.dot(table[:length], x_low, preferred_element_type=f32)
        for at, block in enumerate(layout.blocks):
            for k in range(width):
                layout.sent(*block, early, late)[r + k] = y[
                    depth * at : depth * at + depth, lanes * k : lanes * k + lanes
                ]


def spanwise(layout, values, table):
    share = values[0].shape[1:]
    length = len(layout.blocks) * share[1]
    return pl.pallas_call(
        functools.partial(spanwise_kernel, layout, len(values)),
        out_shape=[jax.ShapeDtypeStruct(shape, f32) for shape in layout.shapes(share)],
        compiler_params=pltpu.CompilerParams(vmem_limit_bytes=VMEM),
        cost_estimate=pl.CostEstimate(
            flops=6 * length * length * share[0] * LANES,
            bytes_accessed=8 * length * share[0] * LANES,
            transcendentals=0,
        ),
        name="spanwise",
    )(*values, table)


def total_kernel(layout, u_ref, *refs):
    total_ref, faces_ref = refs[-2:]
    for (k, s), ref in layout.got(refs[:-2]).items():
        share = ref.shape[0]
        rows = pl.ds(layout.place(-k, s) * share, share)
        total_ref[rows] = u_ref[rows] + ref[...]
    for place, row in enumerate((RIGHT, LEFT)):
        for c in range(3):
            faces_ref[place, c] = total_ref[3 * INNER + c * EXTRA + row]


def totals(layout, u, values):
    return pl.pallas_call(
        functools.partial(total_kernel, layout),
        out_shape=[
            jax.ShapeDtypeStruct(u.shape, f32),
            jax.ShapeDtypeStruct((2, 3) + u.shape[1:], f32),
        ],
        compiler_params=pltpu.CompilerParams(vmem_limit_bytes=VMEM),
        cost_estimate=pl.CostEstimate(flops=u.size, bytes_accessed=12 * u.size, transcendentals=0),
        name="totals",
    )(u, *values)


def to_slots(nodes, select):
    return lax.dot_general(nodes, select, (((1,), (1,)), ((), ())), preferred_element_type=f32)


def pair_selector(slots_ref):
    select = selector(slots_ref[...]).astype(bf16)
    return jnp.concatenate([select, select], axis=1)


def middle_kernel(t_ref, slots_ref, out_ref, nodes_ref, slots_out_ref, sems):
    depth, lanes = t_ref.shape[1:]
    select = pair_selector(slots_ref)
    across = lane_index(depth) % EY
    count = (SIDE - 1) * (SIDE + 1)
    copies = []
    for c in range(3):
        end = t_ref[3 * INNER + c * EXTRA + ACROSS]

        def put(at, value):
            high, low = split(value)
            nodes_ref[pl.ds(at * depth, depth), :] = jnp.concatenate([high, low], axis=1)

        for i in range(1, SIDE):
            for j in range(SIDE):
                value = t_ref[c * INNER + SIDE * (i - 1) + j]
                put((SIDE + 1) * (i - 1) + j, value)
                if j == 0:
                    last = jnp.where(across == EY - 1, roll(end, EY - 1 - i), roll(value, -1))
                    put((SIDE + 1) * (i - 1) + SIDE, last)
        slots_out_ref[c] = to_slots(nodes_ref[...], select).reshape(count, depth, lanes)
        copy = pltpu.make_async_copy(
            slots_out_ref.at[c], out_ref.at[c, pl.ds(SIDE + 1, count)], sems.at[c]
        )
        copy.start()
        copies.append(copy)
    for copy in copies:
        copy.wait()


def faces_kernel(
    t_ref, before_ref, after_ref, slots_ref, _, out_ref, nodes_ref, slots_out_ref, sems
):
    depth, lanes = t_ref.shape[1:]
    select = pair_selector(slots_ref)
    lane = lane_index(depth)
    across = lane % EY
    count = SIDE + 1
    copies = []
    for c in range(3):
        extra = lambda k: t_ref[3 * INNER + c * EXTRA + k]
        before = before_ref[c]
        face = extra(RIGHT) + after_ref[c]
        end = extra(ACROSS) + jnp.where(lane == 0, roll(before, -FACE), 0.0)

        def put(at, value):
            high, low = split(value)
            nodes_ref[pl.ds(at * depth, depth), :] = jnp.concatenate([high, low], axis=1)

        for j in range(SIDE):
            value = extra(j) + jnp.where(lane < EY, roll(before, -EY * j), 0.0)
            moved = roll(face, lanes - EY - EY * j)
            beyond = jnp.where(lane >= lanes - EY, moved, roll(value, -EY))
            put(j, value)
            put(count + j, beyond)
            if j == 0:
                last = jnp.where(across == EY - 1, roll(end, EY - 1), roll(value, -1))
                put(SIDE, last)
                corner = jnp.where(across == EY - 1, roll(end, -1), roll(beyond, -1))
                corner = jnp.where(lane == lanes - 1, roll(face, lanes - 1 - FACE), corner)
                put(count + SIDE, corner)
        slots_out_ref[c] = to_slots(nodes_ref[...], select).reshape(2, count, depth, lanes)
        for side in range(2):
            copy = pltpu.make_async_copy(
                slots_out_ref.at[c, side],
                out_ref.at[c, pl.ds(side * (NODES - count), count)],
                sems.at[c, side],
            )
            copy.start()
            copies.append(copy)
    for copy in copies:
        copy.wait()


def expand(kernel, name, nodes, args, result=None):
    depth = args[0].shape[1]
    shape = (3, *nodes, depth, LANES)
    count = math.prod(nodes)
    vmem = pl.BlockSpec(memory_space=pltpu.VMEM)
    in_specs = [vmem] * len(args)
    aliases = {}
    if result is not None:
        aliases = {len(args): 0}
        args = (*args, result)
        in_specs.append(pl.BlockSpec(memory_space=pl.ANY))
    return pl.pallas_call(
        kernel,
        in_specs=in_specs,
        out_specs=pl.BlockSpec(memory_space=pl.ANY),
        out_shape=jax.ShapeDtypeStruct((3, NODES, depth, LANES), f32),
        scratch_shapes=[
            pltpu.VMEM((count * depth, 2 * LANES), bf16),
            pltpu.VMEM(shape, f32),
            pltpu.SemaphoreType.DMA((3,) + tuple(nodes[:-1])),
        ],
        input_output_aliases=aliases,
        compiler_params=pltpu.CompilerParams(vmem_limit_bytes=VMEM),
        cost_estimate=pl.CostEstimate(
            flops=2 * 3 * count * depth * 256 * 128,
            bytes_accessed=4 * 3 * depth * LANES * 4 * count,
            transcendentals=0,
        ),
        name=name,
    )(*args)


def local(velocity, slot_of_cell, elem_mats, geometry):
    depth = velocity.shape[1]
    parts = lax.axis_size("modes")
    layout = Layout(parts)
    rows = -(-3 * (INNER + EXTRA) // parts) * parts
    args = (velocity.transpose(0, 2, 1, 3), slot_of_cell, elem_mats.transpose(1, 0, 2), geometry)
    table = jnp.asarray(operator(layout, depth))
    table = lax.dynamic_index_in_dim(
        table, lax.rem(lax.axis_index("modes"), layout.inner), keepdims=False
    )
    z = elements("mass", (3,), layout, rows, args)
    pencil = layout.swap(*layout.divide(z))
    (u,) = elements("stiff", (0, 1, 2), None, rows, args)
    y = layout.swap(*layout.divide(spanwise(layout, pencil, table)))
    total, faces = totals(layout, u, y)
    count = lax.axis_size("dom")
    onward = [(k, (k + 1) % count) for k in range(count)]
    back = [(k, (k - 1) % count) for k in range(count)]
    if onward == back:
        before, after = lax.ppermute(faces, "dom", onward)
    else:
        before, after = lax.ppermute(faces[0], "dom", onward), lax.ppermute(faces[1], "dom", back)
    result = expand(middle_kernel, "middle", ((SIDE - 1) * (SIDE + 1),), (total, slot_of_cell))
    args = (total, before, after, slot_of_cell)
    result = expand(faces_kernel, "faces", (2, SIDE + 1), args, result)
    return result.transpose(0, 2, 1, 3)


def solution(mesh):
    in_specs = (P(None, "modes", None, "dom"), P("dom", None), P(), P(None, "dom"))
    out_specs = P(None, "modes", None, "dom")
    return jax.shard_map(local, mesh=mesh, in_specs=in_specs, out_specs=out_specs, check_vma=False)
```

time: 293 us -> 98.9 us (0.34)
  local copies, waits for them, and re-layouts: 134 us -> 2.08 us
  other arithmetic: 42.9 us -> 0.21 us
  waiting for transfers between devices: 83.2 us -> 65 us
  matrix products: 17.2 us -> 0 us
  Pallas kernels: 0 us -> 17 us
    all_to_all x2 -> x0, waiting for transfers between devices: 79.9 us -> none  [the longest x1 67 us: to_planes(): lax.all_to_all(physical, 'modes', split_axis=1, concat_axis=3, tiled=True)]
    ppermute x2 -> x19, waiting for transfers between devices: 3.3 us -> 65 us  [the longest x6 39.8 us: onward(): return lax.ppermute(value, 'modes', steps)]
    reshape x5 -> x0, local copies, waits for them, and re-layouts: 58.1 us -> none  [the longest x1 17.3 us: local(): mass_kron = jnp.einsum('ij,e,ef->iejf', elem_mats[3], block_geo[3], ident...]
    scatter x3 -> x0, local copies, waits for them, and re-layouts: 30.7 us -> none  [the longest x2 29.7 us: assemble(): cells_grid.at[:, :, :, 8, :, :-1].set(across).at[:, :, :, 0, :, 1:]]
    transpose x2 -> x0, other arithmetic: 21.9 us -> none  [the longest x1 11.6 us: local(): jnp.einsum('ij,e,ef->iejf', elem_mats[3], block_geo[3], identity, precisi...]
    dot_general x5 -> x0, matrix products: 17.2 us -> none  [the longest x1 5.55 us: local(): jnp.einsum('xy,cmy->cmx', stiff_kron, spectra, precision=lax.Precision.HI...]
    pallas_call x0 -> x6, Pallas kernels: none -> 17 us  [the longest x2 13.1 us: elements(): pl.pallas_call(functools.partial(element_kernel, terms, layout, len(shape...]
    unnamed x17 -> x10, local copies, waits for them, and re-layouts: 13.8 us -> 0.03 us
  transfers between devices with their start and end apart: 4 -> 19, of which waited for: 4 -> 11; matrix products, arithmetic and copies ran while one was open for 22% -> 2% of each run, Pallas kernels for 0% -> 8%
where the time goes in v2:
time: 98.9 us; the launch traced here: 98.7 us
  waiting for transfers between devices  65 us (66%)
  Pallas kernels  17 us (17%)
  starting transfers between devices  14 us (14%)
  local copies, waits for them, and re-layouts  2.08 us (2%)
    ppermute x6, waiting for transfers between devices, onward(): return lax.ppermute(value, 'modes', steps)  39.8 us
    ppermute x12, waiting for transfers between devices, across(): lax.ppermute(value, 'modes', pairs(s))  24.2 us
    pallas_call x2, Pallas kernels, elements(): pl.pallas_call(functools.partial(element_kernel, terms, layout, len(shape...  13.1 us
    ppermute x12, starting transfers between devices, across(): lax.ppermute(value, 'modes', pairs(s))  7.87 us
    ppermute x6, starting transfers between devices, onward(): return lax.ppermute(value, 'modes', steps)  4.56 us
    pallas_call x2, Pallas kernels, expand(): pl.pallas_call(kernel, in_specs=in_specs, out_specs=pl.BlockSpec(memory_s...  2.77 us
  transfers between devices with their start and end apart: 19, of which 11 were waited for; matrix products, arithmetic and copies ran while one was open for 2% of the time, Pallas kernels for 8%

profile of v2, /device:TPU:16, one launch (start us, length us, event | category | flops | bytes accessed | tf_op | source)
XLA Modules:
  0.0 98.7 jit_solution(13959027649688690848)
XLA Ops:
  0.0 6.6 %mass.1 = (f32[4,13,16,128]{3,2,1,0:T(8,128)}, f32[4,13,16,128]{3,2,1,0:T(8,128)}, f32[2,13,16,128]{3,2,1,0:T(8,128)}, f32[2,13,16,128]{3,2,1,0:T(8,128)}, f32[2...) custom-call(f32[3,81,16,128]{3,2,1,0:T(8,128)} %bitcast.9, s32[1,128]{1,0:T(1,128)} %slots_ref.3, ...), custom_call_target="tpu_custom_call" | custom-call | flops 339738624 | bytes 3686400 | tf_op jit(solution)/shard_map/mass/pallas_call | solution.py:260
  6.7 1.6 %collective-permute-start.4 = (f32[4,13,16,128]{3,2,1,0:T(8,128)}, f32[4,13,16,128]{3,2,1,0:T(8,128)S(1)}, u32[]{:S(2)}, u32[]{:S(2)}) collective-permute-start(f32[4,13,16,128]{3,2,1,0:T(8,128)} %get-tuple-element.23), channel_id=1, source_target_pairs={{0,8},{2,10},{4,12},{6,14},{8,16},{10,18},{12,20},{14,22},{16,24},... | collective-permute-start | bytes 1277960 | tf_op jit(solution)/shard_map/ppermute | solution.py:74
  8.3 0.0 collective-permute-start
  8.3 1.5 %collective-permute-start.1 = (f32[2,13,16,128]{3,2,1,0:T(8,128)}, f32[2,13,16,128]{3,2,1,0:T(8,128)S(1)}, u32[]{:S(2)}, u32[]{:S(2)}) collective-permute-start(f32[2,13,16,128]{3,2,1,0:T(8,128)} %get-tuple-element.21), channel_id=1, source_target_pairs={{0,4},{2,6},{4,0},{6,2},{8,12},{10,14},{12,8},{14,10},{16,20},{18,... | collective-permute-start | bytes 638984 | tf_op jit(solution)/shard_map/ppermute | solution.py:79
  9.8 0.3 collective-permute-start.2
  10.2 0.4 collective-permute-start.5
  10.6 0.9 slice.72
  11.5 0.0 collective-permute-done.refs_1_
  11.5 5.0 %collective-permute-done.1.refs_2_ = f32[2,13,16,128]{3,2,1,0:T(8,128)S(1)} collective-permute-done((f32[2,13,16,128]{3,2,1,0:T(8,128)}, f32[2,13,16,128]{3,2,1,0:T(8,128)S(1)}, u32[]{:S(2)}, u32[]{:S(2)}) %collective-permute-start.1) | collective-permute-done | bytes 213024 | tf_op jit(solution)/shard_map/ppermute | solution.py:79
  16.6 3.8 %collective-permute-done.2.refs_3_ = f32[2,13,16,128]{3,2,1,0:T(8,128)S(1)} collective-permute-done((f32[2,13,16,128]{3,2,1,0:T(8,128)}, f32[2,13,16,128]{3,2,1,0:T(8,128)S(1)}, u32[]{:S(2)}, u32[]{:S(2)}) %collective-permute-start.2) | collective-permute-done | bytes 213024 | tf_op jit(solution)/shard_map/ppermute | solution.py:79
  20.4 0.4 collective-permute-start.3
  20.8 15.9 %collective-permute-done.4 = f32[4,13,16,128]{3,2,1,0:T(8,128)S(1)} collective-permute-done((f32[4,13,16,128]{3,2,1,0:T(8,128)}, f32[4,13,16,128]{3,2,1,0:T(8,128)S(1)}, u32[]{:S(2)}, u32[]{:S(2)}) %collective-permute-start.4) | collective-permute-done | bytes 426016 | tf_op jit(solution)/shard_map/ppermute | solution.py:74
  36.8 0.0 collective-permute-done.5
  36.8 0.1 collective-permute-start.6
  37.0 1.6 %collective-permute-start.7 = (f32[2,13,16,128]{3,2,1,0:T(8,128)S(1)}, f32[2,13,16,128]{3,2,1,0:T(8,128)S(1)}, u32[]{:S(2)}, u32[]{:S(2)}) collective-permute-start(f32[2,13,16,128]{3,2,1,0:T(8,128)S(1)} %pad_maximum_fusion.4), channel_id=1, source_target_pairs={{0,4},{2,6},{4,0},{6,2},{8,12},{10,14},{12,8},{14,10},{16,20},{18,... | collective-permute-start | bytes 638984 | tf_op jit(solution)/shard_map/ppermute | solution.py:79
  38.6 0.4 collective-permute-start.8
  38.9 1.0 dynamic-slice_bitcast_fusion.refs_9_
  39.9 4.8 %collective-permute-done.3.refs_4_ = f32[4,13,16,128]{3,2,1,0:T(8,128)S(1)} collective-permute-done((f32[4,13,16,128]{3,2,1,0:T(8,128)S(1)}, f32[4,13,16,128]{3,2,1,0:T(8,128)S(1)}, u32[]{:S(2)}, u32[]{:S(2)}) %collective-permute-start.3) | collective-permute-done | bytes 426016 | tf_op jit(solution)/shard_map/ppermute | solution.py:74
  44.7 0.0 collective-permute-done.6.refs_6_
  44.7 0.4 collective-permute-done.7.refs_7_
  45.1 3.8 %collective-permute-done.8.refs_8_ = f32[2,13,16,128]{3,2,1,0:T(8,128)S(1)} collective-permute-done((f32[2,13,16,128]{3,2,1,0:T(8,128)S(1)}, f32[2,13,16,128]{3,2,1,0:T(8,128)S(1)}, u32[]{:S(2)}, u32[]{:S(2)}) %collective-permute-start.8) | collective-permute-done | bytes 213024 | tf_op jit(solution)/shard_map/ppermute | solution.py:79
  48.8 0.9 spanwise.1
  49.7 0.1 collective-permute-start.13
  49.8 0.3 collective-permute-start.9
  50.1 1.5 %collective-permute-start.10 = (f32[2,13,16,128]{3,2,1,0:T(8,128)S(1)}, f32[2,13,16,128]{3,2,1,0:T(8,128)S(1)}, u32[]{:S(2)}, u32[]{:S(2)}) collective-permute-start(f32[2,13,16,128]{3,2,1,0:T(8,128)S(1)} %get-tuple-element.27), channel_id=1, source_target_pairs={{0,4},{2,6},{4,0},{6,2},{8,12},{10,14},{12,8},{14,10},{16,20},{18,... | collective-permute-start | bytes 638984 | tf_op jit(solution)/shard_map/ppermute | solution.py:79
  51.6 0.1 collective-permute-start.11
  51.7 1.9 %collective-permute-start.14 = (f32[4,13,16,128]{3,2,1,0:T(8,128)S(1)}, f32[4,13,16,128]{3,2,1,0:T(8,128)S(1)}, u32[]{:S(2)}, u32[]{:S(2)}) collective-permute-start(f32[4,13,16,128]{3,2,1,0:T(8,128)S(1)} %get-tuple-element.30), channel_id=1, source_target_pairs={{0,24},{2,26},{4,28},{6,30},{8,0},{10,2},{12,4},{14,6},{16,8},{18,... | collective-permute-start | bytes 1277960 | tf_op jit(solution)/shard_map/ppermute | solution.py:74
  53.7 0.0 collective-permute-done.9.refs_1_
  53.7 4.5 %collective-permute-done.10.refs_2_ = f32[2,13,16,128]{3,2,1,0:T(8,128)S(1)} collective-permute-done((f32[2,13,16,128]{3,2,1,0:T(8,128)S(1)}, f32[2,13,16,128]{3,2,1,0:T(8,128)S(1)}, u32[]{:S(2)}, u32[]{:S(2)}) %collective-permute-start.10) | collective-permute-done | bytes 213024 | tf_op jit(solution)/shard_map/ppermute | solution.py:79
  58.2 0.0 copy-start
  58.2 0.0 copy-start.1
  58.2 0.0 copy-start.3
  58.2 0.0 copy-start.4
  58.2 3.2 %collective-permute-done.11.refs_3_ = f32[2,13,16,128]{3,2,1,0:T(8,128)S(1)} collective-permute-done((f32[2,13,16,128]{3,2,1,0:T(8,128)S(1)}, f32[2,13,16,128]{3,2,1,0:T(8,128)S(1)}, u32[]{:S(2)}, u32[]{:S(2)}) %collective-permute-start.11) | collective-permute-done | bytes 213024 | tf_op jit(solution)/shard_map/ppermute | solution.py:79
  61.5 0.1 collective-permute-start.12
  61.6 19.1 %collective-permute-done.13 = f32[4,13,16,128]{3,2,1,0:T(8,128)S(1)} collective-permute-done((f32[4,13,16,128]{3,2,1,0:T(8,128)S(1)}, f32[4,13,16,128]{3,2,1,0:T(8,128)S(1)}, u32[]{:S(2)}, u32[]{:S(2)}) %collective-permute-start.13) | collective-permute-done | bytes 426016 | tf_op jit(solution)/shard_map/ppermute | solution.py:74
  80.7 0.0 collective-permute-done.14
  80.8 0.1 collective-permute-start.17
  80.9 1.6 %collective-permute-start.16 = (f32[2,13,16,128]{3,2,1,0:T(8,128)S(1)}, f32[2,13,16,128]{3,2,1,0:T(8,128)S(1)}, u32[]{:S(2)}, u32[]{:S(2)}) collective-permute-start(f32[2,13,16,128]{3,2,1,0:T(8,128)S(1)} %pad_maximum_fusion.8), channel_id=1, source_target_pairs={{0,4},{2,6},{4,0},{6,2},{8,12},{10,14},{12,8},{14,10},{16,20},{18,... | collective-permute-start | bytes 638984 | tf_op jit(solution)/shard_map/ppermute | solution.py:79
  82.5 0.4 collective-permute-start.15
  82.9 6.5 %stiff.1.u_ref = f32[208,16,128]{2,1,0:T(8,128)S(1)} custom-call(f32[3,81,16,128]{3,2,1,0:T(8,128)S(1)} %bitcast.10, s32[1,128]{1,0:T(1,128)S(1)} %copy-done.4, f32[81,4,81]{2,1,0:T(4,128)S(1)} %bitcast.12, f32[4,128]{1,0:T(4,128)S(1)} %copy-done.3), custom_call_target="tpu_custom_call" | custom-call | flops 1019215872 | bytes 3686400 | tf_op jit(solution)/shard_map/stiff/pallas_call | solution.py:260
  89.4 0.0 collective-permute-done.17.refs_8_
  89.4 3.5 %collective-permute-done.16.refs_7_ = f32[2,13,16,128]{3,2,1,0:T(8,128)S(1)} collective-permute-done((f32[2,13,16,128]{3,2,1,0:T(8,128)S(1)}, f32[2,13,16,128]{3,2,1,0:T(8,128)S(1)}, u32[]{:S(2)}, u32[]{:S(2)}) %collective-permute-start.16) | collective-permute-done | bytes 213024 | tf_op jit(solution)/shard_map/ppermute | solution.py:79
  93.0 0.2 totals.1
  93.2 1.6 %collective-permute-start.18 = (f32[2,3,16,128]{3,2,1,0:T(8,128)S(1)}, f32[2,3,16,128]{3,2,1,0:T(8,128)S(1)}, u32[]{:S(2)}, u32[]{:S(2)}) collective-permute-start(f32[2,3,16,128]{3,2,1,0:T(8,128)S(1)} %get-tuple-element.32), channel_id=1, source_target_pairs={{0,1},{1,0},{2,3},{3,2},{4,5},{5,4},{6,7},{7,6},{8,9},{9,8},{10,11... | collective-permute-start | bytes 147464 | tf_op jit(solution)/shard_map/ppermute | solution.py:474
  94.7 1.6 %middle.1._ = f32[3,81,16,128]{3,2,1,0:T(8,128)} custom-call(f32[208,16,128]{2,1,0:T(8,128)S(1)} %get-tuple-element.31.t_ref, s32[1,128]{1,0:T(1,128)S(1)} %copy-done.4), custom_call_target="tpu_custom_call" | custom-call | flops 198180864 | bytes 6193152 | tf_op jit(solution)/shard_map/middle/pallas_call | solution.py:434
  96.3 1.0 %collective-permute-done.18 = f32[2,3,16,128]{3,2,1,0:T(8,128)S(1)} collective-permute-done((f32[2,3,16,128]{3,2,1,0:T(8,128)S(1)}, f32[2,3,16,128]{3,2,1,0:T(8,128)S(1)}, u32[]{:S(2)}, u32[]{:S(2)}) %collective-permute-start.18) | collective-permute-done | bytes 49184 | tf_op jit(solution)/shard_map/ppermute | solution.py:474
  97.3 1.2 %faces.1 = f32[3,81,16,128]{3,2,1,0:T(8,128)} custom-call(f32[208,16,128]{2,1,0:T(8,128)S(1)} %get-tuple-element.31.t_ref, f32[3,16,128]{2,1,0:T(8,128)S(1)} %get-tuple-element.50.before_ref, f32[3,16,128]{2,1,0:T(8,128)S(1)} %get-tuple-element.49.after_ref, s32[1,128]{1,0:T(1,128)S(1)} %copy-done.4, ...), custom_call_target="tpu_custom_call", output_to_operand_aliasing={{}: (4, {})} | custom-call | flops 56623104 | bytes 1769472 | tf_op jit(solution)/shard_map/faces/pallas_call | solution.py:434
  (30 shorter events, 0.4 us)
Async XLA Ops:
  6.7 30.1 %collective-permute-start.4 = (f32[4,13,16,128]{3,2,1,0:T(8,128)}, f32[4,13,16,128]{3,2,1,0:T(8,128)S(1)}, u32[]{:S(2)}, u32[]{:S(2)}) collective-permute-start(f32[4,13,16,128]{3,2,1,0:T(8,128)} %get-tuple-element.23), channel_id=1, source_target_pairs={{0,8},{2,10},{4,12},{6,14},{8,16},{10,18},{12,20},{14,22},{16,24},... | collective-permute-start | bytes 1277960 | tf_op jit(solution)/shard_map/ppermute | solution.py:74
  8.3 3.2 %collective-permute-start = (f32[2,13,16,128]{3,2,1,0:T(8,128)}, f32[2,13,16,128]{3,2,1,0:T(8,128)S(1)}, u32[]{:S(2)}, u32[]{:S(2)}) collective-permute-start(f32[2,13,16,128]{3,2,1,0:T(8,128)} %get-tuple-element.20), channel_id=1, source_target_pairs={{0,2},{2,0},{4,6},{6,4},{8,10},{10,8},{12,14},{14,12},{16,18},{18,... | collective-permute-start | bytes 638984 | tf_op jit(solution)/shard_map/ppermute | solution.py:79
  8.3 8.3 %collective-permute-start.1 = (f32[2,13,16,128]{3,2,1,0:T(8,128)}, f32[2,13,16,128]{3,2,1,0:T(8,128)S(1)}, u32[]{:S(2)}, u32[]{:S(2)}) collective-permute-start(f32[2,13,16,128]{3,2,1,0:T(8,128)} %get-tuple-element.21), channel_id=1, source_target_pairs={{0,4},{2,6},{4,0},{6,2},{8,12},{10,14},{12,8},{14,10},{16,20},{18,... | collective-permute-start | bytes 638984 | tf_op jit(solution)/shard_map/ppermute | solution.py:79
  9.8 10.5 %collective-permute-start.2 = (f32[2,13,16,128]{3,2,1,0:T(8,128)}, f32[2,13,16,128]{3,2,1,0:T(8,128)S(1)}, u32[]{:S(2)}, u32[]{:S(2)}) collective-permute-start(f32[2,13,16,128]{3,2,1,0:T(8,128)} %get-tuple-element.22), channel_id=1, source_target_pairs={{0,6},{2,4},{4,2},{6,0},{8,14},{10,12},{12,10},{14,8},{16,22},{18,... | collective-permute-start | bytes 638984 | tf_op jit(solution)/shard_map/ppermute | solution.py:79
  10.2 26.6 %collective-permute-start.5 = (f32[4,13,16,128]{3,2,1,0:T(8,128)}, f32[4,13,16,128]{3,2,1,0:T(8,128)S(1)}, u32[]{:S(2)}, u32[]{:S(2)}) collective-permute-start(f32[4,13,16,128]{3,2,1,0:T(8,128)} %get-tuple-element.24), channel_id=1, source_target_pairs={{0,24},{2,26},{4,28},{6,30},{8,0},{10,2},{12,4},{14,6},{16,8},{18,... | collective-permute-start | bytes 1277960 | tf_op jit(solution)/shard_map/ppermute | solution.py:74
  20.4 28.4 %copy-start.2 = (f32[2,13,16,128]{3,2,1,0:T(8,128)S(1)}, f32[2,13,16,128]{3,2,1,0:T(8,128)}, u32[]{:S(2)}) copy-start(f32[2,13,16,128]{3,2,1,0:T(8,128)} %get-tuple-element.19.refs_0_) | copy-start | bytes 638980
  20.4 24.3 %collective-permute-start.3 = (f32[4,13,16,128]{3,2,1,0:T(8,128)S(1)}, f32[4,13,16,128]{3,2,1,0:T(8,128)S(1)}, u32[]{:S(2)}, u32[]{:S(2)}) collective-permute-start(f32[4,13,16,128]{3,2,1,0:T(8,128)S(1)} %pad_maximum_fusion), channel_id=1, source_target_pairs={{0,16},{2,18},{4,20},{6,22},{8,24},{10,26},{12,28},{14,30},{16,0},... | collective-permute-start | bytes 1277960 | tf_op jit(solution)/shard_map/ppermute | solution.py:74
  36.8 7.8 %collective-permute-start.6 = (f32[2,13,16,128]{3,2,1,0:T(8,128)S(1)}, f32[2,13,16,128]{3,2,1,0:T(8,128)S(1)}, u32[]{:S(2)}, u32[]{:S(2)}) collective-permute-start(f32[2,13,16,128]{3,2,1,0:T(8,128)S(1)} %pad_maximum_fusion.3), channel_id=1, source_target_pairs={{0,2},{2,0},{4,6},{6,4},{8,10},{10,8},{12,14},{14,12},{16,18},{18,... | collective-permute-start | bytes 638984 | tf_op jit(solution)/shard_map/ppermute | solution.py:79
  37.0 8.1 %collective-permute-start.7 = (f32[2,13,16,128]{3,2,1,0:T(8,128)S(1)}, f32[2,13,16,128]{3,2,1,0:T(8,128)S(1)}, u32[]{:S(2)}, u32[]{:S(2)}) collective-permute-start(f32[2,13,16,128]{3,2,1,0:T(8,128)S(1)} %pad_maximum_fusion.4), channel_id=1, source_target_pairs={{0,4},{2,6},{4,0},{6,2},{8,12},{10,14},{12,8},{14,10},{16,20},{18,... | collective-permute-start | bytes 638984 | tf_op jit(solution)/shard_map/ppermute | solution.py:79
  38.6 10.3 %collective-permute-start.8 = (f32[2,13,16,128]{3,2,1,0:T(8,128)S(1)}, f32[2,13,16,128]{3,2,1,0:T(8,128)S(1)}, u32[]{:S(2)}, u32[]{:S(2)}) collective-permute-start(f32[2,13,16,128]{3,2,1,0:T(8,128)S(1)} %pad_maximum_fusion.5), channel_id=1, source_target_pairs={{0,6},{2,4},{4,2},{6,0},{8,14},{10,12},{12,10},{14,8},{16,22},{18,... | collective-permute-start | bytes 638984 | tf_op jit(solution)/shard_map/ppermute | solution.py:79
  49.7 31.0 %collective-permute-start.13 = (f32[4,13,16,128]{3,2,1,0:T(8,128)S(1)}, f32[4,13,16,128]{3,2,1,0:T(8,128)S(1)}, u32[]{:S(2)}, u32[]{:S(2)}) collective-permute-start(f32[4,13,16,128]{3,2,1,0:T(8,128)S(1)} %get-tuple-element.29), channel_id=1, source_target_pairs={{0,8},{2,10},{4,12},{6,14},{8,16},{10,18},{12,20},{14,22},{16,24},... | collective-permute-start | bytes 1277960 | tf_op jit(solution)/shard_map/ppermute | solution.py:74
  49.8 3.9 %collective-permute-start.9 = (f32[2,13,16,128]{3,2,1,0:T(8,128)S(1)}, f32[2,13,16,128]{3,2,1,0:T(8,128)S(1)}, u32[]{:S(2)}, u32[]{:S(2)}) collective-permute-start(f32[2,13,16,128]{3,2,1,0:T(8,128)S(1)} %get-tuple-element.26), channel_id=1, source_target_pairs={{0,2},{2,0},{4,6},{6,4},{8,10},{10,8},{12,14},{14,12},{16,18},{18,... | collective-permute-start | bytes 638984 | tf_op jit(solution)/shard_map/ppermute | solution.py:79
  50.1 8.1 %collective-permute-start.10 = (f32[2,13,16,128]{3,2,1,0:T(8,128)S(1)}, f32[2,13,16,128]{3,2,1,0:T(8,128)S(1)}, u32[]{:S(2)}, u32[]{:S(2)}) collective-permute-start(f32[2,13,16,128]{3,2,1,0:T(8,128)S(1)} %get-tuple-element.27), channel_id=1, source_target_pairs={{0,4},{2,6},{4,0},{6,2},{8,12},{10,14},{12,8},{14,10},{16,20},{18,... | collective-permute-start | bytes 638984 | tf_op jit(solution)/shard_map/ppermute | solution.py:79
  51.6 9.8 %collective-permute-start.11 = (f32[2,13,16,128]{3,2,1,0:T(8,128)S(1)}, f32[2,13,16,128]{3,2,1,0:T(8,128)S(1)}, u32[]{:S(2)}, u32[]{:S(2)}) collective-permute-start(f32[2,13,16,128]{3,2,1,0:T(8,128)S(1)} %get-tuple-element.28), channel_id=1, source_target_pairs={{0,6},{2,4},{4,2},{6,0},{8,14},{10,12},{12,10},{14,8},{16,22},{18,... | collective-permute-start | bytes 638984 | tf_op jit(solution)/shard_map/ppermute | solution.py:79
  51.7 29.0 %collective-permute-start.14 = (f32[4,13,16,128]{3,2,1,0:T(8,128)S(1)}, f32[4,13,16,128]{3,2,1,0:T(8,128)S(1)}, u32[]{:S(2)}, u32[]{:S(2)}) collective-permute-start(f32[4,13,16,128]{3,2,1,0:T(8,128)S(1)} %get-tuple-element.30), channel_id=1, source_target_pairs={{0,24},{2,26},{4,28},{6,30},{8,0},{10,2},{12,4},{14,6},{16,8},{18,... | collective-permute-start | bytes 1277960 | tf_op jit(solution)/shard_map/ppermute | solution.py:74
  58.2 24.7 %copy-start = (f32[3,16,81,128]{3,1,2,0:T(8,128)S(1)}, f32[3,16,81,128]{3,1,2,0:T(8,128)}, u32[]{:S(2)}) copy-start(f32[3,16,81,128]{3,1,2,0:T(8,128)} %param.5) | copy-start | bytes 5971972
  58.2 24.7 %copy-start.1 = (f32[4,81,81]{2,0,1:T(4,128)S(1)}, f32[4,81,81]{2,0,1:T(4,128)}, u32[]{:S(2)}) copy-start(f32[4,81,81]{2,0,1:T(4,128)} %param.7) | copy-start | bytes 314932
  58.2 24.7 %copy-start.3 = (f32[4,128]{1,0:T(4,128)S(1)}, f32[4,128]{1,0:T(4,128)}, u32[]{:S(2)}) copy-start(f32[4,128]{1,0:T(4,128)} %refs_3_.3) | copy-start | bytes 6148
  58.2 24.7 %copy-start.4 = (s32[1,128]{1,0:T(1,128)S(1)}, s32[1,128]{1,0:T(1,128)}, u32[]{:S(2)}) copy-start(s32[1,128]{1,0:T(1,128)} %slots_ref.3) | copy-start | bytes 1540
  61.5 31.5 %collective-permute-start.12 = (f32[4,13,16,128]{3,2,1,0:T(8,128)S(1)}, f32[4,13,16,128]{3,2,1,0:T(8,128)S(1)}, u32[]{:S(2)}, u32[]{:S(2)}) collective-permute-start(f32[4,13,16,128]{3,2,1,0:T(8,128)S(1)} %pad_maximum_fusion.1), channel_id=1, source_target_pairs={{0,16},{2,18},{4,20},{6,22},{8,24},{10,26},{12,28},{14,30},{16,0},... | collective-permute-start | bytes 1277960 | tf_op jit(solution)/shard_map/ppermute | solution.py:74
  80.8 8.6 %collective-permute-start.17 = (f32[2,13,16,128]{3,2,1,0:T(8,128)S(1)}, f32[2,13,16,128]{3,2,1,0:T(8,128)S(1)}, u32[]{:S(2)}, u32[]{:S(2)}) collective-permute-start(f32[2,13,16,128]{3,2,1,0:T(8,128)S(1)} %pad_maximum_fusion.9), channel_id=1, source_target_pairs={{0,6},{2,4},{4,2},{6,0},{8,14},{10,12},{12,10},{14,8},{16,22},{18,... | collective-permute-start | bytes 638984 | tf_op jit(solution)/shard_map/ppermute | solution.py:79
  80.9 12.1 %collective-permute-start.16 = (f32[2,13,16,128]{3,2,1,0:T(8,128)S(1)}, f32[2,13,16,128]{3,2,1,0:T(8,128)S(1)}, u32[]{:S(2)}, u32[]{:S(2)}) collective-permute-start(f32[2,13,16,128]{3,2,1,0:T(8,128)S(1)} %pad_maximum_fusion.8), channel_id=1, source_target_pairs={{0,4},{2,6},{4,0},{6,2},{8,12},{10,14},{12,8},{14,10},{16,20},{18,... | collective-permute-start | bytes 638984 | tf_op jit(solution)/shard_map/ppermute | solution.py:79
  82.5 10.5 %collective-permute-start.15 = (f32[2,13,16,128]{3,2,1,0:T(8,128)S(1)}, f32[2,13,16,128]{3,2,1,0:T(8,128)S(1)}, u32[]{:S(2)}, u32[]{:S(2)}) collective-permute-start(f32[2,13,16,128]{3,2,1,0:T(8,128)S(1)} %pad_maximum_fusion.7), channel_id=1, source_target_pairs={{0,2},{2,0},{4,6},{6,4},{8,10},{10,8},{12,14},{14,12},{16,18},{18,... | collective-permute-start | bytes 638984 | tf_op jit(solution)/shard_map/ppermute | solution.py:79
  93.2 4.2 %collective-permute-start.18 = (f32[2,3,16,128]{3,2,1,0:T(8,128)S(1)}, f32[2,3,16,128]{3,2,1,0:T(8,128)S(1)}, u32[]{:S(2)}, u32[]{:S(2)}) collective-permute-start(f32[2,3,16,128]{3,2,1,0:T(8,128)S(1)} %get-tuple-element.32), channel_id=1, source_target_pairs={{0,1},{1,0},{2,3},{3,2},{4,5},{5,4},{6,7},{7,6},{8,9},{9,8},{10,11... | collective-permute-start | bytes 147464 | tf_op jit(solution)/shard_map/ppermute | solution.py:474

commit v3 on v2

--- a/solution.py
+++ b/solution.py
@@ -16,8 +16,12 @@
 SIDE = 8
 INNER = SIDE * (SIDE - 1)
 FACE = SIDE * EY
-ACROSS, RIGHT, LEFT, EXTRA = SIDE, SIDE + 1, SIDE + 2, SIDE + 3
+FULL = SIDE * SIDE
+ENDS = 3 * FULL
+HALF = LANES // 2
+HALVES = 10
 DEEP = 96
+TALL = 88
 VMEM = 48 * 1024 * 1024
 WIDE = 60 * 1024 * 1024
 
@@ -128,47 +132,48 @@
     return face
 
 
-def prepare(terms, slots_ref, mats_ref, geo_ref, left_ref, cells_ref):
-    select = selector(slots_ref[...])
-    geo = jnp.dot(geo_ref[...], select, precision=lax.Precision.HIGHEST, preferred_element_type=f32)
+def prepare(terms, slots_ref, mats_ref, left_ref):
+    select = selector(slots_ref[...]).astype(bf16)
     left_ref[...] = jnp.zeros_like(left_ref)
     for place, term in enumerate(terms):
         high, low = split(mats_ref[:, term, :])
         left_ref[place, :NODES, 0:NODES] = high
-        left_ref[place, :NODES, DEEP : DEEP + NODES] = high
-        left_ref[place, :NODES, 2 * DEEP : 2 * DEEP + NODES] = low
-    depth = cells_ref.shape[1] // DEEP
-    cells_ref[:, NODES * depth :, :] = jnp.zeros((2, (DEEP - NODES) * depth, LANES), f32)
-    return select.astype(bf16), geo
-
-
-def component(terms, first, second, select, geo, left, cells_ref, nodes_ref, inner, extra):
+        left_ref[place, :NODES, NODES : NODES + 1] = low[:, NODES - 1 :]
+        left_ref[place, :NODES, TALL : TALL + NODES] = high
+        left_ref[place, :NODES, 2 * TALL :] = low[:, : NODES - 1]
+    return jnp.concatenate([select, select], axis=0)
+
+
+def component(terms, first, second, select, geo, left, scratch, row, ends, face):
+    values_ref, images_ref, cells_ref = scratch
     depth = first.shape[1]
-    product = (first[...] * second[...]).reshape(NODES * depth, LANES)
-    for place, part in enumerate(split(product)):
-        cells_ref[place, : NODES * depth, :] = jnp.dot(part, select, preferred_element_type=f32)
-    for pair in range(depth // 2):
-        parts = [
-            jnp.concatenate(
-                [cells_ref[k, pl.ds(2 * pair + p, DEEP, stride=depth), :] for p in (0, 1)], axis=1
-            ).astype(bf16)
-            for k in (0, 1)
-        ]
-        right = jnp.concatenate([parts[0], parts[1], parts[0]], axis=0)
-        images = jnp.dot(left, right, preferred_element_type=f32)
+    count = NODES * depth
+    values_ref[:count] = (first[...] * second[...]).reshape(count, LANES)
+    values_ref[count : count + depth] = values_ref[count - depth : count]
+    for pair in range(0, depth, 2):
+        right = []
+        for p in (pair, pair + 1):
+            value = values_ref[pl.ds(p, TALL, stride=depth), :]
+            high = value.astype(bf16).astype(f32)
+            parts = jnp.concatenate([high, value - high, high[: NODES - 1]], axis=0)
+            right.append(parts.astype(bf16))
+        images = jnp.dot(left, jnp.concatenate(right, axis=1), preferred_element_type=f32)
         for p in (0, 1):
             total = 0.0
             for t, term in enumerate(terms):
                 total = total + (
-                    images[DEEP * t : DEEP * t + 88, LANES * p : LANES * p + LANES]
+                    images[DEEP * t : DEEP * t + DEEP, LANES * p : LANES * p + LANES]
                     * geo[term : term + 1]
                 )
-            nodes_ref[pl.ds(2 * pair + p, 88, stride=depth), :] = total
+            high, low = split(total)
+            images_ref[(pair + p) * DEEP : (pair + p + 1) * DEEP, :LANES] = high
+            images_ref[(pair + p) * DEEP : (pair + p + 1) * DEEP, LANES:] = low
+    cells_ref[...] = jnp.dot(images_ref[...], select, preferred_element_type=f32)
     lane = lane_index(depth)
     across = lane % EY
 
     def node(i, j):
-        value = nodes_ref[(9 * i + j) * depth : (9 * i + j + 1) * depth, :]
+        value = cells_ref[pl.ds((SIDE + 1) * i + j, depth, stride=DEEP), :]
         if i > 0:
             return value
         return value + jnp.where(lane >= EY, roll(node(8, j), EY), 0.0)
@@ -182,80 +187,126 @@
         column[0] = join(column[0], column[SIDE])
         if i < SIDE:
             for j in range(SIDE):
-                inner(SIDE * (i - 1) + j, column[j]) if i else extra(j, column[j])
+                row(SIDE * (i - 1) + j if i else INNER + j, column[j])
             end = jnp.where(across == i, roll(column[SIDE], i + 1 - EY), end)
-        if i in (0, SIDE):
-            extra(RIGHT if i else LEFT, gather_face(column, LANES - EY if i else 0))
-    extra(ACROSS, end)
+    ends(end)
+    face(gather_face(column, LANES - EY))
+
+
+def pack(value, half):
+    lane = lane_index(value.shape[0] // 2)
+    top, bottom = value[: value.shape[0] // 2], value[value.shape[0] // 2 :]
+    if half:
+        return jnp.where(lane < HALF, roll(top, HALF), bottom)
+    return jnp.where(lane < HALF, top, roll(bottom, HALF))
+
+
+def unpack(packed):
+    return jnp.concatenate([packed, roll(packed, HALF)], axis=0)
 
 
 def element_kernel(terms, layout, count, *refs):
     vel_hbm, slots_hbm, mats_hbm, geo_hbm = refs[:4]
     outs, scratch = refs[4 : 4 + count], refs[4 + count :]
-    vel_ref, slots_ref, mats_ref, geo_ref, left_ref, cells_ref, nodes_ref, sems = scratch[:8]
-    out_ref = scratch[8] if layout else outs[0]
+    vel_ref, slots_ref, mats_ref, geo_ref, left_ref, *parts, sems = scratch[:9]
     pairs = [(slots_hbm, slots_ref), (geo_hbm, geo_ref), (mats_hbm, mats_ref)]
     pairs += [(vel_hbm.at[c], vel_ref.at[c]) for c in range(3)]
     copies = [pltpu.make_async_copy(*pair, sems.at[k]) for k, pair in enumerate(pairs)]
     for copy in copies:
         copy.start()
+    depth = vel_ref.shape[2]
+    spare = (TALL - NODES) * depth
+    parts[0][NODES * depth :] = jnp.zeros((spare, LANES), f32)
     for copy in copies[:3]:
         copy.wait()
-    select, geo = prepare(terms, slots_ref, mats_ref, geo_ref, left_ref, cells_ref)
-    left = left_ref[...].reshape(len(terms) * DEEP, 3 * DEEP)
-
-    def put(first, row, value):
-        out_ref[first + row] = value
+    select = prepare(terms, slots_ref, mats_ref, left_ref)
+    left = left_ref[...].reshape(len(terms) * DEEP, 2 * LANES)
+    geo = geo_ref[...]
+    if layout:
+        rows_ref, halves_ref, send_sems = scratch[9:]
+        halves_ref[...] = jnp.zeros_like(halves_ref)
+    else:
+        (out_ref,) = outs
+    lane = lane_index(depth)
+    corners = [jnp.zeros((depth, LANES), f32)]
+
+    def put_row(c, row, value):
+        if layout:
+            rows_ref[(c * FULL + row) * depth : (c * FULL + row + 1) * depth] = value
+        else:
+            out_ref[c * FULL + row] = value
+
+    def put_half(at, value):
+        halves_ref[at * depth // 2 : (at + 1) * depth // 2] = value
+
+    def put_ends(c, value):
+        if layout:
+            put_half(2 * c, pack(value, 0))
+            put_half(2 * c + 1, pack(value, 1))
+        else:
+            out_ref[ENDS + 2 * c] = value
+
+    def put_face(c, value):
+        if layout:
+            put_half(6 + c, pack(value, 0))
+            corners[0] = jnp.where(lane == c, roll(value, c - FACE), corners[0])
+        else:
+            out_ref[ENDS + 2 * c + 1] = value
+
+    sends = []
+    if layout:
+        early, late = layout.divide(outs)
+        for k, s in layout.blocks:
+            place, target, done = layout.place(k, s), layout.sent(k, s, early, late), 0
+            for ref in (rows_ref, halves_ref):
+                size = ref.shape[0] // len(layout.blocks)
+                source = ref.at[pl.ds(pl.multiple_of(place * size, 8), size)]
+                sem = send_sems.at[len(sends)]
+                target_part = target.at[pl.ds(done, size)]
+                sends.append((place, pltpu.make_async_copy(source, target_part, sem)))
+                done += size
 
     copies[3].wait()
+    ready = 0
     for c in range(3):
         if c < 2:
             copies[4 + c].wait()
-        component(
-            terms,
-            vel_ref.at[c],
-            vel_ref.at[(c + 1) % 3],
-            select,
-            geo,
-            left,
-            cells_ref,
-            nodes_ref,
-            functools.partial(put, c * INNER),
-            functools.partial(put, 3 * INNER + c * EXTRA),
-        )
-    for row in range(3 * (INNER + EXTRA), out_ref.shape[0]):
-        out_ref[row] = jnp.zeros(out_ref.shape[1:], f32)
+        puts = [functools.partial(put, c) for put in (put_row, put_ends, put_face)]
+        first, second = vel_ref.at[c], vel_ref.at[(c + 1) % 3]
+        component(terms, first, second, select, geo, left, parts, *puts)
+        if layout:
+            before, ready = ready, (c + 1) * FULL * depth * len(layout.blocks) // rows_ref.shape[0]
+            ready = len(layout.blocks) if c == 2 else ready
+            for place, copy in sends[::2]:
+                pl.when(jnp.logical_and(place >= before, place < ready))(copy.start)
     if layout:
-        send_sems = scratch[9]
-        share = out_ref.shape[0] // len(layout.blocks)
-        early, late = layout.divide(outs)
-        copies = [
-            pltpu.make_async_copy(
-                out_ref.at[pl.ds(layout.place(k, s) * share, share)],
-                layout.sent(k, s, early, late),
-                send_sems.at[at],
-            )
-            for at, (k, s) in enumerate(layout.blocks)
-        ]
-        for copy in copies:
+        put_half(9, pack(corners[0], 0))
+        for _, copy in sends[1::2]:
             copy.start()
-        for copy in copies:
+        for _, copy in sends:
             copy.wait()
 
 
-def elements(name, terms, layout, rows, args):
+def shares(parts, depth):
+    return -(-ENDS // parts) * depth, -(-HALVES // parts) * depth // 2
+
+
+def elements(name, terms, layout, args):
     depth = args[0].shape[2]
     scratch = [
         *(pltpu.VMEM(a.shape, a.dtype) for a in args),
-        pltpu.VMEM((len(terms), DEEP, 3 * DEEP), bf16),
-        pltpu.VMEM((2, DEEP * depth, LANES), f32),
-        pltpu.VMEM((88 * depth, LANES), f32),
+        pltpu.VMEM((len(terms), DEEP, 2 * LANES), bf16),
+        pltpu.VMEM((TALL * depth, LANES), f32),
+        pltpu.VMEM((DEEP * depth, 2 * LANES), bf16),
+        pltpu.VMEM((DEEP * depth, LANES), f32),
         pltpu.SemaphoreType.DMA((6,)),
     ]
-    shapes = [(rows, depth, LANES)]
+    shapes = [(ENDS + 6, depth, LANES)]
     if layout:
-        scratch += [pltpu.VMEM(shapes[0], f32), pltpu.SemaphoreType.DMA((len(layout.blocks),))]
-        shapes = layout.shapes((rows // len(layout.blocks), depth, LANES))
+        sizes = shares(len(layout.blocks), depth)
+        scratch += [pltpu.VMEM((len(layout.blocks) * size, LANES), f32) for size in sizes]
+        scratch.append(pltpu.SemaphoreType.DMA((2 * len(layout.blocks),)))
+        shapes = layout.shapes((sum(sizes), LANES))
     anywhere = pl.BlockSpec(memory_space=pl.ANY)
     return pl.pallas_call(
         functools.partial(element_kernel, terms, layout, len(shapes)),
@@ -273,40 +324,43 @@
     )(*args)
 
 
-def spanwise_kernel(layout, count, *refs):
+def spanwise_kernel(layout, depth, count, *refs):
     got = layout.got(refs[:count])
     table_ref, early, late = refs[count], *layout.divide(refs[count + 1 :])
-    share, depth, lanes = late[0].shape[1:]
+    full, _ = shares(len(layout.blocks), depth)
     length = len(layout.blocks) * depth
     table = table_ref[...]
-    for r in range(0, share, 2):
-        width = min(2, share - r)
-        x = [
-            jnp.concatenate([got[block][r + k] for block in layout.blocks], axis=0)
-            for k in range(width)
-        ]
-        x = x[0] if width == 1 else jnp.concatenate(x, axis=1)
-        x_high, x_low = split(x)
+    rows = [(at, depth) for at in range(0, full, depth)]
+    rows += [(at, depth // 2) for at in range(full, late[0].shape[1], depth // 2)]
+    for first in range(0, len(rows), 2):
+        group = rows[first : first + 2]
+        x = []
+        for at, size in group:
+            blocks = [got[block][at : at + size] for block in layout.blocks]
+            if size < depth:
+                blocks = [unpack(block) for block in blocks]
+            x.append(jnp.concatenate(blocks, axis=0))
+        x_high, x_low = split(jnp.concatenate(x, axis=1))
         y = jnp.dot(table, x_high, preferred_element_type=f32)
         y = y[:length] + y[length:]
         y += jnp.dot(table[:length], x_low, preferred_element_type=f32)
-        for at, block in enumerate(layout.blocks):
-            for k in range(width):
-                layout.sent(*block, early, late)[r + k] = y[
-                    depth * at : depth * at + depth, lanes * k : lanes * k + lanes
-                ]
-
-
-def spanwise(layout, values, table):
+        for place, block in enumerate(layout.blocks):
+            for k, (at, size) in enumerate(group):
+                value = y[depth * place : depth * place + depth, LANES * k : LANES * k + LANES]
+                value = value if size == depth else pack(value, 0)
+                layout.sent(*block, early, late)[at : at + size] = value
+
+
+def spanwise(layout, depth, values, table):
     share = values[0].shape[1:]
-    length = len(layout.blocks) * share[1]
+    length = len(layout.blocks) * depth
     return pl.pallas_call(
-        functools.partial(spanwise_kernel, layout, len(values)),
+        functools.partial(spanwise_kernel, layout, depth, len(values)),
         out_shape=[jax.ShapeDtypeStruct(shape, f32) for shape in layout.shapes(share)],
         compiler_params=pltpu.CompilerParams(vmem_limit_bytes=VMEM),
         cost_estimate=pl.CostEstimate(
-            flops=6 * length * length * share[0] * LANES,
-            bytes_accessed=8 * length * share[0] * LANES,
+            flops=6 * length * len(layout.blocks) * share[0] * LANES,
+            bytes_accessed=8 * len(layout.blocks) * share[0] * LANES,
             transcendentals=0,
         ),
         name="spanwise",
@@ -314,22 +368,44 @@
 
 
 def total_kernel(layout, u_ref, *refs):
-    total_ref, faces_ref = refs[-2:]
-    for (k, s), ref in layout.got(refs[:-2]).items():
-        share = ref.shape[0]
-        rows = pl.ds(layout.place(-k, s) * share, share)
-        total_ref[rows] = u_ref[rows] + ref[...]
-    for place, row in enumerate((RIGHT, LEFT)):
-        for c in range(3):
-            faces_ref[place, c] = total_ref[3 * INNER + c * EXTRA + row]
+    total_ref, faces_ref, rows_ref, halves_ref = refs[-4:]
+    depth = u_ref.shape[1]
+    full, half = shares(len(layout.blocks), depth)
+    for (k, s), ref in layout.got(refs[:-4]).items():
+        place = layout.place(-k, s)
+        rows_ref[pl.ds(place * (full // depth), full // depth)] = ref[:full].reshape(
+            full // depth, depth, LANES
+        )
+        halves_ref[pl.ds(pl.multiple_of(place * half, 8), half)] = ref[full:]
+    total_ref[:ENDS] = u_ref[:ENDS] + rows_ref[:ENDS]
+    lane = lane_index(depth)
+    halves = [
+        unpack(halves_ref[at * depth // 2 : (at + 1) * depth // 2]) for at in range(HALVES)
+    ]
+    for c in range(3):
+        end = jnp.where(lane < HALF, halves[2 * c], roll(halves[2 * c + 1], HALF))
+        end += u_ref[ENDS + 2 * c]
+        face = jnp.where(lane == FACE, roll(halves[9], FACE - c), halves[6 + c])
+        face += u_ref[ENDS + 2 * c + 1]
+        total_ref[ENDS + 2 * c] = end
+        total_ref[ENDS + 2 * c + 1] = face
+        faces_ref[0, c] = face
+        column = [total_ref[c * FULL + INNER + j] for j in range(SIDE)]
+        faces_ref[1, c] = gather_face(column + [roll(end, EY - 1)], 0)
 
 
 def totals(layout, u, values):
+    depth = u.shape[1]
+    full, half = shares(len(layout.blocks), depth)
     return pl.pallas_call(
         functools.partial(total_kernel, layout),
         out_shape=[
             jax.ShapeDtypeStruct(u.shape, f32),
-            jax.ShapeDtypeStruct((2, 3) + u.shape[1:], f32),
+            jax.ShapeDtypeStruct((2, 3, depth, LANES), f32),
+        ],
+        scratch_shapes=[
+            pltpu.VMEM((len(layout.blocks) * full // depth, depth, LANES), f32),
+            pltpu.VMEM((len(layout.blocks) * half, LANES), f32),
         ],
         compiler_params=pltpu.CompilerParams(vmem_limit_bytes=VMEM),
         cost_estimate=pl.CostEstimate(flops=u.size, bytes_accessed=12 * u.size, transcendentals=0),
@@ -353,7 +429,7 @@
     count = (SIDE - 1) * (SIDE + 1)
     copies = []
     for c in range(3):
-        end = t_ref[3 * INNER + c * EXTRA + ACROSS]
+        end = t_ref[ENDS + 2 * c]
 
         def put(at, value):
             high, low = split(value)
@@ -361,7 +437,7 @@
 
         for i in range(1, SIDE):
             for j in range(SIDE):
-                value = t_ref[c * INNER + SIDE * (i - 1) + j]
+                value = t_ref[c * FULL + SIDE * (i - 1) + j]
                 put((SIDE + 1) * (i - 1) + j, value)
                 if j == 0:
                     last = jnp.where(across == EY - 1, roll(end, EY - 1 - i), roll(value, -1))
@@ -386,17 +462,16 @@
     count = SIDE + 1
     copies = []
     for c in range(3):
-        extra = lambda k: t_ref[3 * INNER + c * EXTRA + k]
         before = before_ref[c]
-        face = extra(RIGHT) + after_ref[c]
-        end = extra(ACROSS) + jnp.where(lane == 0, roll(before, -FACE), 0.0)
+        face = t_ref[ENDS + 2 * c + 1] + after_ref[c]
+        end = t_ref[ENDS + 2 * c] + jnp.where(lane == 0, roll(before, -FACE), 0.0)
 
         def put(at, value):
             high, low = split(value)
             nodes_ref[pl.ds(at * depth, depth), :] = jnp.concatenate([high, low], axis=1)
 
         for j in range(SIDE):
-            value = extra(j) + jnp.where(lane < EY, roll(before, -EY * j), 0.0)
+            value = t_ref[c * FULL + INNER + j] + jnp.where(lane < EY, roll(before, -EY * j), 0.0)
             moved = roll(face, lanes - EY - EY * j)
             beyond = jnp.where(lane >= lanes - EY, moved, roll(value, -EY))
             put(j, value)
@@ -456,16 +531,15 @@
     depth = velocity.shape[1]
     parts = lax.axis_size("modes")
     layout = Layout(parts)
-    rows = -(-3 * (INNER + EXTRA) // parts) * parts
     args = (velocity.transpose(0, 2, 1, 3), slot_of_cell, elem_mats.transpose(1, 0, 2), geometry)
     table = jnp.asarray(operator(layout, depth))
     table = lax.dynamic_index_in_dim(
         table, lax.rem(lax.axis_index("modes"), layout.inner), keepdims=False
     )
-    z = elements("mass", (3,), layout, rows, args)
+    z = elements("mass", (3,), layout, args)
     pencil = layout.swap(*layout.divide(z))
-    (u,) = elements("stiff", (0, 1, 2), None, rows, args)
-    y = layout.swap(*layout.divide(spanwise(layout, pencil, table)))
+    (u,) = elements("stiff", (0, 1, 2), None, args)
+    y = layout.swap(*layout.divide(spanwise(layout, depth, pencil, table)))
     total, faces = totals(layout, u, y)
     count = lax.axis_size("dom")
     onward = [(k, (k + 1) % count) for k in range(count)]

time: 98.9 us -> 95.8 us (0.969)
  waiting for transfers between devices: 65 us -> 63.4 us
  Pallas kernels: 17 us -> 15.6 us
    pallas_call x2, Pallas kernels: 13.1 us -> 11.4 us  [elements(): pl.pallas_call(functools.partial(element_kernel, terms, layout, len(shape...]
    ppermute x6, waiting for transfers between devices: 39.8 us -> 38.1 us  [onward(): return lax.ppermute(value, 'modes', steps)]
  transfers between devices with their start and end apart: 19 -> 19, of which waited for: 11 -> 12; matrix products, arithmetic and copies ran while one was open for 2% -> 2% of each run, Pallas kernels for 8% -> 7%
where the time goes in v3:
time: 95.8 us; the launch traced here: 95.6 us
  waiting for transfers between devices  63.4 us (66%)
  Pallas kernels  15.6 us (16%)
  starting transfers between devices  13.9 us (15%)
  local copies, waits for them, and re-layouts  2.07 us (2%)
    ppermute x6, waiting for transfers between devices, onward(): return lax.ppermute(value, 'modes', steps)  38.1 us
    ppermute x12, waiting for transfers between devices, across(): lax.ppermute(value, 'modes', pairs(s))  24.2 us
    pallas_call x2, Pallas kernels, elements(): pl.pallas_call(functools.partial(element_kernel, terms, layout, len(shape...  11.4 us
    ppermute x12, starting transfers between devices, across(): lax.ppermute(value, 'modes', pairs(s))  7.87 us
    ppermute x6, starting transfers between devices, onward(): return lax.ppermute(value, 'modes', steps)  4.45 us
    pallas_call x2, Pallas kernels, expand(): pl.pallas_call(kernel, in_specs=in_specs, out_specs=pl.BlockSpec(memory_s...  2.78 us
  transfers between devices with their start and end apart: 19, of which 12 were waited for; matrix products, arithmetic and copies ran while one was open for 2% of the time, Pallas kernels for 7%

profile of v3, /device:TPU:16, one launch (start us, length us, event | category | flops | bytes accessed | tf_op | source)
XLA Modules:
  0.0 95.6 jit_solution(2870738233349314191)
XLA Ops:
  0.0 6.3 %mass.1 = (f32[4,200,128]{2,1,0:T(8,128)}, f32[4,200,128]{2,1,0:T(8,128)}, f32[2,200,128]{2,1,0:T(8,128)}, f32[2,200,128]{2,1,0:T(8,128)}, f32[2,200,128]{2,1,0:T(8,128)}, /*index=5*/f32[2,200,128]{2,1,0:T(8,128)}) custom-call(f32[3,81,16,128]{3,2,1,0:T(8,128)} %bitcast.9, s32[1,128]{1,0:T(1,128)} %slots_ref.3, f32[81,4,81]{2,1,0:T(4,128)} %bitcast.11, ...), custom_call_target="tpu_custom_call" | custom-call | flops 339738624 | bytes 3686400 | tf_op jit(solution)/shard_map/mass/pallas_call | solution.py:311
  6.3 1.7 %collective-permute-start.4 = (f32[4,200,128]{2,1,0:T(8,128)}, f32[4,200,128]{2,1,0:T(8,128)S(1)}, u32[]{:S(2)}, u32[]{:S(2)}) collective-permute-start(f32[4,200,128]{2,1,0:T(8,128)} %get-tuple-element.23), channel_id=1, source_target_pairs={{0,8},{2,10},{4,12},{6,14},{8,16},{10,18},{12,20},{14,22},{16,24},... | collective-permute-start | bytes 1228808 | tf_op jit(solution)/shard_map/ppermute | solution.py:78
  8.0 0.0 collective-permute-start
  8.0 1.5 %collective-permute-start.1 = (f32[2,200,128]{2,1,0:T(8,128)}, f32[2,200,128]{2,1,0:T(8,128)S(1)}, u32[]{:S(2)}, u32[]{:S(2)}) collective-permute-start(f32[2,200,128]{2,1,0:T(8,128)} %get-tuple-element.21), channel_id=1, source_target_pairs={{0,4},{2,6},{4,0},{6,2},{8,12},{10,14},{12,8},{14,10},{16,20},{18,... | collective-permute-start | bytes 614408 | tf_op jit(solution)/shard_map/ppermute | solution.py:83
  9.5 0.3 collective-permute-start.2
  9.9 0.4 collective-permute-start.5
  10.2 0.9 slice.72
  11.1 0.0 collective-permute-done.refs_1_
  11.1 4.9 %collective-permute-done.1.refs_2_ = f32[2,200,128]{2,1,0:T(8,128)S(1)} collective-permute-done((f32[2,200,128]{2,1,0:T(8,128)}, f32[2,200,128]{2,1,0:T(8,128)S(1)}, u32[]{:S(2)}, u32[]{:S(2)}) %collective-permute-start.1) | collective-permute-done | bytes 204832 | tf_op jit(solution)/shard_map/ppermute | solution.py:83
  16.1 3.6 %collective-permute-done.2.refs_3_ = f32[2,200,128]{2,1,0:T(8,128)S(1)} collective-permute-done((f32[2,200,128]{2,1,0:T(8,128)}, f32[2,200,128]{2,1,0:T(8,128)S(1)}, u32[]{:S(2)}, u32[]{:S(2)}) %collective-permute-start.2) | collective-permute-done | bytes 204832 | tf_op jit(solution)/shard_map/ppermute | solution.py:83
  19.8 0.3 collective-permute-start.3
  20.1 15.2 %collective-permute-done.4 = f32[4,200,128]{2,1,0:T(8,128)S(1)} collective-permute-done((f32[4,200,128]{2,1,0:T(8,128)}, f32[4,200,128]{2,1,0:T(8,128)S(1)}, u32[]{:S(2)}, u32[]{:S(2)}) %collective-permute-start.4) | collective-permute-done | bytes 409632 | tf_op jit(solution)/shard_map/ppermute | solution.py:78
  35.4 0.1 collective-permute-start.6
  35.5 1.6 %collective-permute-start.7 = (f32[2,200,128]{2,1,0:T(8,128)S(1)}, f32[2,200,128]{2,1,0:T(8,128)S(1)}, u32[]{:S(2)}, u32[]{:S(2)}) collective-permute-start(f32[2,200,128]{2,1,0:T(8,128)S(1)} %pad_maximum_fusion.4), channel_id=1, source_target_pairs={{0,4},{2,6},{4,0},{6,2},{8,12},{10,14},{12,8},{14,10},{16,20},{18,... | collective-permute-start | bytes 614408 | tf_op jit(solution)/shard_map/ppermute | solution.py:83
  37.1 0.4 collective-permute-start.8
  37.5 1.0 %dynamic-slice_bitcast_fusion.refs_9_ = bf16[512,256]{1,0:T(8,128)(2,1)S(1)} fusion(bf16[4,512,256]{2,1,0:T(8,128)(2,1)} %constant.18.clone, s32[]{:T(128)S(6)} %select_n.4), kind=kLoop, calls=%fused_computation.2 | loop fusion | bytes 524292 | tf_op jit(solution)/shard_map/jit(dynamic_index_in_dim)/squeeze | solution.py:536
  38.5 4.5 %collective-permute-done.3.refs_4_ = f32[4,200,128]{2,1,0:T(8,128)S(1)} collective-permute-done((f32[4,200,128]{2,1,0:T(8,128)S(1)}, f32[4,200,128]{2,1,0:T(8,128)S(1)}, u32[]{:S(2)}, u32[]{:S(2)}) %collective-permute-start.3) | collective-permute-done | bytes 409632 | tf_op jit(solution)/shard_map/ppermute | solution.py:78
  43.0 0.0 collective-permute-done.6.refs_6_
  43.0 0.4 collective-permute-done.7.refs_7_
  43.4 3.6 %collective-permute-done.8.refs_8_ = f32[2,200,128]{2,1,0:T(8,128)S(1)} collective-permute-done((f32[2,200,128]{2,1,0:T(8,128)S(1)}, f32[2,200,128]{2,1,0:T(8,128)S(1)}, u32[]{:S(2)}, u32[]{:S(2)}) %collective-permute-start.8) | collective-permute-done | bytes 204832 | tf_op jit(solution)/shard_map/ppermute | solution.py:83
  47.0 1.0 %spanwise.1 = (f32[4,200,128]{2,1,0:T(8,128)S(1)}, f32[4,200,128]{2,1,0:T(8,128)S(1)}, f32[2,200,128]{2,1,0:T(8,128)S(1)}, f32[2,200,128]{2,1,0:T(8,128)S(1)}, f...) custom-call(f32[2,200,128]{2,1,0:T(8,128)S(1)} %copy-done.2, f32[2,200,128]{2,1,0:T(8,128)S(1)} %collective-permute-done.refs_1_, ...), custom_call_target="tpu_custom_call" | custom-call | flops 629145600 | bytes 3276800 | tf_op jit(solution)/shard_map/spanwise/pallas_call | solution.py:357
  48.0 0.1 collective-permute-start.13
  48.1 0.3 collective-permute-start.9
  48.3 1.5 %collective-permute-start.10 = (f32[2,200,128]{2,1,0:T(8,128)S(1)}, f32[2,200,128]{2,1,0:T(8,128)S(1)}, u32[]{:S(2)}, u32[]{:S(2)}) collective-permute-start(f32[2,200,128]{2,1,0:T(8,128)S(1)} %get-tuple-element.27), channel_id=1, source_target_pairs={{0,4},{2,6},{4,0},{6,2},{8,12},{10,14},{12,8},{14,10},{16,20},{18,... | collective-permute-start | bytes 614408 | tf_op jit(solution)/shard_map/ppermute | solution.py:83
  49.9 0.1 collective-permute-start.11
  50.0 1.9 %collective-permute-start.14 = (f32[4,200,128]{2,1,0:T(8,128)S(1)}, f32[4,200,128]{2,1,0:T(8,128)S(1)}, u32[]{:S(2)}, u32[]{:S(2)}) collective-permute-start(f32[4,200,128]{2,1,0:T(8,128)S(1)} %get-tuple-element.30), channel_id=1, source_target_pairs={{0,24},{2,26},{4,28},{6,30},{8,0},{10,2},{12,4},{14,6},{16,8},{18,... | collective-permute-start | bytes 1228808 | tf_op jit(solution)/shard_map/ppermute | solution.py:78
  51.9 0.0 collective-permute-done.9.refs_1_
  52.0 4.3 %collective-permute-done.10.refs_2_ = f32[2,200,128]{2,1,0:T(8,128)S(1)} collective-permute-done((f32[2,200,128]{2,1,0:T(8,128)S(1)}, f32[2,200,128]{2,1,0:T(8,128)S(1)}, u32[]{:S(2)}, u32[]{:S(2)}) %collective-permute-start.10) | collective-permute-done | bytes 204832 | tf_op jit(solution)/shard_map/ppermute | solution.py:83
  56.3 0.0 copy-start
  56.3 0.0 copy-start.1
  56.3 0.0 copy-start.3
  56.3 0.0 copy-start.4
  56.3 3.0 %collective-permute-done.11.refs_3_ = f32[2,200,128]{2,1,0:T(8,128)S(1)} collective-permute-done((f32[2,200,128]{2,1,0:T(8,128)S(1)}, f32[2,200,128]{2,1,0:T(8,128)S(1)}, u32[]{:S(2)}, u32[]{:S(2)}) %collective-permute-start.11) | collective-permute-done | bytes 204832 | tf_op jit(solution)/shard_map/ppermute | solution.py:83
  59.4 0.1 collective-permute-start.12
  59.5 18.4 %collective-permute-done.13 = f32[4,200,128]{2,1,0:T(8,128)S(1)} collective-permute-done((f32[4,200,128]{2,1,0:T(8,128)S(1)}, f32[4,200,128]{2,1,0:T(8,128)S(1)}, u32[]{:S(2)}, u32[]{:S(2)}) %collective-permute-start.13) | collective-permute-done | bytes 409632 | tf_op jit(solution)/shard_map/ppermute | solution.py:78
  77.9 0.0 collective-permute-done.14
  78.0 0.1 collective-permute-start.15
  78.1 1.6 %collective-permute-start.16 = (f32[2,200,128]{2,1,0:T(8,128)S(1)}, f32[2,200,128]{2,1,0:T(8,128)S(1)}, u32[]{:S(2)}, u32[]{:S(2)}) collective-permute-start(f32[2,200,128]{2,1,0:T(8,128)S(1)} %pad_maximum_fusion.8), channel_id=1, source_target_pairs={{0,4},{2,6},{4,0},{6,2},{8,12},{10,14},{12,8},{14,10},{16,20},{18,... | collective-permute-start | bytes 614408 | tf_op jit(solution)/shard_map/ppermute | solution.py:83
  79.7 0.4 collective-permute-start.17
  80.1 5.1 %stiff.1.u_ref = f32[198,16,128]{2,1,0:T(8,128)S(1)} custom-call(f32[3,81,16,128]{3,2,1,0:T(8,128)S(1)} %bitcast.10, s32[1,128]{1,0:T(1,128)S(1)} %copy-done.4, f32[81,4,81]{2,1,0:T(4,128)S(1)} %bitcast.12, f32[4,128]{1,0:T(4,128)S(1)} %copy-done.3), custom_call_target="tpu_custom_call" | custom-call | flops 1019215872 | bytes 3686400 | tf_op jit(solution)/shard_map/stiff/pallas_call | solution.py:311
  85.3 0.0 collective-permute-done.12.refs_4_
  85.3 0.7 collective-permute-done.16.refs_7_
  86.0 3.6 %collective-permute-done.17.refs_8_ = f32[2,200,128]{2,1,0:T(8,128)S(1)} collective-permute-done((f32[2,200,128]{2,1,0:T(8,128)S(1)}, f32[2,200,128]{2,1,0:T(8,128)S(1)}, u32[]{:S(2)}, u32[]{:S(2)}) %collective-permute-start.17) | collective-permute-done | bytes 204832 | tf_op jit(solution)/shard_map/ppermute | solution.py:83
  89.6 0.5 totals.1
  90.1 1.6 %collective-permute-start.18 = (f32[2,3,16,128]{3,2,1,0:T(8,128)S(1)}, f32[2,3,16,128]{3,2,1,0:T(8,128)S(1)}, u32[]{:S(2)}, u32[]{:S(2)}) collective-permute-start(f32[2,3,16,128]{3,2,1,0:T(8,128)S(1)} %get-tuple-element.32), channel_id=1, source_target_pairs={{0,1},{1,0},{2,3},{3,2},{4,5},{5,4},{6,7},{7,6},{8,9},{9,8},{10,11... | collective-permute-start | bytes 147464 | tf_op jit(solution)/shard_map/ppermute | solution.py:548
  91.7 1.6 %middle.1._ = f32[3,81,16,128]{3,2,1,0:T(8,128)} custom-call(f32[198,16,128]{2,1,0:T(8,128)S(1)} %get-tuple-element.31.t_ref, s32[1,128]{1,0:T(1,128)S(1)} %copy-done.4), custom_call_target="tpu_custom_call" | custom-call | flops 198180864 | bytes 6193152 | tf_op jit(solution)/shard_map/middle/pallas_call | solution.py:509
  93.3 1.0 %collective-permute-done.18 = f32[2,3,16,128]{3,2,1,0:T(8,128)S(1)} collective-permute-done((f32[2,3,16,128]{3,2,1,0:T(8,128)S(1)}, f32[2,3,16,128]{3,2,1,0:T(8,128)S(1)}, u32[]{:S(2)}, u32[]{:S(2)}) %collective-permute-start.18) | collective-permute-done | bytes 49184 | tf_op jit(solution)/shard_map/ppermute | solution.py:548
  94.3 1.2 %faces.1 = f32[3,81,16,128]{3,2,1,0:T(8,128)} custom-call(f32[198,16,128]{2,1,0:T(8,128)S(1)} %get-tuple-element.31.t_ref, f32[3,16,128]{2,1,0:T(8,128)S(1)} %get-tuple-element.50.before_ref, f32[3,16,128]{2,1,0:T(8,128)S(1)} %get-tuple-element.49.after_ref, s32[1,128]{1,0:T(1,128)S(1)} %copy-done.4, ...), custom_call_target="tpu_custom_call", output_to_operand_aliasing={{}: (4, {})} | custom-call | flops 56623104 | bytes 1769472 | tf_op jit(solution)/shard_map/faces/pallas_call | solution.py:509
  (30 shorter events, 0.4 us)
Async XLA Ops:
  6.3 29.0 %collective-permute-start.4 = (f32[4,200,128]{2,1,0:T(8,128)}, f32[4,200,128]{2,1,0:T(8,128)S(1)}, u32[]{:S(2)}, u32[]{:S(2)}) collective-permute-start(f32[4,200,128]{2,1,0:T(8,128)} %get-tuple-element.23), channel_id=1, source_target_pairs={{0,8},{2,10},{4,12},{6,14},{8,16},{10,18},{12,20},{14,22},{16,24},... | collective-permute-start | bytes 1228808 | tf_op jit(solution)/shard_map/ppermute | solution.py:78
  8.0 3.1 %collective-permute-start = (f32[2,200,128]{2,1,0:T(8,128)}, f32[2,200,128]{2,1,0:T(8,128)S(1)}, u32[]{:S(2)}, u32[]{:S(2)}) collective-permute-start(f32[2,200,128]{2,1,0:T(8,128)} %get-tuple-element.20), channel_id=1, source_target_pairs={{0,2},{2,0},{4,6},{6,4},{8,10},{10,8},{12,14},{14,12},{16,18},{18,... | collective-permute-start | bytes 614408 | tf_op jit(solution)/shard_map/ppermute | solution.py:83
  8.0 8.1 %collective-permute-start.1 = (f32[2,200,128]{2,1,0:T(8,128)}, f32[2,200,128]{2,1,0:T(8,128)S(1)}, u32[]{:S(2)}, u32[]{:S(2)}) collective-permute-start(f32[2,200,128]{2,1,0:T(8,128)} %get-tuple-element.21), channel_id=1, source_target_pairs={{0,4},{2,6},{4,0},{6,2},{8,12},{10,14},{12,8},{14,10},{16,20},{18,... | collective-permute-start | bytes 614408 | tf_op jit(solution)/shard_map/ppermute | solution.py:83
  9.5 10.2 %collective-permute-start.2 = (f32[2,200,128]{2,1,0:T(8,128)}, f32[2,200,128]{2,1,0:T(8,128)S(1)}, u32[]{:S(2)}, u32[]{:S(2)}) collective-permute-start(f32[2,200,128]{2,1,0:T(8,128)} %get-tuple-element.22), channel_id=1, source_target_pairs={{0,6},{2,4},{4,2},{6,0},{8,14},{10,12},{12,10},{14,8},{16,22},{18,... | collective-permute-start | bytes 614408 | tf_op jit(solution)/shard_map/ppermute | solution.py:83
  9.9 25.5 %collective-permute-start.5 = (f32[4,200,128]{2,1,0:T(8,128)}, f32[4,200,128]{2,1,0:T(8,128)S(1)}, u32[]{:S(2)}, u32[]{:S(2)}) collective-permute-start(f32[4,200,128]{2,1,0:T(8,128)} %get-tuple-element.24), channel_id=1, source_target_pairs={{0,24},{2,26},{4,28},{6,30},{8,0},{10,2},{12,4},{14,6},{16,8},{18,... | collective-permute-start | bytes 1228808 | tf_op jit(solution)/shard_map/ppermute | solution.py:78
  19.8 27.3 %copy-start.2 = (f32[2,200,128]{2,1,0:T(8,128)S(1)}, f32[2,200,128]{2,1,0:T(8,128)}, u32[]{:S(2)}) copy-start(f32[2,200,128]{2,1,0:T(8,128)} %get-tuple-element.19.refs_0_) | copy-start | bytes 614404
  19.8 23.2 %collective-permute-start.3 = (f32[4,200,128]{2,1,0:T(8,128)S(1)}, f32[4,200,128]{2,1,0:T(8,128)S(1)}, u32[]{:S(2)}, u32[]{:S(2)}) collective-permute-start(f32[4,200,128]{2,1,0:T(8,128)S(1)} %pad_maximum_fusion), channel_id=1, source_target_pairs={{0,16},{2,18},{4,20},{6,22},{8,24},{10,26},{12,28},{14,30},{16,0},... | collective-permute-start | bytes 1228808 | tf_op jit(solution)/shard_map/ppermute | solution.py:78
  35.4 7.6 %collective-permute-start.6 = (f32[2,200,128]{2,1,0:T(8,128)S(1)}, f32[2,200,128]{2,1,0:T(8,128)S(1)}, u32[]{:S(2)}, u32[]{:S(2)}) collective-permute-start(f32[2,200,128]{2,1,0:T(8,128)S(1)} %pad_maximum_fusion.3), channel_id=1, source_target_pairs={{0,2},{2,0},{4,6},{6,4},{8,10},{10,8},{12,14},{14,12},{16,18},{18,... | collective-permute-start | bytes 614408 | tf_op jit(solution)/shard_map/ppermute | solution.py:83
  35.5 7.9 %collective-permute-start.7 = (f32[2,200,128]{2,1,0:T(8,128)S(1)}, f32[2,200,128]{2,1,0:T(8,128)S(1)}, u32[]{:S(2)}, u32[]{:S(2)}) collective-permute-start(f32[2,200,128]{2,1,0:T(8,128)S(1)} %pad_maximum_fusion.4), channel_id=1, source_target_pairs={{0,4},{2,6},{4,0},{6,2},{8,12},{10,14},{12,8},{14,10},{16,20},{18,... | collective-permute-start | bytes 614408 | tf_op jit(solution)/shard_map/ppermute | solution.py:83
  37.1 9.9 %collective-permute-start.8 = (f32[2,200,128]{2,1,0:T(8,128)S(1)}, f32[2,200,128]{2,1,0:T(8,128)S(1)}, u32[]{:S(2)}, u32[]{:S(2)}) collective-permute-start(f32[2,200,128]{2,1,0:T(8,128)S(1)} %pad_maximum_fusion.5), channel_id=1, source_target_pairs={{0,6},{2,4},{4,2},{6,0},{8,14},{10,12},{12,10},{14,8},{16,22},{18,... | collective-permute-start | bytes 614408 | tf_op jit(solution)/shard_map/ppermute | solution.py:83
  48.0 29.9 %collective-permute-start.13 = (f32[4,200,128]{2,1,0:T(8,128)S(1)}, f32[4,200,128]{2,1,0:T(8,128)S(1)}, u32[]{:S(2)}, u32[]{:S(2)}) collective-permute-start(f32[4,200,128]{2,1,0:T(8,128)S(1)} %get-tuple-element.29), channel_id=1, source_target_pairs={{0,8},{2,10},{4,12},{6,14},{8,16},{10,18},{12,20},{14,22},{16,24},... | collective-permute-start | bytes 1228808 | tf_op jit(solution)/shard_map/ppermute | solution.py:78
  48.1 3.9 %collective-permute-start.9 = (f32[2,200,128]{2,1,0:T(8,128)S(1)}, f32[2,200,128]{2,1,0:T(8,128)S(1)}, u32[]{:S(2)}, u32[]{:S(2)}) collective-permute-start(f32[2,200,128]{2,1,0:T(8,128)S(1)} %get-tuple-element.26), channel_id=1, source_target_pairs={{0,2},{2,0},{4,6},{6,4},{8,10},{10,8},{12,14},{14,12},{16,18},{18,... | collective-permute-start | bytes 614408 | tf_op jit(solution)/shard_map/ppermute | solution.py:83
  48.3 7.9 %collective-permute-start.10 = (f32[2,200,128]{2,1,0:T(8,128)S(1)}, f32[2,200,128]{2,1,0:T(8,128)S(1)}, u32[]{:S(2)}, u32[]{:S(2)}) collective-permute-start(f32[2,200,128]{2,1,0:T(8,128)S(1)} %get-tuple-element.27), channel_id=1, source_target_pairs={{0,4},{2,6},{4,0},{6,2},{8,12},{10,14},{12,8},{14,10},{16,20},{18,... | collective-permute-start | bytes 614408 | tf_op jit(solution)/shard_map/ppermute | solution.py:83
  49.9 9.5 %collective-permute-start.11 = (f32[2,200,128]{2,1,0:T(8,128)S(1)}, f32[2,200,128]{2,1,0:T(8,128)S(1)}, u32[]{:S(2)}, u32[]{:S(2)}) collective-permute-start(f32[2,200,128]{2,1,0:T(8,128)S(1)} %get-tuple-element.28), channel_id=1, source_target_pairs={{0,6},{2,4},{4,2},{6,0},{8,14},{10,12},{12,10},{14,8},{16,22},{18,... | collective-permute-start | bytes 614408 | tf_op jit(solution)/shard_map/ppermute | solution.py:83
  50.0 27.9 %collective-permute-start.14 = (f32[4,200,128]{2,1,0:T(8,128)S(1)}, f32[4,200,128]{2,1,0:T(8,128)S(1)}, u32[]{:S(2)}, u32[]{:S(2)}) collective-permute-start(f32[4,200,128]{2,1,0:T(8,128)S(1)} %get-tuple-element.30), channel_id=1, source_target_pairs={{0,24},{2,26},{4,28},{6,30},{8,0},{10,2},{12,4},{14,6},{16,8},{18,... | collective-permute-start | bytes 1228808 | tf_op jit(solution)/shard_map/ppermute | solution.py:78
  56.3 23.8 %copy-start = (f32[3,16,81,128]{3,1,2,0:T(8,128)S(1)}, f32[3,16,81,128]{3,1,2,0:T(8,128)}, u32[]{:S(2)}) copy-start(f32[3,16,81,128]{3,1,2,0:T(8,128)} %param.5) | copy-start | bytes 5971972
  56.3 23.8 %copy-start.1 = (f32[4,81,81]{2,0,1:T(4,128)S(1)}, f32[4,81,81]{2,0,1:T(4,128)}, u32[]{:S(2)}) copy-start(f32[4,81,81]{2,0,1:T(4,128)} %param.7) | copy-start | bytes 314932
  56.3 23.8 %copy-start.3 = (f32[4,128]{1,0:T(4,128)S(1)}, f32[4,128]{1,0:T(4,128)}, u32[]{:S(2)}) copy-start(f32[4,128]{1,0:T(4,128)} %refs_3_.3) | copy-start | bytes 6148
  56.3 23.8 %copy-start.4 = (s32[1,128]{1,0:T(1,128)S(1)}, s32[1,128]{1,0:T(1,128)}, u32[]{:S(2)}) copy-start(s32[1,128]{1,0:T(1,128)} %slots_ref.3) | copy-start | bytes 1540
  59.4 25.9 %collective-permute-start.12 = (f32[4,200,128]{2,1,0:T(8,128)S(1)}, f32[4,200,128]{2,1,0:T(8,128)S(1)}, u32[]{:S(2)}, u32[]{:S(2)}) collective-permute-start(f32[4,200,128]{2,1,0:T(8,128)S(1)} %pad_maximum_fusion.1), channel_id=1, source_target_pairs={{0,16},{2,18},{4,20},{6,22},{8,24},{10,26},{12,28},{14,30},{16,0},... | collective-permute-start | bytes 1228808 | tf_op jit(solution)/shard_map/ppermute | solution.py:78
  78.0 7.3 %collective-permute-start.15 = (f32[2,200,128]{2,1,0:T(8,128)S(1)}, f32[2,200,128]{2,1,0:T(8,128)S(1)}, u32[]{:S(2)}, u32[]{:S(2)}) collective-permute-start(f32[2,200,128]{2,1,0:T(8,128)S(1)} %pad_maximum_fusion.7), channel_id=1, source_target_pairs={{0,2},{2,0},{4,6},{6,4},{8,10},{10,8},{12,14},{14,12},{16,18},{18,... | collective-permute-start | bytes 614408 | tf_op jit(solution)/shard_map/ppermute | solution.py:83
  78.1 7.9 %collective-permute-start.16 = (f32[2,200,128]{2,1,0:T(8,128)S(1)}, f32[2,200,128]{2,1,0:T(8,128)S(1)}, u32[]{:S(2)}, u32[]{:S(2)}) collective-permute-start(f32[2,200,128]{2,1,0:T(8,128)S(1)} %pad_maximum_fusion.8), channel_id=1, source_target_pairs={{0,4},{2,6},{4,0},{6,2},{8,12},{10,14},{12,8},{14,10},{16,20},{18,... | collective-permute-start | bytes 614408 | tf_op jit(solution)/shard_map/ppermute | solution.py:83
  79.7 9.9 %collective-permute-start.17 = (f32[2,200,128]{2,1,0:T(8,128)S(1)}, f32[2,200,128]{2,1,0:T(8,128)S(1)}, u32[]{:S(2)}, u32[]{:S(2)}) collective-permute-start(f32[2,200,128]{2,1,0:T(8,128)S(1)} %pad_maximum_fusion.9), channel_id=1, source_target_pairs={{0,6},{2,4},{4,2},{6,0},{8,14},{10,12},{12,10},{14,8},{16,22},{18,... | collective-permute-start | bytes 614408 | tf_op jit(solution)/shard_map/ppermute | solution.py:83
  90.1 4.2 %collective-permute-start.18 = (f32[2,3,16,128]{3,2,1,0:T(8,128)S(1)}, f32[2,3,16,128]{3,2,1,0:T(8,128)S(1)}, u32[]{:S(2)}, u32[]{:S(2)}) collective-permute-start(f32[2,3,16,128]{3,2,1,0:T(8,128)S(1)} %get-tuple-element.32), channel_id=1, source_target_pairs={{0,1},{1,0},{2,3},{3,2},{4,5},{5,4},{6,7},{7,6},{8,9},{9,8},{10,11... | collective-permute-start | bytes 147464 | tf_op jit(solution)/shard_map/ppermute | solution.py:548

commit v4 on v3

v4 whole, which is shorter than its diff:
```python
import functools
import math

import jax
import jax.numpy as jnp
import numpy as np
from jax import lax
from jax.experimental import pallas as pl
from jax.experimental.pallas import tpu as pltpu
from jax.sharding import PartitionSpec as P

EX = 16
EY = 8
LANES = EX * EY
NODES = 81
SIDE = 8
INNER = SIDE * (SIDE - 1)
FACE = SIDE * EY
HALF = LANES // 2
ENDS = 3 * SIDE
FACES = ENDS + 3
EXTRAS = FACES + 3
CORNERS = 2 * FACES + 3
HALVES = CORNERS + 1
DEEP = 96
PITCH = 104
TALL = 88
VMEM = 48 * 1024 * 1024
WIDE = 60 * 1024 * 1024

f32 = jnp.float32
bf16 = jnp.bfloat16


def split(values):
    high = values.astype(bf16)
    return high, (values - high.astype(f32)).astype(bf16)


class Layout:

    def __init__(self, parts):
        self.outer = max(d for d in range(1, math.isqrt(parts) + 1) if parts % d == 0)
        self.inner = parts // self.outer
        assert self.inner & (self.inner - 1) == 0
        self.late = [0, self.outer // 2]
        self.early = [k for k in range(1, self.outer) if k not in self.late]
        self.blocks = [(k, s) for k in range(self.outer) for s in range(self.inner)]

    def place(self, k, s):
        me = lax.axis_index("modes")
        out = lax.rem(me // self.inner + (k + self.outer), self.outer)
        return out * self.inner + jnp.bitwise_xor(lax.rem(me, self.inner), s)

    def sent(self, k, s, early, late):
        if k in self.late:
            return late[s].at[self.late.index(k)]
        return early[self.early.index(k)].at[s]

    def share(self, depth):
        count = len(self.blocks)
        full = 3 * INNER // count
        rest = -(-2 * (3 * INNER - full * count) // count)
        if rest == 2:
            full, rest = full + 1, 0
        lower = full // 2
        extra = -(-HALVES // count)
        return lower * depth, extra * depth // 2, (full - lower) * depth, rest * depth // 2

    def base(self, depth):
        return self.share(depth)[0] // depth * len(self.blocks)

    def shapes(self, share):
        early = [(self.inner,) + share] * len(self.early)
        return early + [(len(self.late),) + share] * self.inner

    def divide(self, arrays):
        return arrays[: len(self.early)], arrays[len(self.early) :]

    def got(self, refs):
        inner = self.inner
        late, middle, early = refs[:inner], refs[inner:], refs[inner + len(self.late) - 1 :]
        found = {(0, s): late[s].at[0] for s in range(inner)}
        for at, k in enumerate(self.late[1:]):
            found.update({(k, s): middle[at].at[s] for s in range(inner)})
        for at, k in enumerate(self.early):
            found.update({(k, s): early[s].at[at] for s in range(inner)})
        return found

    def onward(self, value, k):
        parts = self.outer * self.inner
        steps = [(d, (d + k * self.inner) % parts) for d in range(parts)]
        return lax.ppermute(value, "modes", steps)

    def across(self, values):
        pairs = lambda s: [(d, d ^ s) for d in range(self.outer * self.inner)]
        return values[:1] + [
            lax.ppermute(value, "modes", pairs(s)) for s, value in enumerate(values) if s
        ]

    def start(self, early, late):
        early = [self.onward(value, k) for k, value in zip(self.early, early)]
        return early, self.across(list(late))

    def middle(self, late, part=slice(None)):
        return [
            self.onward(jnp.stack([value[at, part] for value in late]), k)
            for at, k in enumerate(self.late)
            if k
        ]

    def end(self, early):
        return self.across([jnp.stack([value[s] for value in early]) for s in range(self.inner)])


def following(values, *earlier):
    return [lax.optimization_barrier((value, *earlier))[0] for value in values]


def operator(layout, depth):
    outer, inner = layout.outer, layout.inner
    length = outer * inner * depth
    half = length // 2
    waves = np.arange(half + 1)
    weights = np.where((waves == 0) | (waves == half), 1.0, 2.0) / length
    sigma = 1.0 + (8.0 * waves / length) ** 2
    phases = (np.arange(length)[:, None] * waves[None, :]) % length
    row = (np.cos(phases * (2.0 * np.pi / length)) * (weights * sigma)).sum(1)
    step, slot, plane = np.meshgrid(np.arange(outer), np.arange(inner), np.arange(depth), indexing="ij")
    step, slot, plane = step.ravel(), slot.ravel(), plane.ravel()
    place = np.arange(inner)[:, None]
    sent = (step * inner + (place ^ slot)) * depth + plane
    got = (-step * inner + (place ^ slot)) * depth + plane
    full = row[(sent[:, :, None] - got[:, None, :]) % length].astype(np.float32)
    high = full.astype(jnp.bfloat16)
    low = (full - high.astype(np.float32)).astype(jnp.bfloat16)
    return np.concatenate([high, low], axis=1)


def selector(slots):
    slot = lax.broadcasted_iota(jnp.int32, (LANES, LANES), 0)
    return jnp.where(slot == slots, 1.0, 0.0).astype(f32)


def lane_index(depth):
    return lax.broadcasted_iota(jnp.int32, (depth, LANES), 1)


def roll(value, shift):
    shift = shift % LANES
    return value if shift == 0 else pltpu.roll(value, shift, 1)


def gather_face(column, origin):
    lane = lane_index(column[0].shape[0])
    face = jnp.where(lane == FACE, roll(column[SIDE], FACE - origin - EY + 1), 0.0)
    for j in range(SIDE):
        face = jnp.where(lane // EY == j, roll(column[j], EY * j - origin), face)
    return face


def prepare(terms, slots_ref, mats_ref, left_ref):
    select = selector(slots_ref[...]).astype(bf16)
    left_ref[...] = jnp.zeros_like(left_ref)
    for place, term in enumerate(terms):
        high, low = split(mats_ref[:, term, :])
        left_ref[place, :NODES, 0:NODES] = high
        left_ref[place, :NODES, NODES : NODES + 1] = low[:, NODES - 1 :]
        left_ref[place, :NODES, TALL : TALL + NODES] = high
        left_ref[place, :NODES, 2 * TALL :] = low[:, : NODES - 1]
    return jnp.concatenate([select, select], axis=0)


def component(terms, first, second, select, geo, left, scratch, row, ends, face):
    values_ref, images_ref, cells_ref = scratch
    depth = first.shape[1]
    values_ref[:NODES, :depth] = first[...] * second[...]
    values_ref[NODES, :depth] = values_ref[NODES - 1, :depth]
    flat = values_ref.reshape(TALL * (depth + 8), LANES)
    for pair in range(0, depth, 2):
        right = []
        for p in (pair, pair + 1):
            value = flat[pl.ds(p, TALL, stride=depth + 8), :]
            high = value.astype(bf16).astype(f32)
            parts = jnp.concatenate([high, value - high, high[: NODES - 1]], axis=0)
            right.append(parts.astype(bf16))
        images = jnp.dot(left, jnp.concatenate(right, axis=1), preferred_element_type=f32)
        for p in (0, 1):
            total = 0.0
            for t, term in enumerate(terms):
                total = total + (
                    images[DEEP * t : DEEP * t + DEEP, LANES * p : LANES * p + LANES]
                    * geo[term : term + 1]
                )
            high, low = split(total)
            images_ref[(pair + p) * DEEP : (pair + p + 1) * DEEP, :LANES] = high
            images_ref[(pair + p) * DEEP : (pair + p + 1) * DEEP, LANES:] = low
    cells = jnp.dot(images_ref[...], select, preferred_element_type=f32)
    for p in range(depth):
        cells_ref[p * PITCH : p * PITCH + DEEP] = cells[p * DEEP : (p + 1) * DEEP]
    lane = lane_index(depth)
    across = lane % EY

    def node(i, j):
        value = cells_ref[pl.ds((SIDE + 1) * i + j, depth, stride=PITCH), :]
        if i > 0:
            return value
        return value + jnp.where(lane >= EY, roll(node(8, j), EY), 0.0)

    def join(low, high):
        return low + jnp.where(across > 0, roll(high, 1), 0.0)

    end = jnp.zeros((depth, LANES), f32)
    for i in range(SIDE + 1):
        column = [node(i, j) for j in range(SIDE + 1)]
        column[0] = join(column[0], column[SIDE])
        if i < SIDE:
            for j in range(SIDE):
                row(SIDE * (i - 1) + j if i else INNER + j, column[j])
            end = jnp.where(across == i, roll(column[SIDE], i + 1 - EY), end)
    ends(end)
    face(gather_face(column, LANES - EY))


def pack(value, half):
    lane = lane_index(value.shape[0] // 2)
    top, bottom = value[: value.shape[0] // 2], value[value.shape[0] // 2 :]
    if half:
        return jnp.where(lane < HALF, roll(top, HALF), bottom)
    return jnp.where(lane < HALF, top, roll(bottom, HALF))


def unpack(packed):
    return jnp.concatenate([packed, roll(packed, HALF)], axis=0)


def element_kernel(terms, layout, count, *refs):
    vel_hbm, slots_hbm, mats_hbm, geo_hbm = refs[:4]
    outs, scratch = refs[4 : 4 + count], refs[4 + count :]
    vel_ref, slots_ref, mats_ref, geo_ref, left_ref, *parts, sems = scratch[:9]
    pairs = [(slots_hbm, slots_ref), (geo_hbm, geo_ref), (mats_hbm, mats_ref)]
    pairs += [(vel_hbm.at[c], vel_ref.at[c]) for c in range(3)]
    copies = [pltpu.make_async_copy(*pair, sems.at[k]) for k, pair in enumerate(pairs)]
    for copy in copies:
        copy.start()
    depth = vel_ref.shape[2]
    parts[0][NODES:] = jnp.zeros((TALL - NODES, depth + 8, LANES), f32)
    sends = []
    corners = [jnp.zeros((depth, LANES), f32)]
    if layout:
        lower_ref, extras_ref, upper_ref, halves_ref, send_sems = scratch[9:]
        halves_ref[...] = jnp.zeros_like(halves_ref)
        extras_ref[...] = jnp.zeros_like(extras_ref)
        early, late = layout.divide(outs)
        sizes, base = layout.share(depth), layout.base(depth)
        full = base + upper_ref.shape[0] // depth
        buffers = ((lower_ref, 0), (extras_ref, None), (upper_ref, base), (halves_ref, None))
        for k, s in layout.blocks:
            place, target, done = layout.place(k, s), layout.sent(k, s, early, late), 0
            for (ref, begin), size in zip(buffers, sizes):
                source = ref.at[pl.ds(pl.multiple_of(place * size, 8), size)]
                if size:
                    target_part = target.at[pl.ds(done, size)]
                    copy = pltpu.make_async_copy(source, target_part, send_sems.at[len(sends)])
                    sends.append((place, begin, size // depth, copy))
                done += size

    def put_half(ref, at, value, half=0):
        ref[at * depth // 2 : (at + 1) * depth // 2] = pack(value, half)

    def put_extra(row, value):
        if layout:
            put_half(extras_ref, 2 * row, value)
            put_half(extras_ref, 2 * row + 1, value, 1)
        else:
            outs[1][row] = value

    def put_row(c, row, value):
        if row >= INNER:
            put_extra(SIDE * c + row - INNER, value)
            return
        row += c * INNER
        if not layout:
            outs[0][row] = value
        elif row < base:
            lower_ref[row * depth : (row + 1) * depth] = value
        elif row < full:
            upper_ref[(row - base) * depth : (row - base + 1) * depth] = value
        else:
            put_half(halves_ref, 2 * (row - full), value)
            put_half(halves_ref, 2 * (row - full) + 1, value, 1)

    def put_end(c, value):
        put_extra(ENDS + c, value)

    def put_face(c, value):
        if layout:
            put_half(extras_ref, 2 * FACES + c, value)
            corners[0] = jnp.where(lane_index(depth) == c, roll(value, c - FACE), corners[0])
        else:
            outs[1][FACES + c] = value

    for copy in copies[:3]:
        copy.wait()
    select = prepare(terms, slots_ref, mats_ref, left_ref)
    left = left_ref[...].reshape(len(terms) * DEEP, 2 * LANES)
    geo = geo_ref[...]
    copies[3].wait()
    for c in range(3):
        if c < 2:
            copies[4 + c].wait()
        puts = [functools.partial(store, c) for store in (put_row, put_end, put_face)]
        first, second = vel_ref.at[c], vel_ref.at[(c + 1) % 3]
        component(terms, first, second, select, geo, left, parts, *puts)
        for place, begin, count, copy in sends:
            if begin is None:
                continue
            blocks = len(layout.blocks)
            before, ready = (
                max(0, min(blocks, (rows - begin) // count)) for rows in (c * INNER, (c + 1) * INNER)
            )
            if before < ready == blocks and before == 0:
                copy.start()
            elif before < ready:
                pl.when(jnp.logical_and(place >= before, place < ready))(copy.start)
    if layout:
        put_half(extras_ref, CORNERS, corners[0])
    for _, begin, _, copy in sends:
        if begin is None:
            copy.start()
    for *_, copy in sends:
        copy.wait()


def elements(name, terms, layout, args):
    depth = args[0].shape[2]
    scratch = [
        *(pltpu.VMEM(a.shape, a.dtype) for a in args),
        pltpu.VMEM((len(terms), DEEP, 2 * LANES), bf16),
        pltpu.VMEM((TALL, depth + 8, LANES), f32),
        pltpu.VMEM((DEEP * depth, 2 * LANES), bf16),
        pltpu.VMEM((PITCH * depth, LANES), f32),
        pltpu.SemaphoreType.DMA((6,)),
    ]
    anywhere, vmem = pl.BlockSpec(memory_space=pl.ANY), pl.BlockSpec(memory_space=pltpu.VMEM)
    shapes, specs = [(3 * INNER, depth, LANES)], [vmem]
    if layout:
        count = len(layout.blocks)
        sizes = layout.share(depth)
        scratch += [pltpu.VMEM((count * max(size, 8), LANES), f32) for size in sizes]
        scratch.append(pltpu.SemaphoreType.DMA((4 * count,)))
        shapes = layout.shapes((sum(sizes), LANES))
        specs = [anywhere] * len(shapes)
    else:
        shapes.append((EXTRAS, depth, LANES))
        specs.append(vmem)
    return pl.pallas_call(
        functools.partial(element_kernel, terms, layout, len(shapes)),
        in_specs=[anywhere] * len(args),
        out_specs=specs,
        out_shape=[jax.ShapeDtypeStruct(shape, f32) for shape in shapes],
        scratch_shapes=scratch,
        compiler_params=pltpu.CompilerParams(vmem_limit_bytes=WIDE if layout else VMEM),
        cost_estimate=pl.CostEstimate(
            flops=2 * 3 * depth * len(terms) * DEEP * 3 * DEEP * LANES,
            bytes_accessed=4 * 3 * depth * LANES * 150,
            transcendentals=0,
        ),
        name=name,
    )(*args)


def left_sums(before, j):
    lane = lane_index(before.shape[0])
    if j < SIDE:
        return jnp.where(lane < EY, roll(before, -EY * j), 0.0)
    return jnp.where(lane == 0, roll(before, -FACE), 0.0)


def spanwise_kernel(layout, depth, count, *refs):
    got = layout.got(refs[:count])
    table_ref, early, late = refs[count], *layout.divide(refs[count + 1 :])
    length = len(layout.blocks) * depth
    table = table_ref[lax.rem(lax.axis_index("modes"), layout.inner)]
    rows, begin = [], 0
    for sublanes, size in zip(layout.share(depth), (depth, depth // 2) * 2):
        rows += [(at, size) for at in range(begin, begin + sublanes, size)]
        begin += sublanes
    for first in range(0, len(rows), 2):
        group = rows[first : first + 2]
        x = []
        for at, size in group:
            blocks = [got[block][at : at + size] for block in layout.blocks]
            if size < depth:
                blocks = [unpack(block) for block in blocks]
            x.append(jnp.concatenate(blocks, axis=0))
        x_high, x_low = split(jnp.concatenate(x, axis=1))
        y = jnp.dot(table, x_high, preferred_element_type=f32)
        y = y[:length] + y[length:]
        y += jnp.dot(table[:length], x_low, preferred_element_type=f32)
        for place, block in enumerate(layout.blocks):
            for k, (at, size) in enumerate(group):
                value = y[depth * place : depth * place + depth, LANES * k : LANES * k + LANES]
                value = value if size == depth else pack(value, 0)
                layout.sent(*block, early, late)[at : at + size] = value


def spanwise(layout, depth, values, table):
    length = len(layout.blocks) * depth
    sizes = layout.share(depth)
    shapes = layout.shapes((sum(sizes), LANES))
    return pl.pallas_call(
        functools.partial(spanwise_kernel, layout, depth, len(values)),
        out_shape=[jax.ShapeDtypeStruct(shape, f32) for shape in shapes],
        compiler_params=pltpu.CompilerParams(vmem_limit_bytes=VMEM),
        cost_estimate=pl.CostEstimate(
            flops=6 * length * len(layout.blocks) * sum(sizes) * LANES,
            bytes_accessed=8 * len(layout.blocks) * sum(sizes) * LANES,
            transcendentals=0,
        ),
        name="spanwise",
    )(*values, table)


def to_slots(nodes, select):
    return lax.dot_general(nodes, select, (((1,), (1,)), ((), ())), preferred_element_type=f32)


def pair_selector(slots_ref):
    select = selector(slots_ref[...]).astype(bf16)
    return jnp.concatenate([select, select], axis=1)


def single(ref, at, depth):
    return unpack(ref[at * depth // 2 : (at + 1) * depth // 2])


def double(ref, at, depth):
    lower, upper = single(ref, at, depth), single(ref, at + 1, depth)
    return jnp.where(lane_index(depth) < HALF, lower, roll(upper, HALF))


def totals_kernel(layout, u_ref, *refs):
    total_ref, faces_ref, halves_ref = refs[-3:]
    depth = u_ref.shape[1]
    begin, size = layout.share(depth)[:2]
    for (k, s), ref in layout.got(refs[:-3]).items():
        at = pl.ds(pl.multiple_of(layout.place(-k, s) * size, 8), size)
        halves_ref[at] = ref[begin : begin + size]
    corners = single(halves_ref, CORNERS, depth)
    lane = lane_index(depth)
    last = jnp.zeros((depth, LANES), f32)
    for c in range(3):
        column = []
        for j in range(SIDE + 1):
            row = ENDS + c if j == SIDE else SIDE * c + j
            column.append(u_ref[row] + double(halves_ref, 2 * row, depth))
            total_ref[row] = column[j]
        face = single(halves_ref, 2 * FACES + c, depth)
        face = jnp.where(lane_index(depth) == FACE, roll(corners, FACE - c), face)
        face += u_ref[FACES + c]
        total_ref[FACES + c] = face
        left = gather_face(column[:SIDE] + [roll(column[SIDE], EY - 1)], 0)
        faces_ref[c] = jnp.where(lane < HALF, face, roll(left, HALF))
        last = jnp.where(lane == c, roll(face, c - FACE), last)
        last = jnp.where(lane == SIDE + c, roll(left, SIDE + c - FACE), last)
    faces_ref[3] = last


def totals(layout, u, values):
    depth = u.shape[1]
    size = layout.share(depth)[1]
    return pl.pallas_call(
        functools.partial(totals_kernel, layout),
        out_shape=[
            jax.ShapeDtypeStruct(u.shape, f32),
            jax.ShapeDtypeStruct((4, depth, LANES), f32),
        ],
        scratch_shapes=[pltpu.VMEM((len(layout.blocks) * size, LANES), f32)],
        compiler_params=pltpu.CompilerParams(vmem_limit_bytes=VMEM),
        cost_estimate=pl.CostEstimate(flops=0, bytes_accessed=0, transcendentals=0),
        name="totals",
    )(u, *values)


def put_node(nodes_ref, depth, at, value):
    high, low = split(value)
    nodes_ref[pl.ds(at * depth, depth), :] = jnp.concatenate([high, low], axis=1)


def faces_kernel(
    t_ref, before_ref, after_ref, slots_ref, _, out_ref, nodes_ref, slots_out_ref, sems
):
    depth, lanes = t_ref.shape[1:]
    select = pair_selector(slots_ref)
    lane = lane_index(depth)
    across = lane % EY
    count = SIDE + 1
    copies = []
    for c in range(3):
        put = functools.partial(put_node, nodes_ref, depth)
        before = jnp.where(lane == FACE, roll(before_ref[3], FACE - c), before_ref[c])
        after = roll(after_ref[c], HALF)
        after = jnp.where(lane == FACE, roll(after_ref[3], FACE - SIDE - c), after)
        face = t_ref[FACES + c] + after
        end = t_ref[ENDS + c] + left_sums(before, SIDE)
        for j in range(SIDE):
            value = t_ref[SIDE * c + j] + left_sums(before, j)
            moved = roll(face, lanes - EY - EY * j)
            beyond = jnp.where(lane >= lanes - EY, moved, roll(value, -EY))
            put(j, value)
            put(count + j, beyond)
            if j == 0:
                last = jnp.where(across == EY - 1, roll(end, EY - 1), roll(value, -1))
                put(SIDE, last)
                corner = jnp.where(across == EY - 1, roll(end, -1), roll(beyond, -1))
                corner = jnp.where(lane == lanes - 1, roll(face, lanes - 1 - FACE), corner)
                put(count + SIDE, corner)
        slots_out_ref[c] = to_slots(nodes_ref[...], select).reshape(2, count, depth, lanes)
        for side in range(2):
            copy = pltpu.make_async_copy(
                slots_out_ref.at[c, side],
                out_ref.at[c, pl.ds(side * (NODES - count), count)],
                sems.at[c, side],
            )
            copy.start()
            copies.append(copy)
    for copy in copies:
        copy.wait()


def middle_groups(layout, depth, upper):
    group = SIDE - 1
    cut = layout.base(depth) // SIDE
    first, last = (cut, 3 * group) if upper else (0, cut)
    groups = []
    while first < last:
        count = min(last - first, group - first % group)
        groups.append((first // group, first % group + 1, count))
        first += count
    return groups


def middle_kernel(layout, upper, u_ref, t_ref, slots_ref, *refs):
    values = refs[: -7 if upper else -6]
    out_ref, nodes_ref, slots_out_ref, sems, rows_ref, halves_ref = refs[-6:]
    depth, lanes = u_ref.shape[1:]
    sizes = layout.share(depth)
    full, half = sizes[2:] if upper else (sizes[0], 0)
    base = layout.base(depth) if upper else 0
    whole = full // depth
    for (k, s), ref in layout.got(values).items():
        place = layout.place(-k, s)
        begin = sum(sizes[:2]) if upper and k != layout.late[1] else 0
        rows_ref[pl.ds(place * whole, whole)] = ref[begin : begin + full].reshape(
            whole, depth, lanes
        )
        if half:
            at = pl.ds(pl.multiple_of(place * half, 8), half)
            halves_ref[at] = ref[begin + full : begin + full + half]
    select = pair_selector(slots_ref)
    across = lane_index(depth) % EY
    line = SIDE + 1
    copies, done = [], 0
    for c, first, count in middle_groups(layout, depth, upper):
        put = functools.partial(put_node, nodes_ref, depth)
        end = t_ref[ENDS + c]
        for i in range(first, first + count):
            for j in range(SIDE):
                row = c * INNER + SIDE * (i - 1) + j
                value = u_ref[row]
                if row - base < rows_ref.shape[0]:
                    value += rows_ref[row - base]
                else:
                    value += double(halves_ref, 2 * (row - base - rows_ref.shape[0]), depth)
                at = line * (done + i - first)
                put(at + j, value)
                if j == 0:
                    last = jnp.where(across == EY - 1, roll(end, EY - 1 - i), roll(value, -1))
                    put(at + SIDE, last)
        nodes = nodes_ref[pl.ds(line * done * depth, line * count * depth), :]
        part = pl.ds(line * done, line * count)
        slots_out_ref[part] = to_slots(nodes, select).reshape(line * count, depth, lanes)
        copy = pltpu.make_async_copy(
            slots_out_ref.at[part],
            out_ref.at[c, pl.ds(line * first, line * count)],
            sems.at[len(copies)],
        )
        copy.start()
        copies.append(copy)
        done += count
    for copy in copies:
        copy.wait()


def middle(layout, upper, args, values, result):
    depth = args[0].shape[1]
    sizes = layout.share(depth)
    groups = middle_groups(layout, depth, upper)
    count = (SIDE + 1) * sum(group[2] for group in groups)
    blocks = len(layout.blocks)
    full, half = sizes[2:] if upper else (sizes[0], 0)
    scratch = [
        pltpu.VMEM((count * depth, 2 * LANES), bf16),
        pltpu.VMEM((count, depth, LANES), f32),
        pltpu.SemaphoreType.DMA((len(groups),)),
        pltpu.VMEM((blocks * full // depth, depth, LANES), f32),
        pltpu.VMEM((blocks * max(half, 8), LANES), f32),
    ]
    kernel = functools.partial(middle_kernel, layout, upper)
    return expand(kernel, "upper" if upper else "lower", scratch, (*args, *values), result)


def expand(kernel, name, scratch, args, result=None):
    depth = args[0].shape[1]
    in_specs = [pl.BlockSpec(memory_space=pltpu.VMEM)] * len(args)
    aliases = {}
    if result is not None:
        aliases = {len(args): 0}
        args = (*args, result)
        in_specs.append(pl.BlockSpec(memory_space=pl.ANY))
    return pl.pallas_call(
        kernel,
        in_specs=in_specs,
        out_specs=pl.BlockSpec(memory_space=pl.ANY),
        out_shape=jax.ShapeDtypeStruct((3, NODES, depth, LANES), f32),
        scratch_shapes=scratch,
        input_output_aliases=aliases,
        compiler_params=pltpu.CompilerParams(vmem_limit_bytes=VMEM),
        cost_estimate=pl.CostEstimate(flops=0, bytes_accessed=0, transcendentals=0),
        name=name,
    )(*args)


def beside(faces):
    count = lax.axis_size("dom")
    onward = [(k, (k + 1) % count) for k in range(count)]
    back = [(k, (k - 1) % count) for k in range(count)]
    before = lax.ppermute(faces, "dom", onward)
    return before, before if onward == back else lax.ppermute(faces, "dom", back)


def local(velocity, slot_of_cell, elem_mats, geometry):
    depth = velocity.shape[1]
    layout = Layout(lax.axis_size("modes"))
    args = (velocity.transpose(0, 2, 1, 3), slot_of_cell, elem_mats.transpose(1, 0, 2), geometry)
    table = jnp.asarray(operator(layout, depth))
    early, late = layout.start(*layout.divide(elements("mass", (3,), layout, args)))
    pencil = late + layout.middle(late) + layout.end(early)
    u, u_extras = elements("stiff", (0, 1, 2), None, args)
    table = following([table], u)[0]
    cut = sum(layout.share(depth)[:2])
    early, late = layout.start(*layout.divide(spanwise(layout, depth, pencil, table)))
    lower = layout.middle(late, slice(None, cut))
    upper = layout.middle(late, slice(cut, None))
    ended = layout.end(early)
    total, faces = totals(layout, u_extras, late + lower + ended)
    before, after = beside(faces)
    scratch = [
        pltpu.VMEM((2 * (SIDE + 1) * depth, 2 * LANES), bf16),
        pltpu.VMEM((3, 2, SIDE + 1, depth, LANES), f32),
        pltpu.SemaphoreType.DMA((3, 2)),
    ]
    args = (u, total, slot_of_cell)
    result = middle(layout, False, args, late + lower + ended, None)
    result = expand(faces_kernel, "faces", scratch, (total, before, after, slot_of_cell), result)
    result = middle(layout, True, args, late + upper + ended, result)
    return result.transpose(0, 2, 1, 3)


def solution(mesh):
    in_specs = (P(None, "modes", None, "dom"), P("dom", None), P(), P(None, "dom"))
    out_specs = P(None, "modes", None, "dom")
    return jax.shard_map(local, mesh=mesh, in_specs=in_specs, out_specs=out_specs, check_vma=False)
```

time: 95.8 us -> 92.6 us (0.967)
  waiting for transfers between devices: 63.4 us -> 53.4 us
  starting transfers between devices: 13.9 us -> 22 us
  local copies, waits for them, and re-layouts: 2.07 us -> 1.11 us
    ppermute x6 -> x7, waiting for transfers between devices: 38.1 us -> 22.6 us  [onward(): return lax.ppermute(value, 'modes', steps)]
    ppermute x12, starting transfers between devices: 7.87 us -> 15.8 us  [across(): lax.ppermute(value, 'modes', pairs(s))]
    ppermute x12, waiting for transfers between devices: 24.2 us -> 29.7 us  [across(): lax.ppermute(value, 'modes', pairs(s))]
    pallas_call x2, Pallas kernels: 11.4 us -> 10 us  [elements(): pl.pallas_call(functools.partial(element_kernel, terms, layout, len(shape...]
    pallas_call x2 -> x3, Pallas kernels: 2.78 us -> 3.85 us  [expand(): pl.pallas_call(kernel, in_specs=in_specs, out_specs=pl.BlockSpec(memory_s...]
    squeeze x1 -> x0, local copies, waits for them, and re-layouts: 0.97 us -> none  [local(): lax.dynamic_index_in_dim(table, lax.rem(lax.axis_index('modes'), layout.i...]
    ppermute x6 -> x7, starting transfers between devices: 4.45 us -> 4.6 us  [onward(): return lax.ppermute(value, 'modes', steps)]
  transfers between devices with their start and end apart: 19 -> 20, of which waited for: 12 -> 12; matrix products, arithmetic and copies ran while one was open for 2% -> 1% of each run, Pallas kernels for 7% -> 8%
where the time goes in v4:
time: 92.6 us; the launch traced here: 92.4 us
  waiting for transfers between devices  53.4 us (58%)
  starting transfers between devices  22 us (24%)
  Pallas kernels  15.4 us (17%)
  local copies, waits for them, and re-layouts  1.11 us (1%)
    ppermute x12, waiting for transfers between devices, across(): lax.ppermute(value, 'modes', pairs(s))  29.7 us
    ppermute x7, waiting for transfers between devices, onward(): return lax.ppermute(value, 'modes', steps)  22.6 us
    ppermute x12, starting transfers between devices, across(): lax.ppermute(value, 'modes', pairs(s))  15.8 us
    pallas_call x2, Pallas kernels, elements(): pl.pallas_call(functools.partial(element_kernel, terms, layout, len(shape...  10 us
    ppermute x7, starting transfers between devices, onward(): return lax.ppermute(value, 'modes', steps)  4.6 us
    pallas_call x3, Pallas kernels, expand(): pl.pallas_call(kernel, in_specs=in_specs, out_specs=pl.BlockSpec(memory_s...  3.85 us
  transfers between devices with their start and end apart: 20, of which 12 were waited for; matrix products, arithmetic and copies ran while one was open for 1% of the time, Pallas kernels for 8%

profile of v4, /device:TPU:16, one launch (start us, length us, event | category | flops | bytes accessed | tf_op | source)
XLA Modules:
  0.0 92.4 jit_solution(2778360783847119576)
XLA Ops:
  0.0 5.6 %mass.1 = (f32[4,200,128]{2,1,0:T(8,128)}, f32[4,200,128]{2,1,0:T(8,128)}, f32[2,200,128]{2,1,0:T(8,128)}, f32[2,200,128]{2,1,0:T(8,128)}, f32[2,200,128]{2,1,0:T(8,128)}, /*index=5*/f32[2,200,128]{2,1,0:T(8,128)}) custom-call(f32[3,81,16,128]{3,2,1,0:T(8,128)} %bitcast.3, s32[1,128]{1,0:T(1,128)} %slots_ref.5, f32[81,4,81]{2,1,0:T(4,128)} %bitcast.5, ...), custom_call_target="tpu_custom_call" | custom-call | flops 339738624 | bytes 3686400 | tf_op jit(solution)/shard_map/mass/pallas_call | solution.py:357
  5.6 1.6 %collective-permute-start.4 = (f32[4,200,128]{2,1,0:T(8,128)}, f32[4,200,128]{2,1,0:T(8,128)S(1)}, u32[]{:S(2)}, u32[]{:S(2)}) collective-permute-start(f32[4,200,128]{2,1,0:T(8,128)} %get-tuple-element.28), channel_id=1, source_target_pairs={{0,8},{2,10},{4,12},{6,14},{8,16},{10,18},{12,20},{14,22},{16,24},... | collective-permute-start | bytes 1228808 | tf_op jit(solution)/shard_map/ppermute | solution.py:93
  7.3 0.0 collective-permute-start
  7.3 1.5 %collective-permute-start.1 = (f32[2,200,128]{2,1,0:T(8,128)}, f32[2,200,128]{2,1,0:T(8,128)S(1)}, u32[]{:S(2)}, u32[]{:S(2)}) collective-permute-start(f32[2,200,128]{2,1,0:T(8,128)} %get-tuple-element.26), channel_id=1, source_target_pairs={{0,4},{2,6},{4,0},{6,2},{8,12},{10,14},{12,8},{14,10},{16,20},{18,... | collective-permute-start | bytes 614408 | tf_op jit(solution)/shard_map/ppermute | solution.py:98
  8.8 0.3 collective-permute-start.2
  9.1 0.5 collective-permute-start.5
  9.6 0.9 slice.84
  10.5 0.0 collective-permute-done.refs_1_
  10.5 4.8 %collective-permute-done.1.refs_2_ = f32[2,200,128]{2,1,0:T(8,128)S(1)} collective-permute-done((f32[2,200,128]{2,1,0:T(8,128)}, f32[2,200,128]{2,1,0:T(8,128)S(1)}, u32[]{:S(2)}, u32[]{:S(2)}) %collective-permute-start.1) | collective-permute-done | bytes 204832 | tf_op jit(solution)/shard_map/ppermute | solution.py:98
  15.4 0.0 copy-start
  15.4 0.0 copy-start.3
  15.4 0.0 copy-start.4
  15.4 0.0 copy-start.5
  15.4 3.6 %collective-permute-done.2.refs_3_ = f32[2,200,128]{2,1,0:T(8,128)S(1)} collective-permute-done((f32[2,200,128]{2,1,0:T(8,128)}, f32[2,200,128]{2,1,0:T(8,128)S(1)}, u32[]{:S(2)}, u32[]{:S(2)}) %collective-permute-start.2) | collective-permute-done | bytes 204832 | tf_op jit(solution)/shard_map/ppermute | solution.py:98
  19.0 0.4 collective-permute-start.3
  19.5 7.1 %collective-permute-done.5 = f32[4,200,128]{2,1,0:T(8,128)S(1)} collective-permute-done((f32[4,200,128]{2,1,0:T(8,128)}, f32[4,200,128]{2,1,0:T(8,128)S(1)}, u32[]{:S(2)}, u32[]{:S(2)}) %collective-permute-start.5) | collective-permute-done | bytes 409632 | tf_op jit(solution)/shard_map/ppermute | solution.py:93
  26.7 0.1 collective-permute-start.6
  26.8 9.7 %collective-permute-start.7 = (f32[2,200,128]{2,1,0:T(8,128)S(1)}, f32[2,200,128]{2,1,0:T(8,128)S(1)}, u32[]{:S(2)}, u32[]{:S(2)}) collective-permute-start(f32[2,200,128]{2,1,0:T(8,128)S(1)} %pad_maximum_fusion.4), channel_id=1, source_target_pairs={{0,4},{2,6},{4,0},{6,2},{8,12},{10,14},{12,8},{14,10},{16,20},{18,... | collective-permute-start | bytes 614408 | tf_op jit(solution)/shard_map/ppermute | solution.py:98
  36.5 0.0 copy-start.1
  36.5 0.2 collective-permute-start.8
  36.7 4.4 %stiff.1 = (f32[168,16,128]{2,1,0:T(8,128)S(1)}, f32[30,16,128]{2,1,0:T(8,128)S(1)}) custom-call(f32[3,81,16,128]{3,2,1,0:T(8,128)S(1)} %bitcast.4, s32[1,128]{1,0:T(1,128)S(1)} %copy-done.4, f32[81,4,81]{2,1,0:T(4,128)S(1)} %bitcast.6, f32[4,128]{1,0:T(4,128)S(1)} %copy-done.5), custom_call_target="tpu_custom_call" | custom-call | flops 1019215872 | bytes 3686400 | tf_op jit(solution)/shard_map/stiff/pallas_call | solution.py:357
  41.1 1.1 %collective-permute-done.3.refs_4_ = f32[4,200,128]{2,1,0:T(8,128)S(1)} collective-permute-done((f32[4,200,128]{2,1,0:T(8,128)S(1)}, f32[4,200,128]{2,1,0:T(8,128)S(1)}, u32[]{:S(2)}, u32[]{:S(2)}) %collective-permute-start.3) | collective-permute-done | bytes 409632 | tf_op jit(solution)/shard_map/ppermute | solution.py:93
  42.3 0.1 collective-permute-done.7.refs_7_
  42.4 4.0 %collective-permute-done.8.refs_8_ = f32[2,200,128]{2,1,0:T(8,128)S(1)} collective-permute-done((f32[2,200,128]{2,1,0:T(8,128)S(1)}, f32[2,200,128]{2,1,0:T(8,128)S(1)}, u32[]{:S(2)}, u32[]{:S(2)}) %collective-permute-start.8) | collective-permute-done | bytes 204832 | tf_op jit(solution)/shard_map/ppermute | solution.py:98
  46.4 1.1 %spanwise.1 = (f32[4,200,128]{2,1,0:T(8,128)S(1)}, f32[4,200,128]{2,1,0:T(8,128)S(1)}, f32[2,200,128]{2,1,0:T(8,128)S(1)}, f32[2,200,128]{2,1,0:T(8,128)S(1)}, f...) custom-call(f32[2,200,128]{2,1,0:T(8,128)S(1)} %copy-done.2, f32[2,200,128]{2,1,0:T(8,128)S(1)} %collective-permute-done.refs_1_, ...), custom_call_target="tpu_custom_call" | custom-call | flops 629145600 | bytes 3276800 | tf_op jit(solution)/shard_map/spanwise/pallas_call | solution.py:412
  47.5 0.1 collective-permute-start.13
  47.5 0.2 collective-permute-start.9
  47.7 1.6 %collective-permute-start.10 = (f32[2,200,128]{2,1,0:T(8,128)S(1)}, f32[2,200,128]{2,1,0:T(8,128)S(1)}, u32[]{:S(2)}, u32[]{:S(2)}) collective-permute-start(f32[2,200,128]{2,1,0:T(8,128)S(1)} %get-tuple-element.33), channel_id=1, source_target_pairs={{0,4},{2,6},{4,0},{6,2},{8,12},{10,14},{12,8},{14,10},{16,20},{18,... | collective-permute-start | bytes 614408 | tf_op jit(solution)/shard_map/ppermute | solution.py:98
  49.3 0.1 collective-permute-start.11
  49.5 1.9 %collective-permute-start.14 = (f32[4,200,128]{2,1,0:T(8,128)S(1)}, f32[4,200,128]{2,1,0:T(8,128)S(1)}, u32[]{:S(2)}, u32[]{:S(2)}) collective-permute-start(f32[4,200,128]{2,1,0:T(8,128)S(1)} %get-tuple-element.36), channel_id=1, source_target_pairs={{0,24},{2,26},{4,28},{6,30},{8,0},{10,2},{12,4},{14,6},{16,8},{18,... | collective-permute-start | bytes 1228808 | tf_op jit(solution)/shard_map/ppermute | solution.py:93
  51.4 0.0 collective-permute-done.9.refs_1_
  51.4 4.2 %collective-permute-done.10.refs_2_ = f32[2,200,128]{2,1,0:T(8,128)S(1)} collective-permute-done((f32[2,200,128]{2,1,0:T(8,128)S(1)}, f32[2,200,128]{2,1,0:T(8,128)S(1)}, u32[]{:S(2)}, u32[]{:S(2)}) %collective-permute-start.10) | collective-permute-done | bytes 204832 | tf_op jit(solution)/shard_map/ppermute | solution.py:98
  55.6 3.4 %collective-permute-done.11.refs_3_ = f32[2,200,128]{2,1,0:T(8,128)S(1)} collective-permute-done((f32[2,200,128]{2,1,0:T(8,128)S(1)}, f32[2,200,128]{2,1,0:T(8,128)S(1)}, u32[]{:S(2)}, u32[]{:S(2)}) %collective-permute-start.11) | collective-permute-done | bytes 204832 | tf_op jit(solution)/shard_map/ppermute | solution.py:98
  59.0 0.1 collective-permute-start.12
  59.2 14.4 %collective-permute-done.13 = f32[4,200,128]{2,1,0:T(8,128)S(1)} collective-permute-done((f32[4,200,128]{2,1,0:T(8,128)S(1)}, f32[4,200,128]{2,1,0:T(8,128)S(1)}, u32[]{:S(2)}, u32[]{:S(2)}) %collective-permute-start.13) | collective-permute-done | bytes 409632 | tf_op jit(solution)/shard_map/ppermute | solution.py:93
  73.6 0.1 collective-permute-start.17
  73.7 1.6 %collective-permute-start.16 = (f32[2,200,128]{2,1,0:T(8,128)S(1)}, f32[2,200,128]{2,1,0:T(8,128)S(1)}, u32[]{:S(2)}, u32[]{:S(2)}) collective-permute-start(f32[2,200,128]{2,1,0:T(8,128)S(1)} %pad_maximum_fusion.8), channel_id=1, source_target_pairs={{0,4},{2,6},{4,0},{6,2},{8,12},{10,14},{12,8},{14,10},{16,20},{18,... | collective-permute-start | bytes 614408 | tf_op jit(solution)/shard_map/ppermute | solution.py:98
  75.3 0.4 collective-permute-start.15
  75.7 0.1 collective-permute-start.18
  75.8 5.1 %collective-permute-done.17.refs_8_ = f32[2,200,128]{2,1,0:T(8,128)S(1)} collective-permute-done((f32[2,200,128]{2,1,0:T(8,128)S(1)}, f32[2,200,128]{2,1,0:T(8,128)S(1)}, u32[]{:S(2)}, u32[]{:S(2)}) %collective-permute-start.17) | collective-permute-done | bytes 204832 | tf_op jit(solution)/shard_map/ppermute | solution.py:98
  81.0 4.5 %collective-permute-done.16.refs_7_ = f32[2,200,128]{2,1,0:T(8,128)S(1)} collective-permute-done((f32[2,200,128]{2,1,0:T(8,128)S(1)}, f32[2,200,128]{2,1,0:T(8,128)S(1)}, u32[]{:S(2)}, u32[]{:S(2)}) %collective-permute-start.16) | collective-permute-done | bytes 204832 | tf_op jit(solution)/shard_map/ppermute | solution.py:98
  85.4 0.0 collective-permute-done.15.refs_6_
  85.4 0.4 totals.1
  85.9 1.6 %collective-permute-start.19 = (f32[4,16,128]{2,1,0:T(8,128)S(1)}, f32[4,16,128]{2,1,0:T(8,128)S(1)}, u32[]{:S(2)}, u32[]{:S(2)}) collective-permute-start(f32[4,16,128]{2,1,0:T(8,128)S(1)} %get-tuple-element.38), channel_id=1, source_target_pairs={{0,1},{1,0},{2,3},{3,2},{4,5},{5,4},{6,7},{7,6},{8,9},{9,8},{10,11... | collective-permute-start | bytes 98312 | tf_op jit(solution)/shard_map/ppermute | solution.py:639
  87.4 1.3 %lower.1._ = f32[3,81,16,128]{3,2,1,0:T(8,128)} custom-call(f32[168,16,128]{2,1,0:T(8,128)S(1)} %get-tuple-element.22.u_ref, f32[30,16,128]{2,1,0:T(8,128)S(1)} %get-tuple-element.37.t_ref, s32[1,128]{1,0:T(1,128)S(1)} %copy-done.4, f32[2,200,128]{2,1,0:T(8,128)S(1)} %get-tuple-element.31.refs_0_, f32[2,200,128]{2,1,0:T(8,128)S(1)} %collective-permute-done.9.refs_1_, ...), custom_call_target="tpu_custom_call" | custom-call | tf_op jit(solution)/shard_map/lower/pallas_call | solution.py:622
  88.7 1.1 %collective-permute-done.19.before_ref.after_ref = f32[4,16,128]{2,1,0:T(8,128)S(1)} collective-permute-done((f32[4,16,128]{2,1,0:T(8,128)S(1)}, f32[4,16,128]{2,1,0:T(8,128)S(1)}, u32[]{:S(2)}, u32[]{:S(2)}) %collective-permute-start.19) | collective-permute-done | bytes 32800 | tf_op jit(solution)/shard_map/ppermute | solution.py:639
  89.8 1.2 %faces.1.refs_9_ = f32[3,81,16,128]{3,2,1,0:T(8,128)} custom-call(f32[30,16,128]{2,1,0:T(8,128)S(1)} %get-tuple-element.37.t_ref, f32[4,16,128]{2,1,0:T(8,128)S(1)} %collective-permute-done.19.before_ref.after_ref, f32[4,16,128]{2,1,0:T(8,128)S(1)} %collective-permute-done.19.before_ref.after_ref, ...), custom_call_target="tpu_custom_call", output_to_operand_aliasing={{}: (4, {})} | custom-call | tf_op jit(solution)/shard_map/faces/pallas_call | solution.py:622
  91.1 1.3 %upper.1 = f32[3,81,16,128]{3,2,1,0:T(8,128)} custom-call(f32[168,16,128]{2,1,0:T(8,128)S(1)} %get-tuple-element.22.u_ref, f32[30,16,128]{2,1,0:T(8,128)S(1)} %get-tuple-element.37.t_ref, s32[1,128]{1,0:T(1,128)S(1)} %copy-done.4, f32[2,200,128]{2,1,0:T(8,128)S(1)} %get-tuple-element.31.refs_0_, ...), custom_call_target="tpu_custom_call", output_to_operand_aliasing={{}: (12, {})} | custom-call | tf_op jit(solution)/shard_map/upper/pallas_call | solution.py:622
  (38 shorter events, 0.5 us)
Async XLA Ops:
  5.6 13.8 %collective-permute-start.4 = (f32[4,200,128]{2,1,0:T(8,128)}, f32[4,200,128]{2,1,0:T(8,128)S(1)}, u32[]{:S(2)}, u32[]{:S(2)}) collective-permute-start(f32[4,200,128]{2,1,0:T(8,128)} %get-tuple-element.28), channel_id=1, source_target_pairs={{0,8},{2,10},{4,12},{6,14},{8,16},{10,18},{12,20},{14,22},{16,24},... | collective-permute-start | bytes 1228808 | tf_op jit(solution)/shard_map/ppermute | solution.py:93
  7.3 3.2 %collective-permute-start = (f32[2,200,128]{2,1,0:T(8,128)}, f32[2,200,128]{2,1,0:T(8,128)S(1)}, u32[]{:S(2)}, u32[]{:S(2)}) collective-permute-start(f32[2,200,128]{2,1,0:T(8,128)} %get-tuple-element.25), channel_id=1, source_target_pairs={{0,2},{2,0},{4,6},{6,4},{8,10},{10,8},{12,14},{14,12},{16,18},{18,... | collective-permute-start | bytes 614408 | tf_op jit(solution)/shard_map/ppermute | solution.py:98
  7.3 8.1 %collective-permute-start.1 = (f32[2,200,128]{2,1,0:T(8,128)}, f32[2,200,128]{2,1,0:T(8,128)S(1)}, u32[]{:S(2)}, u32[]{:S(2)}) collective-permute-start(f32[2,200,128]{2,1,0:T(8,128)} %get-tuple-element.26), channel_id=1, source_target_pairs={{0,4},{2,6},{4,0},{6,2},{8,12},{10,14},{12,8},{14,10},{16,20},{18,... | collective-permute-start | bytes 614408 | tf_op jit(solution)/shard_map/ppermute | solution.py:98
  8.8 10.2 %collective-permute-start.2 = (f32[2,200,128]{2,1,0:T(8,128)}, f32[2,200,128]{2,1,0:T(8,128)S(1)}, u32[]{:S(2)}, u32[]{:S(2)}) collective-permute-start(f32[2,200,128]{2,1,0:T(8,128)} %get-tuple-element.27), channel_id=1, source_target_pairs={{0,6},{2,4},{4,2},{6,0},{8,14},{10,12},{12,10},{14,8},{16,22},{18,... | collective-permute-start | bytes 614408 | tf_op jit(solution)/shard_map/ppermute | solution.py:98
  9.1 17.5 %collective-permute-start.5 = (f32[4,200,128]{2,1,0:T(8,128)}, f32[4,200,128]{2,1,0:T(8,128)S(1)}, u32[]{:S(2)}, u32[]{:S(2)}) collective-permute-start(f32[4,200,128]{2,1,0:T(8,128)} %get-tuple-element.29), channel_id=1, source_target_pairs={{0,24},{2,26},{4,28},{6,30},{8,0},{10,2},{12,4},{14,6},{16,8},{18,... | collective-permute-start | bytes 1228808 | tf_op jit(solution)/shard_map/ppermute | solution.py:93
  15.4 21.3 %copy-start = (f32[3,16,81,128]{3,1,2,0:T(8,128)S(1)}, f32[3,16,81,128]{3,1,2,0:T(8,128)}, u32[]{:S(2)}) copy-start(f32[3,16,81,128]{3,1,2,0:T(8,128)} %param.5) | copy-start | bytes 5971972
  15.4 21.3 %copy-start.3 = (f32[4,81,81]{2,0,1:T(4,128)S(1)}, f32[4,81,81]{2,0,1:T(4,128)}, u32[]{:S(2)}) copy-start(f32[4,81,81]{2,0,1:T(4,128)} %param.7) | copy-start | bytes 314932
  15.4 21.3 %copy-start.4 = (s32[1,128]{1,0:T(1,128)S(1)}, s32[1,128]{1,0:T(1,128)}, u32[]{:S(2)}) copy-start(s32[1,128]{1,0:T(1,128)} %slots_ref.5) | copy-start | bytes 1540
  15.4 21.3 %copy-start.5 = (f32[4,128]{1,0:T(4,128)S(1)}, f32[4,128]{1,0:T(4,128)}, u32[]{:S(2)}) copy-start(f32[4,128]{1,0:T(4,128)} %refs_3_.3) | copy-start | bytes 6148
  19.0 23.2 %collective-permute-start.3 = (f32[4,200,128]{2,1,0:T(8,128)S(1)}, f32[4,200,128]{2,1,0:T(8,128)S(1)}, u32[]{:S(2)}, u32[]{:S(2)}) collective-permute-start(f32[4,200,128]{2,1,0:T(8,128)S(1)} %pad_maximum_fusion), channel_id=1, source_target_pairs={{0,16},{2,18},{4,20},{6,22},{8,24},{10,26},{12,28},{14,30},{16,0},... | collective-permute-start | bytes 1228808 | tf_op jit(solution)/shard_map/ppermute | solution.py:93
  26.7 15.6 %collective-permute-start.6 = (f32[2,200,128]{2,1,0:T(8,128)S(1)}, f32[2,200,128]{2,1,0:T(8,128)S(1)}, u32[]{:S(2)}, u32[]{:S(2)}) collective-permute-start(f32[2,200,128]{2,1,0:T(8,128)S(1)} %pad_maximum_fusion.3), channel_id=1, source_target_pairs={{0,2},{2,0},{4,6},{6,4},{8,10},{10,8},{12,14},{14,12},{16,18},{18,... | collective-permute-start | bytes 614408 | tf_op jit(solution)/shard_map/ppermute | solution.py:98
  26.8 15.6 %collective-permute-start.7 = (f32[2,200,128]{2,1,0:T(8,128)S(1)}, f32[2,200,128]{2,1,0:T(8,128)S(1)}, u32[]{:S(2)}, u32[]{:S(2)}) collective-permute-start(f32[2,200,128]{2,1,0:T(8,128)S(1)} %pad_maximum_fusion.4), channel_id=1, source_target_pairs={{0,4},{2,6},{4,0},{6,2},{8,12},{10,14},{12,8},{14,10},{16,20},{18,... | collective-permute-start | bytes 614408 | tf_op jit(solution)/shard_map/ppermute | solution.py:98
  36.5 9.9 %copy-start.1 = (bf16[4,512,256]{2,1,0:T(8,128)(2,1)S(1)}, bf16[4,512,256]{2,1,0:T(8,128)(2,1)}, u32[]{:S(2)}) copy-start(bf16[4,512,256]{2,1,0:T(8,128)(2,1)} %constant.2.clone.refs_9_) | copy-start | bytes 3145732
  36.5 9.9 %copy-start.2 = (f32[2,200,128]{2,1,0:T(8,128)S(1)}, f32[2,200,128]{2,1,0:T(8,128)}, u32[]{:S(2)}) copy-start(f32[2,200,128]{2,1,0:T(8,128)} %get-tuple-element.24.refs_0_) | copy-start | bytes 614404
  36.5 9.9 %collective-permute-start.8 = (f32[2,200,128]{2,1,0:T(8,128)S(1)}, f32[2,200,128]{2,1,0:T(8,128)S(1)}, u32[]{:S(2)}, u32[]{:S(2)}) collective-permute-start(f32[2,200,128]{2,1,0:T(8,128)S(1)} %pad_maximum_fusion.5), channel_id=1, source_target_pairs={{0,6},{2,4},{4,2},{6,0},{8,14},{10,12},{12,10},{14,8},{16,22},{18,... | collective-permute-start | bytes 614408 | tf_op jit(solution)/shard_map/ppermute | solution.py:98
  47.5 26.1 %collective-permute-start.13 = (f32[4,200,128]{2,1,0:T(8,128)S(1)}, f32[4,200,128]{2,1,0:T(8,128)S(1)}, u32[]{:S(2)}, u32[]{:S(2)}) collective-permute-start(f32[4,200,128]{2,1,0:T(8,128)S(1)} %get-tuple-element.35), channel_id=1, source_target_pairs={{0,8},{2,10},{4,12},{6,14},{8,16},{10,18},{12,20},{14,22},{16,24},... | collective-permute-start | bytes 1228808 | tf_op jit(solution)/shard_map/ppermute | solution.py:93
  47.5 3.9 %collective-permute-start.9 = (f32[2,200,128]{2,1,0:T(8,128)S(1)}, f32[2,200,128]{2,1,0:T(8,128)S(1)}, u32[]{:S(2)}, u32[]{:S(2)}) collective-permute-start(f32[2,200,128]{2,1,0:T(8,128)S(1)} %get-tuple-element.32), channel_id=1, source_target_pairs={{0,2},{2,0},{4,6},{6,4},{8,10},{10,8},{12,14},{14,12},{16,18},{18,... | collective-permute-start | bytes 614408 | tf_op jit(solution)/shard_map/ppermute | solution.py:98
  47.7 7.9 %collective-permute-start.10 = (f32[2,200,128]{2,1,0:T(8,128)S(1)}, f32[2,200,128]{2,1,0:T(8,128)S(1)}, u32[]{:S(2)}, u32[]{:S(2)}) collective-permute-start(f32[2,200,128]{2,1,0:T(8,128)S(1)} %get-tuple-element.33), channel_id=1, source_target_pairs={{0,4},{2,6},{4,0},{6,2},{8,12},{10,14},{12,8},{14,10},{16,20},{18,... | collective-permute-start | bytes 614408 | tf_op jit(solution)/shard_map/ppermute | solution.py:98
  49.3 9.7 %collective-permute-start.11 = (f32[2,200,128]{2,1,0:T(8,128)S(1)}, f32[2,200,128]{2,1,0:T(8,128)S(1)}, u32[]{:S(2)}, u32[]{:S(2)}) collective-permute-start(f32[2,200,128]{2,1,0:T(8,128)S(1)} %get-tuple-element.34), channel_id=1, source_target_pairs={{0,6},{2,4},{4,2},{6,0},{8,14},{10,12},{12,10},{14,8},{16,22},{18,... | collective-permute-start | bytes 614408 | tf_op jit(solution)/shard_map/ppermute | solution.py:98
  49.5 24.1 %collective-permute-start.14 = (f32[4,200,128]{2,1,0:T(8,128)S(1)}, f32[4,200,128]{2,1,0:T(8,128)S(1)}, u32[]{:S(2)}, u32[]{:S(2)}) collective-permute-start(f32[4,200,128]{2,1,0:T(8,128)S(1)} %get-tuple-element.36), channel_id=1, source_target_pairs={{0,24},{2,26},{4,28},{6,30},{8,0},{10,2},{12,4},{14,6},{16,8},{18,... | collective-permute-start | bytes 1228808 | tf_op jit(solution)/shard_map/ppermute | solution.py:93
  59.0 16.8 %collective-permute-start.12 = (f32[4,112,128]{2,1,0:T(8,128)S(1)}, f32[4,112,128]{2,1,0:T(8,128)S(1)}, u32[]{:S(2)}, u32[]{:S(2)}) collective-permute-start(f32[4,112,128]{2,1,0:T(8,128)S(1)} %pad_maximum_fusion.1), channel_id=1, source_target_pairs={{0,16},{2,18},{4,20},{6,22},{8,24},{10,26},{12,28},{14,30},{16,0},... | collective-permute-start | bytes 688136 | tf_op jit(solution)/shard_map/ppermute | solution.py:93
  73.6 7.4 %collective-permute-start.17 = (f32[2,200,128]{2,1,0:T(8,128)S(1)}, f32[2,200,128]{2,1,0:T(8,128)S(1)}, u32[]{:S(2)}, u32[]{:S(2)}) collective-permute-start(f32[2,200,128]{2,1,0:T(8,128)S(1)} %pad_maximum_fusion.9), channel_id=1, source_target_pairs={{0,6},{2,4},{4,2},{6,0},{8,14},{10,12},{12,10},{14,8},{16,22},{18,... | collective-permute-start | bytes 614408 | tf_op jit(solution)/shard_map/ppermute | solution.py:98
  73.7 11.7 %collective-permute-start.16 = (f32[2,200,128]{2,1,0:T(8,128)S(1)}, f32[2,200,128]{2,1,0:T(8,128)S(1)}, u32[]{:S(2)}, u32[]{:S(2)}) collective-permute-start(f32[2,200,128]{2,1,0:T(8,128)S(1)} %pad_maximum_fusion.8), channel_id=1, source_target_pairs={{0,4},{2,6},{4,0},{6,2},{8,12},{10,14},{12,8},{14,10},{16,20},{18,... | collective-permute-start | bytes 614408 | tf_op jit(solution)/shard_map/ppermute | solution.py:98
  75.3 10.1 %collective-permute-start.15 = (f32[2,200,128]{2,1,0:T(8,128)S(1)}, f32[2,200,128]{2,1,0:T(8,128)S(1)}, u32[]{:S(2)}, u32[]{:S(2)}) collective-permute-start(f32[2,200,128]{2,1,0:T(8,128)S(1)} %pad_maximum_fusion.7), channel_id=1, source_target_pairs={{0,2},{2,0},{4,6},{6,4},{8,10},{10,8},{12,14},{14,12},{16,18},{18,... | collective-permute-start | bytes 614408 | tf_op jit(solution)/shard_map/ppermute | solution.py:98
  75.7 15.3 %collective-permute-start.18 = (f32[4,88,128]{2,1,0:T(8,128)S(1)}, f32[4,88,128]{2,1,0:T(8,128)S(1)}, u32[]{:S(2)}, u32[]{:S(2)}) collective-permute-start(f32[4,88,128]{2,1,0:T(8,128)S(1)} %pad_maximum_fusion.10), channel_id=1, source_target_pairs={{0,16},{2,18},{4,20},{6,22},{8,24},{10,26},{12,28},{14,30},{16,0},... | collective-permute-start | bytes 540680 | tf_op jit(solution)/shard_map/ppermute | solution.py:93
  85.9 4.0 %collective-permute-start.19 = (f32[4,16,128]{2,1,0:T(8,128)S(1)}, f32[4,16,128]{2,1,0:T(8,128)S(1)}, u32[]{:S(2)}, u32[]{:S(2)}) collective-permute-start(f32[4,16,128]{2,1,0:T(8,128)S(1)} %get-tuple-element.38), channel_id=1, source_target_pairs={{0,1},{1,0},{2,3},{3,2},{4,5},{5,4},{6,7},{7,6},{8,9},{9,8},{10,11... | collective-permute-start | bytes 98312 | tf_op jit(solution)/shard_map/ppermute | solution.py:639

commit v5 on v4

--- a/solution.py
+++ b/solution.py
@@ -248,30 +248,33 @@
     sends = []
     corners = [jnp.zeros((depth, LANES), f32)]
     if layout:
-        lower_ref, extras_ref, upper_ref, halves_ref, send_sems = scratch[9:]
-        halves_ref[...] = jnp.zeros_like(halves_ref)
-        extras_ref[...] = jnp.zeros_like(extras_ref)
+        blocks_ref, send_sems = scratch[9:]
         early, late = layout.divide(outs)
         sizes, base = layout.share(depth), layout.base(depth)
-        full = base + upper_ref.shape[0] // depth
-        buffers = ((lower_ref, 0), (extras_ref, None), (upper_ref, base), (halves_ref, None))
+        total, lower = sum(sizes), sizes[0]
+        full = base + sizes[2] // depth * len(layout.blocks)
         for k, s in layout.blocks:
-            place, target, done = layout.place(k, s), layout.sent(k, s, early, late), 0
-            for (ref, begin), size in zip(buffers, sizes):
-                source = ref.at[pl.ds(pl.multiple_of(place * size, 8), size)]
-                if size:
-                    target_part = target.at[pl.ds(done, size)]
-                    copy = pltpu.make_async_copy(source, target_part, send_sems.at[len(sends)])
-                    sends.append((place, begin, size // depth, copy))
-                done += size
-
-    def put_half(ref, at, value, half=0):
-        ref[at * depth // 2 : (at + 1) * depth // 2] = pack(value, half)
+            place, target = layout.place(k, s), layout.sent(k, s, early, late)
+            for begin, end in ((0, lower), (lower, total)):
+                source = pl.ds(pl.multiple_of(place * total + begin, 8), end - begin)
+                copy = pltpu.make_async_copy(
+                    blocks_ref.at[source], target.at[begin:end], send_sems.at[len(sends)]
+                )
+                sends.append((place, copy))
+
+    def put_block(kind, at, value):
+        size = value.shape[0]
+        count = sizes[kind] // size
+        begin = at // count * total + sum(sizes[:kind]) + at % count * size
+        blocks_ref[begin : begin + size] = value
+
+    def put_half(kind, at, value, half=0):
+        put_block(kind, at, pack(value, half))
 
     def put_extra(row, value):
         if layout:
-            put_half(extras_ref, 2 * row, value)
-            put_half(extras_ref, 2 * row + 1, value, 1)
+            put_half(1, 2 * row, value)
+            put_half(1, 2 * row + 1, value, 1)
         else:
             outs[1][row] = value
 
@@ -283,19 +286,19 @@
         if not layout:
             outs[0][row] = value
         elif row < base:
-            lower_ref[row * depth : (row + 1) * depth] = value
+            put_block(0, row, value)
         elif row < full:
-            upper_ref[(row - base) * depth : (row - base + 1) * depth] = value
+            put_block(2, row - base, value)
         else:
-            put_half(halves_ref, 2 * (row - full), value)
-            put_half(halves_ref, 2 * (row - full) + 1, value, 1)
+            put_half(3, 2 * (row - full), value)
+            put_half(3, 2 * (row - full) + 1, value, 1)
 
     def put_end(c, value):
         put_extra(ENDS + c, value)
 
     def put_face(c, value):
         if layout:
-            put_half(extras_ref, 2 * FACES + c, value)
+            put_half(1, 2 * FACES + c, value)
             corners[0] = jnp.where(lane_index(depth) == c, roll(value, c - FACE), corners[0])
         else:
             outs[1][FACES + c] = value
@@ -312,24 +315,24 @@
         puts = [functools.partial(store, c) for store in (put_row, put_end, put_face)]
         first, second = vel_ref.at[c], vel_ref.at[(c + 1) % 3]
         component(terms, first, second, select, geo, left, parts, *puts)
-        for place, begin, count, copy in sends:
-            if begin is None:
-                continue
-            blocks = len(layout.blocks)
-            before, ready = (
-                max(0, min(blocks, (rows - begin) // count)) for rows in (c * INNER, (c + 1) * INNER)
-            )
-            if before < ready == blocks and before == 0:
-                copy.start()
-            elif before < ready:
+        for place, copy in sends[::2]:
+            count = lower // depth
+            before, ready = (min(len(layout.blocks), k * INNER // count) for k in (c, c + 1))
+            if before < ready:
                 pl.when(jnp.logical_and(place >= before, place < ready))(copy.start)
     if layout:
-        put_half(extras_ref, CORNERS, corners[0])
-    for _, begin, _, copy in sends:
-        if begin is None:
+        put_half(1, CORNERS, corners[0])
+        blank = jnp.zeros((depth, LANES), f32)
+        for at in range(HALVES, sizes[1] * 2 // depth * len(layout.blocks)):
+            put_half(1, at, blank)
+        for at in range(3 * INNER - base, full - base):
+            put_block(2, at, blank)
+        for at in range(2 * max(3 * INNER - full, 0), sizes[3] * 2 // depth * len(layout.blocks)):
+            put_half(3, at, blank)
+        for _, copy in sends[1::2]:
             copy.start()
-    for *_, copy in sends:
-        copy.wait()
+        for _, copy in sends:
+            copy.wait()
 
 
 def elements(name, terms, layout, args):
@@ -347,8 +350,8 @@
     if layout:
         count = len(layout.blocks)
         sizes = layout.share(depth)
-        scratch += [pltpu.VMEM((count * max(size, 8), LANES), f32) for size in sizes]
-        scratch.append(pltpu.SemaphoreType.DMA((4 * count,)))
+        scratch.append(pltpu.VMEM((count * sum(sizes), LANES), f32))
+        scratch.append(pltpu.SemaphoreType.DMA((2 * count,)))
         shapes = layout.shapes((sum(sizes), LANES))
         specs = [anywhere] * len(shapes)
     else:
@@ -488,11 +491,8 @@
     nodes_ref[pl.ds(at * depth, depth), :] = jnp.concatenate([high, low], axis=1)
 
 
-def faces_kernel(
-    t_ref, before_ref, after_ref, slots_ref, _, out_ref, nodes_ref, slots_out_ref, sems
-):
+def faces_nodes(t_ref, before_ref, after_ref, select, out_ref, nodes_ref, slots_out_ref, sems):
     depth, lanes = t_ref.shape[1:]
-    select = pair_selector(slots_ref)
     lane = lane_index(depth)
     across = lane % EY
     count = SIDE + 1
@@ -525,8 +525,7 @@
             )
             copy.start()
             copies.append(copy)
-    for copy in copies:
-        copy.wait()
+    return copies
 
 
 def middle_groups(layout, depth, upper):
@@ -541,9 +540,8 @@
     return groups
 
 
-def middle_kernel(layout, upper, u_ref, t_ref, slots_ref, *refs):
-    values = refs[: -7 if upper else -6]
-    out_ref, nodes_ref, slots_out_ref, sems, rows_ref, halves_ref = refs[-6:]
+def middle_nodes(layout, upper, u_ref, t_ref, select, values, out_ref, scratch):
+    nodes_ref, slots_out_ref, sems, rows_ref, halves_ref = scratch
     depth, lanes = u_ref.shape[1:]
     sizes = layout.share(depth)
     full, half = sizes[2:] if upper else (sizes[0], 0)
@@ -558,7 +556,6 @@
         if half:
             at = pl.ds(pl.multiple_of(place * half, 8), half)
             halves_ref[at] = ref[begin + full : begin + full + half]
-    select = pair_selector(slots_ref)
     across = lane_index(depth) % EY
     line = SIDE + 1
     copies, done = [], 0
@@ -589,26 +586,38 @@
         copy.start()
         copies.append(copy)
         done += count
+    return copies
+
+
+def lower_kernel(layout, u_ref, t_ref, slots_ref, *refs):
+    values, out_ref, scratch = refs[:-6], refs[-6], refs[-5:]
+    select = pair_selector(slots_ref)
+    for copy in middle_nodes(layout, False, u_ref, t_ref, select, values, out_ref, scratch):
+        copy.wait()
+
+
+def upper_kernel(layout, u_ref, t_ref, slots_ref, before_ref, after_ref, *refs):
+    values, out_ref, scratch = refs[:-10], refs[-9], refs[-8:]
+    select = pair_selector(slots_ref)
+    copies = middle_nodes(layout, True, u_ref, t_ref, select, values, out_ref, scratch[:5])
+    copies += faces_nodes(t_ref, before_ref, after_ref, select, out_ref, *scratch[5:])
     for copy in copies:
         copy.wait()
 
 
-def middle(layout, upper, args, values, result):
-    depth = args[0].shape[1]
+def middle_scratch(layout, depth, upper):
     sizes = layout.share(depth)
     groups = middle_groups(layout, depth, upper)
     count = (SIDE + 1) * sum(group[2] for group in groups)
     blocks = len(layout.blocks)
     full, half = sizes[2:] if upper else (sizes[0], 0)
-    scratch = [
+    return [
         pltpu.VMEM((count * depth, 2 * LANES), bf16),
         pltpu.VMEM((count, depth, LANES), f32),
         pltpu.SemaphoreType.DMA((len(groups),)),
         pltpu.VMEM((blocks * full // depth, depth, LANES), f32),
         pltpu.VMEM((blocks * max(half, 8), LANES), f32),
     ]
-    kernel = functools.partial(middle_kernel, layout, upper)
-    return expand(kernel, "upper" if upper else "lower", scratch, (*args, *values), result)
 
 
 def expand(kernel, name, scratch, args, result=None):
@@ -656,15 +665,18 @@
     ended = layout.end(early)
     total, faces = totals(layout, u_extras, late + lower + ended)
     before, after = beside(faces)
-    scratch = [
+    scratch = middle_scratch(layout, depth, False)
+    args = (u, total, slot_of_cell)
+    kernel = functools.partial(lower_kernel, layout)
+    result = expand(kernel, "lower", scratch, (*args, *late, *lower, *ended))
+    scratch = middle_scratch(layout, depth, True) + [
         pltpu.VMEM((2 * (SIDE + 1) * depth, 2 * LANES), bf16),
         pltpu.VMEM((3, 2, SIDE + 1, depth, LANES), f32),
         pltpu.SemaphoreType.DMA((3, 2)),
     ]
-    args = (u, total, slot_of_cell)
-    result = middle(layout, False, args, late + lower + ended, None)
-    result = expand(faces_kernel, "faces", scratch, (total, before, after, slot_of_cell), result)
-    result = middle(layout, True, args, late + upper + ended, result)
+    kernel = functools.partial(upper_kernel, layout)
+    args += (before, after, *late, *upper, *ended)
+    result = expand(kernel, "upper", scratch, args, result)
     return result.transpose(0, 2, 1, 3)
 
 

time: 92.6 us -> 91.1 us (0.984)
  starting transfers between devices: 22 us -> 14 us
  waiting for transfers between devices: 53.4 us -> 61.1 us
  Pallas kernels: 15.4 us -> 14.1 us
    ppermute x7, waiting for transfers between devices: 22.6 us -> 30.7 us  [onward(): return lax.ppermute(value, 'modes', steps)]
    ppermute x12, starting transfers between devices: 15.8 us -> 7.86 us  [across(): lax.ppermute(value, 'modes', pairs(s))]
    pallas_call x3 -> x2, Pallas kernels: 3.85 us -> 2.88 us  [expand(): pl.pallas_call(kernel, in_specs=in_specs, out_specs=pl.BlockSpec(memory_s...]
  transfers between devices with their start and end apart: 20 -> 20, of which waited for: 12 -> 12; matrix products, arithmetic and copies ran while one was open for 1% -> 1% of each run, Pallas kernels for 8% -> 7%
where the time goes in v5:
time: 91.1 us; the launch traced here: 90.9 us
  waiting for transfers between devices  61.1 us (67%)
  Pallas kernels  14.1 us (15%)
  starting transfers between devices  14 us (15%)
  local copies, waits for them, and re-layouts  1.12 us (1%)
    ppermute x7, waiting for transfers between devices, onward(): return lax.ppermute(value, 'modes', steps)  30.7 us
    ppermute x12, waiting for transfers between devices, across(): lax.ppermute(value, 'modes', pairs(s))  29.3 us
    pallas_call x2, Pallas kernels, elements(): pl.pallas_call(functools.partial(element_kernel, terms, layout, len(shape...  9.79 us
    ppermute x12, starting transfers between devices, across(): lax.ppermute(value, 'modes', pairs(s))  7.86 us
    ppermute x7, starting transfers between devices, onward(): return lax.ppermute(value, 'modes', steps)  4.62 us
    pallas_call x2, Pallas kernels, expand(): pl.pallas_call(kernel, in_specs=in_specs, out_specs=pl.BlockSpec(memory_s...  2.88 us
  transfers between devices with their start and end apart: 20, of which 12 were waited for; matrix products, arithmetic and copies ran while one was open for 1% of the time, Pallas kernels for 7%

profile of v5, /device:TPU:16, one launch (start us, length us, event | category | flops | bytes accessed | tf_op | source)
XLA Modules:
  0.0 90.9 jit_solution(9213772153961046535)
XLA Ops:
  0.0 5.4 %mass.1 = (f32[4,200,128]{2,1,0:T(8,128)}, f32[4,200,128]{2,1,0:T(8,128)}, f32[2,200,128]{2,1,0:T(8,128)}, f32[2,200,128]{2,1,0:T(8,128)}, f32[2,200,128]{2,1,0:T(8,128)}, /*index=5*/f32[2,200,128]{2,1,0:T(8,128)}) custom-call(f32[3,81,16,128]{3,2,1,0:T(8,128)} %bitcast.3, s32[1,128]{1,0:T(1,128)} %slots_ref.3, f32[81,4,81]{2,1,0:T(4,128)} %bitcast.5, ...), custom_call_target="tpu_custom_call" | custom-call | flops 339738624 | bytes 3686400 | tf_op jit(solution)/shard_map/mass/pallas_call | solution.py:360
  5.4 1.6 %collective-permute-start.4 = (f32[4,200,128]{2,1,0:T(8,128)}, f32[4,200,128]{2,1,0:T(8,128)S(1)}, u32[]{:S(2)}, u32[]{:S(2)}) collective-permute-start(f32[4,200,128]{2,1,0:T(8,128)} %get-tuple-element.28), channel_id=1, source_target_pairs={{0,8},{2,10},{4,12},{6,14},{8,16},{10,18},{12,20},{14,22},{16,24},... | collective-permute-start | bytes 1228808 | tf_op jit(solution)/shard_map/ppermute | solution.py:93
  7.0 1.5 %collective-permute-start.1 = (f32[2,200,128]{2,1,0:T(8,128)}, f32[2,200,128]{2,1,0:T(8,128)S(1)}, u32[]{:S(2)}, u32[]{:S(2)}) collective-permute-start(f32[2,200,128]{2,1,0:T(8,128)} %get-tuple-element.26), channel_id=1, source_target_pairs={{0,4},{2,6},{4,0},{6,2},{8,12},{10,14},{12,8},{14,10},{16,20},{18,... | collective-permute-start | bytes 614408 | tf_op jit(solution)/shard_map/ppermute | solution.py:98
  8.6 0.3 collective-permute-start.2
  8.9 0.5 collective-permute-start.5
  9.3 0.9 slice.84
  10.2 0.0 collective-permute-done.refs_1_
  10.3 4.9 %collective-permute-done.1.refs_2_ = f32[2,200,128]{2,1,0:T(8,128)S(1)} collective-permute-done((f32[2,200,128]{2,1,0:T(8,128)}, f32[2,200,128]{2,1,0:T(8,128)S(1)}, u32[]{:S(2)}, u32[]{:S(2)}) %collective-permute-start.1) | collective-permute-done | bytes 204832 | tf_op jit(solution)/shard_map/ppermute | solution.py:98
  15.1 0.0 copy-start
  15.1 0.0 copy-start.3
  15.1 0.0 copy-start.4
  15.2 0.0 copy-start.5
  15.2 3.6 %collective-permute-done.2.refs_3_ = f32[2,200,128]{2,1,0:T(8,128)S(1)} collective-permute-done((f32[2,200,128]{2,1,0:T(8,128)}, f32[2,200,128]{2,1,0:T(8,128)S(1)}, u32[]{:S(2)}, u32[]{:S(2)}) %collective-permute-start.2) | collective-permute-done | bytes 204832 | tf_op jit(solution)/shard_map/ppermute | solution.py:98
  18.8 0.4 collective-permute-start.3
  19.2 15.2 %collective-permute-done.4 = f32[4,200,128]{2,1,0:T(8,128)S(1)} collective-permute-done((f32[4,200,128]{2,1,0:T(8,128)}, f32[4,200,128]{2,1,0:T(8,128)S(1)}, u32[]{:S(2)}, u32[]{:S(2)}) %collective-permute-start.4) | collective-permute-done | bytes 409632 | tf_op jit(solution)/shard_map/ppermute | solution.py:93
  34.5 0.1 collective-permute-start.6
  34.6 1.6 %collective-permute-start.7 = (f32[2,200,128]{2,1,0:T(8,128)S(1)}, f32[2,200,128]{2,1,0:T(8,128)S(1)}, u32[]{:S(2)}, u32[]{:S(2)}) collective-permute-start(f32[2,200,128]{2,1,0:T(8,128)S(1)} %pad_maximum_fusion.4), channel_id=1, source_target_pairs={{0,4},{2,6},{4,0},{6,2},{8,12},{10,14},{12,8},{14,10},{16,20},{18,... | collective-permute-start | bytes 614408 | tf_op jit(solution)/shard_map/ppermute | solution.py:98
  36.2 0.0 copy-start.1
  36.3 0.4 collective-permute-start.8
  36.7 4.4 %stiff.1 = (f32[168,16,128]{2,1,0:T(8,128)S(1)}, f32[30,16,128]{2,1,0:T(8,128)S(1)}) custom-call(f32[3,81,16,128]{3,2,1,0:T(8,128)S(1)} %bitcast.4, s32[1,128]{1,0:T(1,128)S(1)} %copy-done.4, f32[81,4,81]{2,1,0:T(4,128)S(1)} %bitcast.6, f32[4,128]{1,0:T(4,128)S(1)} %copy-done.5), custom_call_target="tpu_custom_call" | custom-call | flops 1019215872 | bytes 3686400 | tf_op jit(solution)/shard_map/stiff/pallas_call | solution.py:360
  41.1 0.9 %collective-permute-done.3.refs_4_ = f32[4,200,128]{2,1,0:T(8,128)S(1)} collective-permute-done((f32[4,200,128]{2,1,0:T(8,128)S(1)}, f32[4,200,128]{2,1,0:T(8,128)S(1)}, u32[]{:S(2)}, u32[]{:S(2)}) %collective-permute-start.3) | collective-permute-done | bytes 409632 | tf_op jit(solution)/shard_map/ppermute | solution.py:93
  42.0 0.0 collective-permute-done.6.refs_6_
  42.0 0.5 collective-permute-done.7.refs_7_
  42.6 3.6 %collective-permute-done.8.refs_8_ = f32[2,200,128]{2,1,0:T(8,128)S(1)} collective-permute-done((f32[2,200,128]{2,1,0:T(8,128)S(1)}, f32[2,200,128]{2,1,0:T(8,128)S(1)}, u32[]{:S(2)}, u32[]{:S(2)}) %collective-permute-start.8) | collective-permute-done | bytes 204832 | tf_op jit(solution)/shard_map/ppermute | solution.py:98
  46.2 1.1 %spanwise.1 = (f32[4,200,128]{2,1,0:T(8,128)S(1)}, f32[4,200,128]{2,1,0:T(8,128)S(1)}, f32[2,200,128]{2,1,0:T(8,128)S(1)}, f32[2,200,128]{2,1,0:T(8,128)S(1)}, f...) custom-call(f32[2,200,128]{2,1,0:T(8,128)S(1)} %copy-done.2, f32[2,200,128]{2,1,0:T(8,128)S(1)} %collective-permute-done.refs_1_, ...), custom_call_target="tpu_custom_call" | custom-call | flops 629145600 | bytes 3276800 | tf_op jit(solution)/shard_map/spanwise/pallas_call | solution.py:415
  47.2 0.1 collective-permute-start.13
  47.3 0.3 collective-permute-start.9
  47.6 1.5 %collective-permute-start.10 = (f32[2,200,128]{2,1,0:T(8,128)S(1)}, f32[2,200,128]{2,1,0:T(8,128)S(1)}, u32[]{:S(2)}, u32[]{:S(2)}) collective-permute-start(f32[2,200,128]{2,1,0:T(8,128)S(1)} %get-tuple-element.33), channel_id=1, source_target_pairs={{0,4},{2,6},{4,0},{6,2},{8,12},{10,14},{12,8},{14,10},{16,20},{18,... | collective-permute-start | bytes 614408 | tf_op jit(solution)/shard_map/ppermute | solution.py:98
  49.1 0.1 collective-permute-start.11
  49.2 1.9 %collective-permute-start.14 = (f32[4,200,128]{2,1,0:T(8,128)S(1)}, f32[4,200,128]{2,1,0:T(8,128)S(1)}, u32[]{:S(2)}, u32[]{:S(2)}) collective-permute-start(f32[4,200,128]{2,1,0:T(8,128)S(1)} %get-tuple-element.36), channel_id=1, source_target_pairs={{0,24},{2,26},{4,28},{6,30},{8,0},{10,2},{12,4},{14,6},{16,8},{18,... | collective-permute-start | bytes 1228808 | tf_op jit(solution)/shard_map/ppermute | solution.py:93
  51.2 0.0 collective-permute-done.9.refs_1_
  51.2 4.3 %collective-permute-done.10.refs_2_ = f32[2,200,128]{2,1,0:T(8,128)S(1)} collective-permute-done((f32[2,200,128]{2,1,0:T(8,128)S(1)}, f32[2,200,128]{2,1,0:T(8,128)S(1)}, u32[]{:S(2)}, u32[]{:S(2)}) %collective-permute-start.10) | collective-permute-done | bytes 204832 | tf_op jit(solution)/shard_map/ppermute | solution.py:98
  55.5 3.1 %collective-permute-done.11.refs_3_ = f32[2,200,128]{2,1,0:T(8,128)S(1)} collective-permute-done((f32[2,200,128]{2,1,0:T(8,128)S(1)}, f32[2,200,128]{2,1,0:T(8,128)S(1)}, u32[]{:S(2)}, u32[]{:S(2)}) %collective-permute-start.11) | collective-permute-done | bytes 204832 | tf_op jit(solution)/shard_map/ppermute | solution.py:98
  58.6 0.1 collective-permute-start.12
  58.7 14.5 %collective-permute-done.13 = f32[4,200,128]{2,1,0:T(8,128)S(1)} collective-permute-done((f32[4,200,128]{2,1,0:T(8,128)S(1)}, f32[4,200,128]{2,1,0:T(8,128)S(1)}, u32[]{:S(2)}, u32[]{:S(2)}) %collective-permute-start.13) | collective-permute-done | bytes 409632 | tf_op jit(solution)/shard_map/ppermute | solution.py:93
  73.3 0.0 collective-permute-done.14
  73.4 0.1 collective-permute-start.15
  73.5 1.6 %collective-permute-start.16 = (f32[2,200,128]{2,1,0:T(8,128)S(1)}, f32[2,200,128]{2,1,0:T(8,128)S(1)}, u32[]{:S(2)}, u32[]{:S(2)}) collective-permute-start(f32[2,200,128]{2,1,0:T(8,128)S(1)} %pad_maximum_fusion.8), channel_id=1, source_target_pairs={{0,4},{2,6},{4,0},{6,2},{8,12},{10,14},{12,8},{14,10},{16,20},{18,... | collective-permute-start | bytes 614408 | tf_op jit(solution)/shard_map/ppermute | solution.py:98
  75.1 0.4 collective-permute-start.17
  75.5 0.1 collective-permute-start.19
  75.6 0.0 collective-permute-done.15.refs_6_
  75.6 5.8 %collective-permute-done.16.refs_7_ = f32[2,200,128]{2,1,0:T(8,128)S(1)} collective-permute-done((f32[2,200,128]{2,1,0:T(8,128)S(1)}, f32[2,200,128]{2,1,0:T(8,128)S(1)}, u32[]{:S(2)}, u32[]{:S(2)}) %collective-permute-start.16) | collective-permute-done | bytes 204832 | tf_op jit(solution)/shard_map/ppermute | solution.py:98
  81.4 3.6 %collective-permute-done.17.refs_8_ = f32[2,200,128]{2,1,0:T(8,128)S(1)} collective-permute-done((f32[2,200,128]{2,1,0:T(8,128)S(1)}, f32[2,200,128]{2,1,0:T(8,128)S(1)}, u32[]{:S(2)}, u32[]{:S(2)}) %collective-permute-start.17) | collective-permute-done | bytes 204832 | tf_op jit(solution)/shard_map/ppermute | solution.py:98
  85.0 0.4 totals.1
  85.4 1.6 %collective-permute-start.18 = (f32[4,16,128]{2,1,0:T(8,128)S(1)}, f32[4,16,128]{2,1,0:T(8,128)S(1)}, u32[]{:S(2)}, u32[]{:S(2)}) collective-permute-start(f32[4,16,128]{2,1,0:T(8,128)S(1)} %get-tuple-element.38), channel_id=1, source_target_pairs={{0,1},{1,0},{2,3},{3,2},{4,5},{5,4},{6,7},{7,6},{8,9},{9,8},{10,11... | collective-permute-start | bytes 98312 | tf_op jit(solution)/shard_map/ppermute | solution.py:648
  86.9 1.3 %lower.1.refs_9_ = f32[3,81,16,128]{3,2,1,0:T(8,128)} custom-call(f32[168,16,128]{2,1,0:T(8,128)S(1)} %get-tuple-element.22.u_ref, f32[30,16,128]{2,1,0:T(8,128)S(1)} %get-tuple-element.37.t_ref, s32[1,128]{1,0:T(1,128)S(1)} %copy-done.4, f32[2,200,128]{2,1,0:T(8,128)S(1)} %get-tuple-element.31.refs_0_, f32[2,200,128]{2,1,0:T(8,128)S(1)} %collective-permute-done.9.refs_1_, ...), custom_call_target="tpu_custom_call" | custom-call | tf_op jit(solution)/shard_map/lower/pallas_call | solution.py:631
  88.3 1.1 %collective-permute-done.18.before_ref.after_ref = f32[4,16,128]{2,1,0:T(8,128)S(1)} collective-permute-done((f32[4,16,128]{2,1,0:T(8,128)S(1)}, f32[4,16,128]{2,1,0:T(8,128)S(1)}, u32[]{:S(2)}, u32[]{:S(2)}) %collective-permute-start.18) | collective-permute-done | bytes 32800 | tf_op jit(solution)/shard_map/ppermute | solution.py:648
  89.4 1.6 %upper.1 = f32[3,81,16,128]{3,2,1,0:T(8,128)} custom-call(f32[168,16,128]{2,1,0:T(8,128)S(1)} %get-tuple-element.22.u_ref, f32[30,16,128]{2,1,0:T(8,128)S(1)} %get-tuple-element.37.t_ref, s32[1,128]{1,0:T(1,128)S(1)} %copy-done.4, f32[4,16,128]{2,1,0:T(8,128)S(1)} %collective-permute-done.18.before_ref.after_ref, ...), custom_call_target="tpu_custom_call", output_to_operand_aliasing={{}: (14, {})} | custom-call | tf_op jit(solution)/shard_map/upper/pallas_call | solution.py:631
  (37 shorter events, 0.5 us)
Async XLA Ops:
  5.4 29.0 %collective-permute-start.4 = (f32[4,200,128]{2,1,0:T(8,128)}, f32[4,200,128]{2,1,0:T(8,128)S(1)}, u32[]{:S(2)}, u32[]{:S(2)}) collective-permute-start(f32[4,200,128]{2,1,0:T(8,128)} %get-tuple-element.28), channel_id=1, source_target_pairs={{0,8},{2,10},{4,12},{6,14},{8,16},{10,18},{12,20},{14,22},{16,24},... | collective-permute-start | bytes 1228808 | tf_op jit(solution)/shard_map/ppermute | solution.py:93
  7.0 3.2 %collective-permute-start = (f32[2,200,128]{2,1,0:T(8,128)}, f32[2,200,128]{2,1,0:T(8,128)S(1)}, u32[]{:S(2)}, u32[]{:S(2)}) collective-permute-start(f32[2,200,128]{2,1,0:T(8,128)} %get-tuple-element.25), channel_id=1, source_target_pairs={{0,2},{2,0},{4,6},{6,4},{8,10},{10,8},{12,14},{14,12},{16,18},{18,... | collective-permute-start | bytes 614408 | tf_op jit(solution)/shard_map/ppermute | solution.py:98
  7.0 8.1 %collective-permute-start.1 = (f32[2,200,128]{2,1,0:T(8,128)}, f32[2,200,128]{2,1,0:T(8,128)S(1)}, u32[]{:S(2)}, u32[]{:S(2)}) collective-permute-start(f32[2,200,128]{2,1,0:T(8,128)} %get-tuple-element.26), channel_id=1, source_target_pairs={{0,4},{2,6},{4,0},{6,2},{8,12},{10,14},{12,8},{14,10},{16,20},{18,... | collective-permute-start | bytes 614408 | tf_op jit(solution)/shard_map/ppermute | solution.py:98
  8.6 10.2 %collective-permute-start.2 = (f32[2,200,128]{2,1,0:T(8,128)}, f32[2,200,128]{2,1,0:T(8,128)S(1)}, u32[]{:S(2)}, u32[]{:S(2)}) collective-permute-start(f32[2,200,128]{2,1,0:T(8,128)} %get-tuple-element.27), channel_id=1, source_target_pairs={{0,6},{2,4},{4,2},{6,0},{8,14},{10,12},{12,10},{14,8},{16,22},{18,... | collective-permute-start | bytes 614408 | tf_op jit(solution)/shard_map/ppermute | solution.py:98
  8.9 25.6 %collective-permute-start.5 = (f32[4,200,128]{2,1,0:T(8,128)}, f32[4,200,128]{2,1,0:T(8,128)S(1)}, u32[]{:S(2)}, u32[]{:S(2)}) collective-permute-start(f32[4,200,128]{2,1,0:T(8,128)} %get-tuple-element.29), channel_id=1, source_target_pairs={{0,24},{2,26},{4,28},{6,30},{8,0},{10,2},{12,4},{14,6},{16,8},{18,... | collective-permute-start | bytes 1228808 | tf_op jit(solution)/shard_map/ppermute | solution.py:93
  15.1 21.5 %copy-start = (f32[3,16,81,128]{3,1,2,0:T(8,128)S(1)}, f32[3,16,81,128]{3,1,2,0:T(8,128)}, u32[]{:S(2)}) copy-start(f32[3,16,81,128]{3,1,2,0:T(8,128)} %param.5) | copy-start | bytes 5971972
  15.1 21.5 %copy-start.3 = (f32[4,81,81]{2,0,1:T(4,128)S(1)}, f32[4,81,81]{2,0,1:T(4,128)}, u32[]{:S(2)}) copy-start(f32[4,81,81]{2,0,1:T(4,128)} %param.7) | copy-start | bytes 314932
  15.1 21.5 %copy-start.4 = (s32[1,128]{1,0:T(1,128)S(1)}, s32[1,128]{1,0:T(1,128)}, u32[]{:S(2)}) copy-start(s32[1,128]{1,0:T(1,128)} %slots_ref.3) | copy-start | bytes 1540
  15.2 21.5 %copy-start.5 = (f32[4,128]{1,0:T(4,128)S(1)}, f32[4,128]{1,0:T(4,128)}, u32[]{:S(2)}) copy-start(f32[4,128]{1,0:T(4,128)} %refs_3_.3) | copy-start | bytes 6148
  18.8 23.2 %collective-permute-start.3 = (f32[4,200,128]{2,1,0:T(8,128)S(1)}, f32[4,200,128]{2,1,0:T(8,128)S(1)}, u32[]{:S(2)}, u32[]{:S(2)}) collective-permute-start(f32[4,200,128]{2,1,0:T(8,128)S(1)} %pad_maximum_fusion), channel_id=1, source_target_pairs={{0,16},{2,18},{4,20},{6,22},{8,24},{10,26},{12,28},{14,30},{16,0},... | collective-permute-start | bytes 1228808 | tf_op jit(solution)/shard_map/ppermute | solution.py:93
  34.5 7.5 %collective-permute-start.6 = (f32[2,200,128]{2,1,0:T(8,128)S(1)}, f32[2,200,128]{2,1,0:T(8,128)S(1)}, u32[]{:S(2)}, u32[]{:S(2)}) collective-permute-start(f32[2,200,128]{2,1,0:T(8,128)S(1)} %pad_maximum_fusion.3), channel_id=1, source_target_pairs={{0,2},{2,0},{4,6},{6,4},{8,10},{10,8},{12,14},{14,12},{16,18},{18,... | collective-permute-start | bytes 614408 | tf_op jit(solution)/shard_map/ppermute | solution.py:98
  34.6 7.9 %collective-permute-start.7 = (f32[2,200,128]{2,1,0:T(8,128)S(1)}, f32[2,200,128]{2,1,0:T(8,128)S(1)}, u32[]{:S(2)}, u32[]{:S(2)}) collective-permute-start(f32[2,200,128]{2,1,0:T(8,128)S(1)} %pad_maximum_fusion.4), channel_id=1, source_target_pairs={{0,4},{2,6},{4,0},{6,2},{8,12},{10,14},{12,8},{14,10},{16,20},{18,... | collective-permute-start | bytes 614408 | tf_op jit(solution)/shard_map/ppermute | solution.py:98
  36.2 9.9 %copy-start.1 = (bf16[4,512,256]{2,1,0:T(8,128)(2,1)S(1)}, bf16[4,512,256]{2,1,0:T(8,128)(2,1)}, u32[]{:S(2)}) copy-start(bf16[4,512,256]{2,1,0:T(8,128)(2,1)} %constant.2.clone.refs_9_) | copy-start | bytes 3145732
  36.2 9.9 %copy-start.2 = (f32[2,200,128]{2,1,0:T(8,128)S(1)}, f32[2,200,128]{2,1,0:T(8,128)}, u32[]{:S(2)}) copy-start(f32[2,200,128]{2,1,0:T(8,128)} %get-tuple-element.24.refs_0_) | copy-start | bytes 614404
  36.3 9.9 %collective-permute-start.8 = (f32[2,200,128]{2,1,0:T(8,128)S(1)}, f32[2,200,128]{2,1,0:T(8,128)S(1)}, u32[]{:S(2)}, u32[]{:S(2)}) collective-permute-start(f32[2,200,128]{2,1,0:T(8,128)S(1)} %pad_maximum_fusion.5), channel_id=1, source_target_pairs={{0,6},{2,4},{4,2},{6,0},{8,14},{10,12},{12,10},{14,8},{16,22},{18,... | collective-permute-start | bytes 614408 | tf_op jit(solution)/shard_map/ppermute | solution.py:98
  47.2 26.0 %collective-permute-start.13 = (f32[4,200,128]{2,1,0:T(8,128)S(1)}, f32[4,200,128]{2,1,0:T(8,128)S(1)}, u32[]{:S(2)}, u32[]{:S(2)}) collective-permute-start(f32[4,200,128]{2,1,0:T(8,128)S(1)} %get-tuple-element.35), channel_id=1, source_target_pairs={{0,8},{2,10},{4,12},{6,14},{8,16},{10,18},{12,20},{14,22},{16,24},... | collective-permute-start | bytes 1228808 | tf_op jit(solution)/shard_map/ppermute | solution.py:93
  47.3 3.9 %collective-permute-start.9 = (f32[2,200,128]{2,1,0:T(8,128)S(1)}, f32[2,200,128]{2,1,0:T(8,128)S(1)}, u32[]{:S(2)}, u32[]{:S(2)}) collective-permute-start(f32[2,200,128]{2,1,0:T(8,128)S(1)} %get-tuple-element.32), channel_id=1, source_target_pairs={{0,2},{2,0},{4,6},{6,4},{8,10},{10,8},{12,14},{14,12},{16,18},{18,... | collective-permute-start | bytes 614408 | tf_op jit(solution)/shard_map/ppermute | solution.py:98
  47.6 7.9 %collective-permute-start.10 = (f32[2,200,128]{2,1,0:T(8,128)S(1)}, f32[2,200,128]{2,1,0:T(8,128)S(1)}, u32[]{:S(2)}, u32[]{:S(2)}) collective-permute-start(f32[2,200,128]{2,1,0:T(8,128)S(1)} %get-tuple-element.33), channel_id=1, source_target_pairs={{0,4},{2,6},{4,0},{6,2},{8,12},{10,14},{12,8},{14,10},{16,20},{18,... | collective-permute-start | bytes 614408 | tf_op jit(solution)/shard_map/ppermute | solution.py:98
  49.1 9.5 %collective-permute-start.11 = (f32[2,200,128]{2,1,0:T(8,128)S(1)}, f32[2,200,128]{2,1,0:T(8,128)S(1)}, u32[]{:S(2)}, u32[]{:S(2)}) collective-permute-start(f32[2,200,128]{2,1,0:T(8,128)S(1)} %get-tuple-element.34), channel_id=1, source_target_pairs={{0,6},{2,4},{4,2},{6,0},{8,14},{10,12},{12,10},{14,8},{16,22},{18,... | collective-permute-start | bytes 614408 | tf_op jit(solution)/shard_map/ppermute | solution.py:98
  49.2 24.1 %collective-permute-start.14 = (f32[4,200,128]{2,1,0:T(8,128)S(1)}, f32[4,200,128]{2,1,0:T(8,128)S(1)}, u32[]{:S(2)}, u32[]{:S(2)}) collective-permute-start(f32[4,200,128]{2,1,0:T(8,128)S(1)} %get-tuple-element.36), channel_id=1, source_target_pairs={{0,24},{2,26},{4,28},{6,30},{8,0},{10,2},{12,4},{14,6},{16,8},{18,... | collective-permute-start | bytes 1228808 | tf_op jit(solution)/shard_map/ppermute | solution.py:93
  58.6 17.0 %collective-permute-start.12 = (f32[4,112,128]{2,1,0:T(8,128)S(1)}, f32[4,112,128]{2,1,0:T(8,128)S(1)}, u32[]{:S(2)}, u32[]{:S(2)}) collective-permute-start(f32[4,112,128]{2,1,0:T(8,128)S(1)} %pad_maximum_fusion.1), channel_id=1, source_target_pairs={{0,16},{2,18},{4,20},{6,22},{8,24},{10,26},{12,28},{14,30},{16,0},... | collective-permute-start | bytes 688136 | tf_op jit(solution)/shard_map/ppermute | solution.py:93
  73.4 2.2 %collective-permute-start.15 = (f32[2,200,128]{2,1,0:T(8,128)S(1)}, f32[2,200,128]{2,1,0:T(8,128)S(1)}, u32[]{:S(2)}, u32[]{:S(2)}) collective-permute-start(f32[2,200,128]{2,1,0:T(8,128)S(1)} %pad_maximum_fusion.7), channel_id=1, source_target_pairs={{0,2},{2,0},{4,6},{6,4},{8,10},{10,8},{12,14},{14,12},{16,18},{18,... | collective-permute-start | bytes 614408 | tf_op jit(solution)/shard_map/ppermute | solution.py:98
  73.5 7.9 %collective-permute-start.16 = (f32[2,200,128]{2,1,0:T(8,128)S(1)}, f32[2,200,128]{2,1,0:T(8,128)S(1)}, u32[]{:S(2)}, u32[]{:S(2)}) collective-permute-start(f32[2,200,128]{2,1,0:T(8,128)S(1)} %pad_maximum_fusion.8), channel_id=1, source_target_pairs={{0,4},{2,6},{4,0},{6,2},{8,12},{10,14},{12,8},{14,10},{16,20},{18,... | collective-permute-start | bytes 614408 | tf_op jit(solution)/shard_map/ppermute | solution.py:98
  75.1 9.9 %collective-permute-start.17 = (f32[2,200,128]{2,1,0:T(8,128)S(1)}, f32[2,200,128]{2,1,0:T(8,128)S(1)}, u32[]{:S(2)}, u32[]{:S(2)}) collective-permute-start(f32[2,200,128]{2,1,0:T(8,128)S(1)} %pad_maximum_fusion.9), channel_id=1, source_target_pairs={{0,6},{2,4},{4,2},{6,0},{8,14},{10,12},{12,10},{14,8},{16,22},{18,... | collective-permute-start | bytes 614408 | tf_op jit(solution)/shard_map/ppermute | solution.py:98
  75.5 12.8 %collective-permute-start.19 = (f32[4,88,128]{2,1,0:T(8,128)S(1)}, f32[4,88,128]{2,1,0:T(8,128)S(1)}, u32[]{:S(2)}, u32[]{:S(2)}) collective-permute-start(f32[4,88,128]{2,1,0:T(8,128)S(1)} %pad_maximum_fusion.10), channel_id=1, source_target_pairs={{0,16},{2,18},{4,20},{6,22},{8,24},{10,26},{12,28},{14,30},{16,0},... | collective-permute-start | bytes 540680 | tf_op jit(solution)/shard_map/ppermute | solution.py:93
  85.4 4.0 %collective-permute-start.18 = (f32[4,16,128]{2,1,0:T(8,128)S(1)}, f32[4,16,128]{2,1,0:T(8,128)S(1)}, u32[]{:S(2)}, u32[]{:S(2)}) collective-permute-start(f32[4,16,128]{2,1,0:T(8,128)S(1)} %get-tuple-element.38), channel_id=1, source_target_pairs={{0,1},{1,0},{2,3},{3,2},{4,5},{5,4},{6,7},{7,6},{8,9},{9,8},{10,11... | collective-permute-start | bytes 98312 | tf_op jit(solution)/shard_map/ppermute | solution.py:648

commit v6 on v5

--- a/solution.py
+++ b/solution.py
@@ -176,7 +176,7 @@
     depth = first.shape[1]
     values_ref[:NODES, :depth] = first[...] * second[...]
     values_ref[NODES, :depth] = values_ref[NODES - 1, :depth]
-    flat = values_ref.reshape(TALL * (depth + 8), LANES)
+    flat = values_ref.reshape((TALL + 1) * (depth + 8), LANES)
     for pair in range(0, depth, 2):
         right = []
         for p in (pair, pair + 1):
@@ -244,7 +244,7 @@
     for copy in copies:
         copy.start()
     depth = vel_ref.shape[2]
-    parts[0][NODES:] = jnp.zeros((TALL - NODES, depth + 8, LANES), f32)
+    parts[0][NODES:] = jnp.zeros((TALL + 1 - NODES, depth + 8, LANES), f32)
     sends = []
     corners = [jnp.zeros((depth, LANES), f32)]
     if layout:
@@ -340,9 +340,9 @@
     scratch = [
         *(pltpu.VMEM(a.shape, a.dtype) for a in args),
         pltpu.VMEM((len(terms), DEEP, 2 * LANES), bf16),
-        pltpu.VMEM((TALL, depth + 8, LANES), f32),
+        pltpu.VMEM((TALL + 1, depth + 8, LANES), f32),
         pltpu.VMEM((DEEP * depth, 2 * LANES), bf16),
-        pltpu.VMEM((PITCH * depth, LANES), f32),
+        pltpu.VMEM((PITCH * (depth + 1), LANES), f32),
         pltpu.SemaphoreType.DMA((6,)),
     ]
     anywhere, vmem = pl.BlockSpec(memory_space=pl.ANY), pl.BlockSpec(memory_space=pltpu.VMEM)

time: 91.1 us -> 91.1 us (level)
  no operation moved by 1% of the time
where the time goes in v6:
time: 91.1 us; the launch traced here: 90.9 us
  waiting for transfers between devices  61.1 us (67%)
  Pallas kernels  14.1 us (15%)
  starting transfers between devices  14 us (15%)
  local copies, waits for them, and re-layouts  1.12 us (1%)
    ppermute x7, waiting for transfers between devices, onward(): return lax.ppermute(value, 'modes', steps)  30.7 us
    ppermute x12, waiting for transfers between devices, across(): lax.ppermute(value, 'modes', pairs(s))  29.3 us
    pallas_call x2, Pallas kernels, elements(): pl.pallas_call(functools.partial(element_kernel, terms, layout, len(shape...  9.79 us
    ppermute x12, starting transfers between devices, across(): lax.ppermute(value, 'modes', pairs(s))  7.86 us
    ppermute x7, starting transfers between devices, onward(): return lax.ppermute(value, 'modes', steps)  4.62 us
    pallas_call x2, Pallas kernels, expand(): pl.pallas_call(kernel, in_specs=in_specs, out_specs=pl.BlockSpec(memory_s...  2.88 us
  transfers between devices with their start and end apart: 20, of which 12 were waited for; matrix products, arithmetic and copies ran while one was open for 1% of the time, Pallas kernels for 7%

profile of v6, /device:TPU:16, one launch (start us, length us, event | category | flops | bytes accessed | tf_op | source)
XLA Modules:
  0.0 90.9 jit_solution(10357045752729164601)
XLA Ops:
  0.0 5.4 %mass.1 = (f32[4,200,128]{2,1,0:T(8,128)}, f32[4,200,128]{2,1,0:T(8,128)}, f32[2,200,128]{2,1,0:T(8,128)}, f32[2,200,128]{2,1,0:T(8,128)}, f32[2,200,128]{2,1,0:T(8,128)}, /*index=5*/f32[2,200,128]{2,1,0:T(8,128)}) custom-call(f32[3,81,16,128]{3,2,1,0:T(8,128)} %bitcast.3, s32[1,128]{1,0:T(1,128)} %slots_ref.3, f32[81,4,81]{2,1,0:T(4,128)} %bitcast.5, ...), custom_call_target="tpu_custom_call" | custom-call | flops 339738624 | bytes 3686400 | tf_op jit(solution)/shard_map/mass/pallas_call | solution.py:360
  5.4 1.6 %collective-permute-start.4 = (f32[4,200,128]{2,1,0:T(8,128)}, f32[4,200,128]{2,1,0:T(8,128)S(1)}, u32[]{:S(2)}, u32[]{:S(2)}) collective-permute-start(f32[4,200,128]{2,1,0:T(8,128)} %get-tuple-element.28), channel_id=1, source_target_pairs={{0,8},{2,10},{4,12},{6,14},{8,16},{10,18},{12,20},{14,22},{16,24},... | collective-permute-start | bytes 1228808 | tf_op jit(solution)/shard_map/ppermute | solution.py:93
  7.0 0.0 collective-permute-start
  7.0 1.5 %collective-permute-start.1 = (f32[2,200,128]{2,1,0:T(8,128)}, f32[2,200,128]{2,1,0:T(8,128)S(1)}, u32[]{:S(2)}, u32[]{:S(2)}) collective-permute-start(f32[2,200,128]{2,1,0:T(8,128)} %get-tuple-element.26), channel_id=1, source_target_pairs={{0,4},{2,6},{4,0},{6,2},{8,12},{10,14},{12,8},{14,10},{16,20},{18,... | collective-permute-start | bytes 614408 | tf_op jit(solution)/shard_map/ppermute | solution.py:98
  8.5 0.3 collective-permute-start.2
  8.9 0.5 collective-permute-start.5
  9.3 0.9 slice.84
  10.2 0.0 collective-permute-done.refs_1_
  10.3 4.8 %collective-permute-done.1.refs_2_ = f32[2,200,128]{2,1,0:T(8,128)S(1)} collective-permute-done((f32[2,200,128]{2,1,0:T(8,128)}, f32[2,200,128]{2,1,0:T(8,128)S(1)}, u32[]{:S(2)}, u32[]{:S(2)}) %collective-permute-start.1) | collective-permute-done | bytes 204832 | tf_op jit(solution)/shard_map/ppermute | solution.py:98
  15.1 0.0 copy-start
  15.1 0.0 copy-start.3
  15.1 0.0 copy-start.4
  15.2 0.0 copy-start.5
  15.2 3.6 %collective-permute-done.2.refs_3_ = f32[2,200,128]{2,1,0:T(8,128)S(1)} collective-permute-done((f32[2,200,128]{2,1,0:T(8,128)}, f32[2,200,128]{2,1,0:T(8,128)S(1)}, u32[]{:S(2)}, u32[]{:S(2)}) %collective-permute-start.2) | collective-permute-done | bytes 204832 | tf_op jit(solution)/shard_map/ppermute | solution.py:98
  18.8 0.4 collective-permute-start.3
  19.2 15.2 %collective-permute-done.4 = f32[4,200,128]{2,1,0:T(8,128)S(1)} collective-permute-done((f32[4,200,128]{2,1,0:T(8,128)}, f32[4,200,128]{2,1,0:T(8,128)S(1)}, u32[]{:S(2)}, u32[]{:S(2)}) %collective-permute-start.4) | collective-permute-done | bytes 409632 | tf_op jit(solution)/shard_map/ppermute | solution.py:93
  34.4 0.0 collective-permute-done.5
  34.5 0.1 collective-permute-start.6
  34.6 1.6 %collective-permute-start.7 = (f32[2,200,128]{2,1,0:T(8,128)S(1)}, f32[2,200,128]{2,1,0:T(8,128)S(1)}, u32[]{:S(2)}, u32[]{:S(2)}) collective-permute-start(f32[2,200,128]{2,1,0:T(8,128)S(1)} %pad_maximum_fusion.4), channel_id=1, source_target_pairs={{0,4},{2,6},{4,0},{6,2},{8,12},{10,14},{12,8},{14,10},{16,20},{18,... | collective-permute-start | bytes 614408 | tf_op jit(solution)/shard_map/ppermute | solution.py:98
  36.2 0.0 copy-start.1
  36.2 0.4 collective-permute-start.8
  36.6 4.4 %stiff.1 = (f32[168,16,128]{2,1,0:T(8,128)S(1)}, f32[30,16,128]{2,1,0:T(8,128)S(1)}) custom-call(f32[3,81,16,128]{3,2,1,0:T(8,128)S(1)} %bitcast.4, s32[1,128]{1,0:T(1,128)S(1)} %copy-done.4, f32[81,4,81]{2,1,0:T(4,128)S(1)} %bitcast.6, f32[4,128]{1,0:T(4,128)S(1)} %copy-done.5), custom_call_target="tpu_custom_call" | custom-call | flops 1019215872 | bytes 3686400 | tf_op jit(solution)/shard_map/stiff/pallas_call | solution.py:360
  41.1 0.9 %collective-permute-done.3.refs_4_ = f32[4,200,128]{2,1,0:T(8,128)S(1)} collective-permute-done((f32[4,200,128]{2,1,0:T(8,128)S(1)}, f32[4,200,128]{2,1,0:T(8,128)S(1)}, u32[]{:S(2)}, u32[]{:S(2)}) %collective-permute-start.3) | collective-permute-done | bytes 409632 | tf_op jit(solution)/shard_map/ppermute | solution.py:93
  42.0 0.0 collective-permute-done.6.refs_6_
  42.0 0.5 collective-permute-done.7.refs_7_
  42.6 3.6 %collective-permute-done.8.refs_8_ = f32[2,200,128]{2,1,0:T(8,128)S(1)} collective-permute-done((f32[2,200,128]{2,1,0:T(8,128)S(1)}, f32[2,200,128]{2,1,0:T(8,128)S(1)}, u32[]{:S(2)}, u32[]{:S(2)}) %collective-permute-start.8) | collective-permute-done | bytes 204832 | tf_op jit(solution)/shard_map/ppermute | solution.py:98
  46.1 1.1 %spanwise.1 = (f32[4,200,128]{2,1,0:T(8,128)S(1)}, f32[4,200,128]{2,1,0:T(8,128)S(1)}, f32[2,200,128]{2,1,0:T(8,128)S(1)}, f32[2,200,128]{2,1,0:T(8,128)S(1)}, f...) custom-call(f32[2,200,128]{2,1,0:T(8,128)S(1)} %copy-done.2, f32[2,200,128]{2,1,0:T(8,128)S(1)} %collective-permute-done.refs_1_, ...), custom_call_target="tpu_custom_call" | custom-call | flops 629145600 | bytes 3276800 | tf_op jit(solution)/shard_map/spanwise/pallas_call | solution.py:415
  47.2 0.1 collective-permute-start.13
  47.3 0.3 collective-permute-start.9
  47.6 1.5 %collective-permute-start.10 = (f32[2,200,128]{2,1,0:T(8,128)S(1)}, f32[2,200,128]{2,1,0:T(8,128)S(1)}, u32[]{:S(2)}, u32[]{:S(2)}) collective-permute-start(f32[2,200,128]{2,1,0:T(8,128)S(1)} %get-tuple-element.33), channel_id=1, source_target_pairs={{0,4},{2,6},{4,0},{6,2},{8,12},{10,14},{12,8},{14,10},{16,20},{18,... | collective-permute-start | bytes 614408 | tf_op jit(solution)/shard_map/ppermute | solution.py:98
  49.1 0.1 collective-permute-start.11
  49.2 1.9 %collective-permute-start.14 = (f32[4,200,128]{2,1,0:T(8,128)S(1)}, f32[4,200,128]{2,1,0:T(8,128)S(1)}, u32[]{:S(2)}, u32[]{:S(2)}) collective-permute-start(f32[4,200,128]{2,1,0:T(8,128)S(1)} %get-tuple-element.36), channel_id=1, source_target_pairs={{0,24},{2,26},{4,28},{6,30},{8,0},{10,2},{12,4},{14,6},{16,8},{18,... | collective-permute-start | bytes 1228808 | tf_op jit(solution)/shard_map/ppermute | solution.py:93
  51.2 4.3 %collective-permute-done.10.refs_2_ = f32[2,200,128]{2,1,0:T(8,128)S(1)} collective-permute-done((f32[2,200,128]{2,1,0:T(8,128)S(1)}, f32[2,200,128]{2,1,0:T(8,128)S(1)}, u32[]{:S(2)}, u32[]{:S(2)}) %collective-permute-start.10) | collective-permute-done | bytes 204832 | tf_op jit(solution)/shard_map/ppermute | solution.py:98
  55.5 3.1 %collective-permute-done.11.refs_3_ = f32[2,200,128]{2,1,0:T(8,128)S(1)} collective-permute-done((f32[2,200,128]{2,1,0:T(8,128)S(1)}, f32[2,200,128]{2,1,0:T(8,128)S(1)}, u32[]{:S(2)}, u32[]{:S(2)}) %collective-permute-start.11) | collective-permute-done | bytes 204832 | tf_op jit(solution)/shard_map/ppermute | solution.py:98
  58.6 0.1 collective-permute-start.12
  58.7 14.5 %collective-permute-done.13 = f32[4,200,128]{2,1,0:T(8,128)S(1)} collective-permute-done((f32[4,200,128]{2,1,0:T(8,128)S(1)}, f32[4,200,128]{2,1,0:T(8,128)S(1)}, u32[]{:S(2)}, u32[]{:S(2)}) %collective-permute-start.13) | collective-permute-done | bytes 409632 | tf_op jit(solution)/shard_map/ppermute | solution.py:93
  73.4 0.1 collective-permute-start.15
  73.5 1.6 %collective-permute-start.16 = (f32[2,200,128]{2,1,0:T(8,128)S(1)}, f32[2,200,128]{2,1,0:T(8,128)S(1)}, u32[]{:S(2)}, u32[]{:S(2)}) collective-permute-start(f32[2,200,128]{2,1,0:T(8,128)S(1)} %pad_maximum_fusion.8), channel_id=1, source_target_pairs={{0,4},{2,6},{4,0},{6,2},{8,12},{10,14},{12,8},{14,10},{16,20},{18,... | collective-permute-start | bytes 614408 | tf_op jit(solution)/shard_map/ppermute | solution.py:98
  75.1 0.4 collective-permute-start.17
  75.5 0.1 collective-permute-start.19
  75.6 0.0 collective-permute-done.15.refs_6_
  75.6 5.8 %collective-permute-done.16.refs_7_ = f32[2,200,128]{2,1,0:T(8,128)S(1)} collective-permute-done((f32[2,200,128]{2,1,0:T(8,128)S(1)}, f32[2,200,128]{2,1,0:T(8,128)S(1)}, u32[]{:S(2)}, u32[]{:S(2)}) %collective-permute-start.16) | collective-permute-done | bytes 204832 | tf_op jit(solution)/shard_map/ppermute | solution.py:98
  81.4 3.6 %collective-permute-done.17.refs_8_ = f32[2,200,128]{2,1,0:T(8,128)S(1)} collective-permute-done((f32[2,200,128]{2,1,0:T(8,128)S(1)}, f32[2,200,128]{2,1,0:T(8,128)S(1)}, u32[]{:S(2)}, u32[]{:S(2)}) %collective-permute-start.17) | collective-permute-done | bytes 204832 | tf_op jit(solution)/shard_map/ppermute | solution.py:98
  85.0 0.4 totals.1
  85.4 1.6 %collective-permute-start.18 = (f32[4,16,128]{2,1,0:T(8,128)S(1)}, f32[4,16,128]{2,1,0:T(8,128)S(1)}, u32[]{:S(2)}, u32[]{:S(2)}) collective-permute-start(f32[4,16,128]{2,1,0:T(8,128)S(1)} %get-tuple-element.38), channel_id=1, source_target_pairs={{0,1},{1,0},{2,3},{3,2},{4,5},{5,4},{6,7},{7,6},{8,9},{9,8},{10,11... | collective-permute-start | bytes 98312 | tf_op jit(solution)/shard_map/ppermute | solution.py:648
  87.0 1.3 %lower.1.refs_9_ = f32[3,81,16,128]{3,2,1,0:T(8,128)} custom-call(f32[168,16,128]{2,1,0:T(8,128)S(1)} %get-tuple-element.22.u_ref, f32[30,16,128]{2,1,0:T(8,128)S(1)} %get-tuple-element.37.t_ref, s32[1,128]{1,0:T(1,128)S(1)} %copy-done.4, f32[2,200,128]{2,1,0:T(8,128)S(1)} %get-tuple-element.31.refs_0_, f32[2,200,128]{2,1,0:T(8,128)S(1)} %collective-permute-done.9.refs_1_, ...), custom_call_target="tpu_custom_call" | custom-call | tf_op jit(solution)/shard_map/lower/pallas_call | solution.py:631
  88.3 1.1 %collective-permute-done.18.before_ref.after_ref = f32[4,16,128]{2,1,0:T(8,128)S(1)} collective-permute-done((f32[4,16,128]{2,1,0:T(8,128)S(1)}, f32[4,16,128]{2,1,0:T(8,128)S(1)}, u32[]{:S(2)}, u32[]{:S(2)}) %collective-permute-start.18) | collective-permute-done | bytes 32800 | tf_op jit(solution)/shard_map/ppermute | solution.py:648
  89.4 1.6 %upper.1 = f32[3,81,16,128]{3,2,1,0:T(8,128)} custom-call(f32[168,16,128]{2,1,0:T(8,128)S(1)} %get-tuple-element.22.u_ref, f32[30,16,128]{2,1,0:T(8,128)S(1)} %get-tuple-element.37.t_ref, s32[1,128]{1,0:T(1,128)S(1)} %copy-done.4, f32[4,16,128]{2,1,0:T(8,128)S(1)} %collective-permute-done.18.before_ref.after_ref, ...), custom_call_target="tpu_custom_call", output_to_operand_aliasing={{}: (14, {})} | custom-call | tf_op jit(solution)/shard_map/upper/pallas_call | solution.py:631
  (37 shorter events, 0.5 us)
Async XLA Ops:
  5.4 29.0 %collective-permute-start.4 = (f32[4,200,128]{2,1,0:T(8,128)}, f32[4,200,128]{2,1,0:T(8,128)S(1)}, u32[]{:S(2)}, u32[]{:S(2)}) collective-permute-start(f32[4,200,128]{2,1,0:T(8,128)} %get-tuple-element.28), channel_id=1, source_target_pairs={{0,8},{2,10},{4,12},{6,14},{8,16},{10,18},{12,20},{14,22},{16,24},... | collective-permute-start | bytes 1228808 | tf_op jit(solution)/shard_map/ppermute | solution.py:93
  7.0 3.2 %collective-permute-start = (f32[2,200,128]{2,1,0:T(8,128)}, f32[2,200,128]{2,1,0:T(8,128)S(1)}, u32[]{:S(2)}, u32[]{:S(2)}) collective-permute-start(f32[2,200,128]{2,1,0:T(8,128)} %get-tuple-element.25), channel_id=1, source_target_pairs={{0,2},{2,0},{4,6},{6,4},{8,10},{10,8},{12,14},{14,12},{16,18},{18,... | collective-permute-start | bytes 614408 | tf_op jit(solution)/shard_map/ppermute | solution.py:98
  7.0 8.1 %collective-permute-start.1 = (f32[2,200,128]{2,1,0:T(8,128)}, f32[2,200,128]{2,1,0:T(8,128)S(1)}, u32[]{:S(2)}, u32[]{:S(2)}) collective-permute-start(f32[2,200,128]{2,1,0:T(8,128)} %get-tuple-element.26), channel_id=1, source_target_pairs={{0,4},{2,6},{4,0},{6,2},{8,12},{10,14},{12,8},{14,10},{16,20},{18,... | collective-permute-start | bytes 614408 | tf_op jit(solution)/shard_map/ppermute | solution.py:98
  8.5 10.2 %collective-permute-start.2 = (f32[2,200,128]{2,1,0:T(8,128)}, f32[2,200,128]{2,1,0:T(8,128)S(1)}, u32[]{:S(2)}, u32[]{:S(2)}) collective-permute-start(f32[2,200,128]{2,1,0:T(8,128)} %get-tuple-element.27), channel_id=1, source_target_pairs={{0,6},{2,4},{4,2},{6,0},{8,14},{10,12},{12,10},{14,8},{16,22},{18,... | collective-permute-start | bytes 614408 | tf_op jit(solution)/shard_map/ppermute | solution.py:98
  8.9 25.6 %collective-permute-start.5 = (f32[4,200,128]{2,1,0:T(8,128)}, f32[4,200,128]{2,1,0:T(8,128)S(1)}, u32[]{:S(2)}, u32[]{:S(2)}) collective-permute-start(f32[4,200,128]{2,1,0:T(8,128)} %get-tuple-element.29), channel_id=1, source_target_pairs={{0,24},{2,26},{4,28},{6,30},{8,0},{10,2},{12,4},{14,6},{16,8},{18,... | collective-permute-start | bytes 1228808 | tf_op jit(solution)/shard_map/ppermute | solution.py:93
  15.1 21.5 %copy-start = (f32[3,16,81,128]{3,1,2,0:T(8,128)S(1)}, f32[3,16,81,128]{3,1,2,0:T(8,128)}, u32[]{:S(2)}) copy-start(f32[3,16,81,128]{3,1,2,0:T(8,128)} %param.5) | copy-start | bytes 5971972
  15.1 21.5 %copy-start.3 = (f32[4,81,81]{2,0,1:T(4,128)S(1)}, f32[4,81,81]{2,0,1:T(4,128)}, u32[]{:S(2)}) copy-start(f32[4,81,81]{2,0,1:T(4,128)} %param.7) | copy-start | bytes 314932
  15.1 21.5 %copy-start.4 = (s32[1,128]{1,0:T(1,128)S(1)}, s32[1,128]{1,0:T(1,128)}, u32[]{:S(2)}) copy-start(s32[1,128]{1,0:T(1,128)} %slots_ref.3) | copy-start | bytes 1540
  15.2 21.5 %copy-start.5 = (f32[4,128]{1,0:T(4,128)S(1)}, f32[4,128]{1,0:T(4,128)}, u32[]{:S(2)}) copy-start(f32[4,128]{1,0:T(4,128)} %refs_3_.3) | copy-start | bytes 6148
  18.8 23.2 %collective-permute-start.3 = (f32[4,200,128]{2,1,0:T(8,128)S(1)}, f32[4,200,128]{2,1,0:T(8,128)S(1)}, u32[]{:S(2)}, u32[]{:S(2)}) collective-permute-start(f32[4,200,128]{2,1,0:T(8,128)S(1)} %pad_maximum_fusion), channel_id=1, source_target_pairs={{0,16},{2,18},{4,20},{6,22},{8,24},{10,26},{12,28},{14,30},{16,0},... | collective-permute-start | bytes 1228808 | tf_op jit(solution)/shard_map/ppermute | solution.py:93
  34.5 7.5 %collective-permute-start.6 = (f32[2,200,128]{2,1,0:T(8,128)S(1)}, f32[2,200,128]{2,1,0:T(8,128)S(1)}, u32[]{:S(2)}, u32[]{:S(2)}) collective-permute-start(f32[2,200,128]{2,1,0:T(8,128)S(1)} %pad_maximum_fusion.3), channel_id=1, source_target_pairs={{0,2},{2,0},{4,6},{6,4},{8,10},{10,8},{12,14},{14,12},{16,18},{18,... | collective-permute-start | bytes 614408 | tf_op jit(solution)/shard_map/ppermute | solution.py:98
  34.6 7.9 %collective-permute-start.7 = (f32[2,200,128]{2,1,0:T(8,128)S(1)}, f32[2,200,128]{2,1,0:T(8,128)S(1)}, u32[]{:S(2)}, u32[]{:S(2)}) collective-permute-start(f32[2,200,128]{2,1,0:T(8,128)S(1)} %pad_maximum_fusion.4), channel_id=1, source_target_pairs={{0,4},{2,6},{4,0},{6,2},{8,12},{10,14},{12,8},{14,10},{16,20},{18,... | collective-permute-start | bytes 614408 | tf_op jit(solution)/shard_map/ppermute | solution.py:98
  36.2 9.9 %copy-start.1 = (bf16[4,512,256]{2,1,0:T(8,128)(2,1)S(1)}, bf16[4,512,256]{2,1,0:T(8,128)(2,1)}, u32[]{:S(2)}) copy-start(bf16[4,512,256]{2,1,0:T(8,128)(2,1)} %constant.2.clone.refs_9_) | copy-start | bytes 3145732
  36.2 9.9 %copy-start.2 = (f32[2,200,128]{2,1,0:T(8,128)S(1)}, f32[2,200,128]{2,1,0:T(8,128)}, u32[]{:S(2)}) copy-start(f32[2,200,128]{2,1,0:T(8,128)} %get-tuple-element.24.refs_0_) | copy-start | bytes 614404
  36.2 9.9 %collective-permute-start.8 = (f32[2,200,128]{2,1,0:T(8,128)S(1)}, f32[2,200,128]{2,1,0:T(8,128)S(1)}, u32[]{:S(2)}, u32[]{:S(2)}) collective-permute-start(f32[2,200,128]{2,1,0:T(8,128)S(1)} %pad_maximum_fusion.5), channel_id=1, source_target_pairs={{0,6},{2,4},{4,2},{6,0},{8,14},{10,12},{12,10},{14,8},{16,22},{18,... | collective-permute-start | bytes 614408 | tf_op jit(solution)/shard_map/ppermute | solution.py:98
  47.2 26.0 %collective-permute-start.13 = (f32[4,200,128]{2,1,0:T(8,128)S(1)}, f32[4,200,128]{2,1,0:T(8,128)S(1)}, u32[]{:S(2)}, u32[]{:S(2)}) collective-permute-start(f32[4,200,128]{2,1,0:T(8,128)S(1)} %get-tuple-element.35), channel_id=1, source_target_pairs={{0,8},{2,10},{4,12},{6,14},{8,16},{10,18},{12,20},{14,22},{16,24},... | collective-permute-start | bytes 1228808 | tf_op jit(solution)/shard_map/ppermute | solution.py:93
  47.3 3.9 %collective-permute-start.9 = (f32[2,200,128]{2,1,0:T(8,128)S(1)}, f32[2,200,128]{2,1,0:T(8,128)S(1)}, u32[]{:S(2)}, u32[]{:S(2)}) collective-permute-start(f32[2,200,128]{2,1,0:T(8,128)S(1)} %get-tuple-element.32), channel_id=1, source_target_pairs={{0,2},{2,0},{4,6},{6,4},{8,10},{10,8},{12,14},{14,12},{16,18},{18,... | collective-permute-start | bytes 614408 | tf_op jit(solution)/shard_map/ppermute | solution.py:98
  47.6 7.9 %collective-permute-start.10 = (f32[2,200,128]{2,1,0:T(8,128)S(1)}, f32[2,200,128]{2,1,0:T(8,128)S(1)}, u32[]{:S(2)}, u32[]{:S(2)}) collective-permute-start(f32[2,200,128]{2,1,0:T(8,128)S(1)} %get-tuple-element.33), channel_id=1, source_target_pairs={{0,4},{2,6},{4,0},{6,2},{8,12},{10,14},{12,8},{14,10},{16,20},{18,... | collective-permute-start | bytes 614408 | tf_op jit(solution)/shard_map/ppermute | solution.py:98
  49.1 9.5 %collective-permute-start.11 = (f32[2,200,128]{2,1,0:T(8,128)S(1)}, f32[2,200,128]{2,1,0:T(8,128)S(1)}, u32[]{:S(2)}, u32[]{:S(2)}) collective-permute-start(f32[2,200,128]{2,1,0:T(8,128)S(1)} %get-tuple-element.34), channel_id=1, source_target_pairs={{0,6},{2,4},{4,2},{6,0},{8,14},{10,12},{12,10},{14,8},{16,22},{18,... | collective-permute-start | bytes 614408 | tf_op jit(solution)/shard_map/ppermute | solution.py:98
  49.2 24.1 %collective-permute-start.14 = (f32[4,200,128]{2,1,0:T(8,128)S(1)}, f32[4,200,128]{2,1,0:T(8,128)S(1)}, u32[]{:S(2)}, u32[]{:S(2)}) collective-permute-start(f32[4,200,128]{2,1,0:T(8,128)S(1)} %get-tuple-element.36), channel_id=1, source_target_pairs={{0,24},{2,26},{4,28},{6,30},{8,0},{10,2},{12,4},{14,6},{16,8},{18,... | collective-permute-start | bytes 1228808 | tf_op jit(solution)/shard_map/ppermute | solution.py:93
  58.6 17.0 %collective-permute-start.12 = (f32[4,112,128]{2,1,0:T(8,128)S(1)}, f32[4,112,128]{2,1,0:T(8,128)S(1)}, u32[]{:S(2)}, u32[]{:S(2)}) collective-permute-start(f32[4,112,128]{2,1,0:T(8,128)S(1)} %pad_maximum_fusion.1), channel_id=1, source_target_pairs={{0,16},{2,18},{4,20},{6,22},{8,24},{10,26},{12,28},{14,30},{16,0},... | collective-permute-start | bytes 688136 | tf_op jit(solution)/shard_map/ppermute | solution.py:93
  73.4 2.2 %collective-permute-start.15 = (f32[2,200,128]{2,1,0:T(8,128)S(1)}, f32[2,200,128]{2,1,0:T(8,128)S(1)}, u32[]{:S(2)}, u32[]{:S(2)}) collective-permute-start(f32[2,200,128]{2,1,0:T(8,128)S(1)} %pad_maximum_fusion.7), channel_id=1, source_target_pairs={{0,2},{2,0},{4,6},{6,4},{8,10},{10,8},{12,14},{14,12},{16,18},{18,... | collective-permute-start | bytes 614408 | tf_op jit(solution)/shard_map/ppermute | solution.py:98
  73.5 7.9 %collective-permute-start.16 = (f32[2,200,128]{2,1,0:T(8,128)S(1)}, f32[2,200,128]{2,1,0:T(8,128)S(1)}, u32[]{:S(2)}, u32[]{:S(2)}) collective-permute-start(f32[2,200,128]{2,1,0:T(8,128)S(1)} %pad_maximum_fusion.8), channel_id=1, source_target_pairs={{0,4},{2,6},{4,0},{6,2},{8,12},{10,14},{12,8},{14,10},{16,20},{18,... | collective-permute-start | bytes 614408 | tf_op jit(solution)/shard_map/ppermute | solution.py:98
  75.1 9.9 %collective-permute-start.17 = (f32[2,200,128]{2,1,0:T(8,128)S(1)}, f32[2,200,128]{2,1,0:T(8,128)S(1)}, u32[]{:S(2)}, u32[]{:S(2)}) collective-permute-start(f32[2,200,128]{2,1,0:T(8,128)S(1)} %pad_maximum_fusion.9), channel_id=1, source_target_pairs={{0,6},{2,4},{4,2},{6,0},{8,14},{10,12},{12,10},{14,8},{16,22},{18,... | collective-permute-start | bytes 614408 | tf_op jit(solution)/shard_map/ppermute | solution.py:98
  75.5 12.8 %collective-permute-start.19 = (f32[4,88,128]{2,1,0:T(8,128)S(1)}, f32[4,88,128]{2,1,0:T(8,128)S(1)}, u32[]{:S(2)}, u32[]{:S(2)}) collective-permute-start(f32[4,88,128]{2,1,0:T(8,128)S(1)} %pad_maximum_fusion.10), channel_id=1, source_target_pairs={{0,16},{2,18},{4,20},{6,22},{8,24},{10,26},{12,28},{14,30},{16,0},... | collective-permute-start | bytes 540680 | tf_op jit(solution)/shard_map/ppermute | solution.py:93
  85.4 4.0 %collective-permute-start.18 = (f32[4,16,128]{2,1,0:T(8,128)S(1)}, f32[4,16,128]{2,1,0:T(8,128)S(1)}, u32[]{:S(2)}, u32[]{:S(2)}) collective-permute-start(f32[4,16,128]{2,1,0:T(8,128)S(1)} %get-tuple-element.38), channel_id=1, source_target_pairs={{0,1},{1,0},{2,3},{3,2},{4,5},{5,4},{6,7},{7,6},{8,9},{9,8},{10,11... | collective-permute-start | bytes 98312 | tf_op jit(solution)/shard_map/ppermute | solution.py:648

commit v7 on v6

--- a/solution.py
+++ b/solution.py
@@ -241,8 +241,8 @@
     pairs = [(slots_hbm, slots_ref), (geo_hbm, geo_ref), (mats_hbm, mats_ref)]
     pairs += [(vel_hbm.at[c], vel_ref.at[c]) for c in range(3)]
     copies = [pltpu.make_async_copy(*pair, sems.at[k]) for k, pair in enumerate(pairs)]
-    for copy in copies:
-        copy.start()
+    for k in (3, 2, 4, 0, 1, 5):
+        copies[k].start()
     depth = vel_ref.shape[2]
     parts[0][NODES:] = jnp.zeros((TALL + 1 - NODES, depth + 8, LANES), f32)
     sends = []

time: 91.1 us -> 91.1 us (level)
  no operation moved by 1% of the time
where the time goes in v7:
time: 91.1 us; the launch traced here: 90.9 us
  waiting for transfers between devices  61.1 us (67%)
  Pallas kernels  14.1 us (15%)
  starting transfers between devices  14 us (15%)
  local copies, waits for them, and re-layouts  1.12 us (1%)
    ppermute x7, waiting for transfers between devices, onward(): return lax.ppermute(value, 'modes', steps)  30.7 us
    ppermute x12, waiting for transfers between devices, across(): lax.ppermute(value, 'modes', pairs(s))  29.3 us
    pallas_call x2, Pallas kernels, elements(): pl.pallas_call(functools.partial(element_kernel, terms, layout, len(shape...  9.75 us
    ppermute x12, starting transfers between devices, across(): lax.ppermute(value, 'modes', pairs(s))  7.86 us
    ppermute x7, starting transfers between devices, onward(): return lax.ppermute(value, 'modes', steps)  4.62 us
    pallas_call x2, Pallas kernels, expand(): pl.pallas_call(kernel, in_specs=in_specs, out_specs=pl.BlockSpec(memory_s...  2.88 us
  transfers between devices with their start and end apart: 20, of which 12 were waited for; matrix products, arithmetic and copies ran while one was open for 1% of the time, Pallas kernels for 7%

profile of v7, /device:TPU:16, one launch (start us, length us, event | category | flops | bytes accessed | tf_op | source)
XLA Modules:
  0.0 90.9 jit_solution(7582141877352914168)
XLA Ops:
  0.0 5.4 %mass.1 = (f32[4,200,128]{2,1,0:T(8,128)}, f32[4,200,128]{2,1,0:T(8,128)}, f32[2,200,128]{2,1,0:T(8,128)}, f32[2,200,128]{2,1,0:T(8,128)}, f32[2,200,128]{2,1,0:T(8,128)}, /*index=5*/f32[2,200,128]{2,1,0:T(8,128)}) custom-call(f32[3,81,16,128]{3,2,1,0:T(8,128)} %bitcast.3, s32[1,128]{1,0:T(1,128)} %slots_ref.3, f32[81,4,81]{2,1,0:T(4,128)} %bitcast.5, ...), custom_call_target="tpu_custom_call" | custom-call | flops 339738624 | bytes 3686400 | tf_op jit(solution)/shard_map/mass/pallas_call | solution.py:360
  5.4 1.6 %collective-permute-start.4 = (f32[4,200,128]{2,1,0:T(8,128)}, f32[4,200,128]{2,1,0:T(8,128)S(1)}, u32[]{:S(2)}, u32[]{:S(2)}) collective-permute-start(f32[4,200,128]{2,1,0:T(8,128)} %get-tuple-element.28), channel_id=1, source_target_pairs={{0,8},{2,10},{4,12},{6,14},{8,16},{10,18},{12,20},{14,22},{16,24},... | collective-permute-start | bytes 1228808 | tf_op jit(solution)/shard_map/ppermute | solution.py:93
  7.0 0.0 collective-permute-start
  7.0 1.5 %collective-permute-start.1 = (f32[2,200,128]{2,1,0:T(8,128)}, f32[2,200,128]{2,1,0:T(8,128)S(1)}, u32[]{:S(2)}, u32[]{:S(2)}) collective-permute-start(f32[2,200,128]{2,1,0:T(8,128)} %get-tuple-element.26), channel_id=1, source_target_pairs={{0,4},{2,6},{4,0},{6,2},{8,12},{10,14},{12,8},{14,10},{16,20},{18,... | collective-permute-start | bytes 614408 | tf_op jit(solution)/shard_map/ppermute | solution.py:98
  8.5 0.3 collective-permute-start.2
  8.9 0.4 collective-permute-start.5
  9.3 0.9 slice.84
  10.2 0.0 collective-permute-done.refs_1_
  10.2 4.9 %collective-permute-done.1.refs_2_ = f32[2,200,128]{2,1,0:T(8,128)S(1)} collective-permute-done((f32[2,200,128]{2,1,0:T(8,128)}, f32[2,200,128]{2,1,0:T(8,128)S(1)}, u32[]{:S(2)}, u32[]{:S(2)}) %collective-permute-start.1) | collective-permute-done | bytes 204832 | tf_op jit(solution)/shard_map/ppermute | solution.py:98
  15.1 0.0 copy-start
  15.1 0.0 copy-start.3
  15.1 0.0 copy-start.4
  15.1 0.0 copy-start.5
  15.1 3.6 %collective-permute-done.2.refs_3_ = f32[2,200,128]{2,1,0:T(8,128)S(1)} collective-permute-done((f32[2,200,128]{2,1,0:T(8,128)}, f32[2,200,128]{2,1,0:T(8,128)S(1)}, u32[]{:S(2)}, u32[]{:S(2)}) %collective-permute-start.2) | collective-permute-done | bytes 204832 | tf_op jit(solution)/shard_map/ppermute | solution.py:98
  18.8 0.4 collective-permute-start.3
  19.2 15.2 %collective-permute-done.4 = f32[4,200,128]{2,1,0:T(8,128)S(1)} collective-permute-done((f32[4,200,128]{2,1,0:T(8,128)}, f32[4,200,128]{2,1,0:T(8,128)S(1)}, u32[]{:S(2)}, u32[]{:S(2)}) %collective-permute-start.4) | collective-permute-done | bytes 409632 | tf_op jit(solution)/shard_map/ppermute | solution.py:93
  34.4 0.0 collective-permute-done.5
  34.5 0.1 collective-permute-start.6
  34.6 1.6 %collective-permute-start.7 = (f32[2,200,128]{2,1,0:T(8,128)S(1)}, f32[2,200,128]{2,1,0:T(8,128)S(1)}, u32[]{:S(2)}, u32[]{:S(2)}) collective-permute-start(f32[2,200,128]{2,1,0:T(8,128)S(1)} %pad_maximum_fusion.4), channel_id=1, source_target_pairs={{0,4},{2,6},{4,0},{6,2},{8,12},{10,14},{12,8},{14,10},{16,20},{18,... | collective-permute-start | bytes 614408 | tf_op jit(solution)/shard_map/ppermute | solution.py:98
  36.2 0.0 copy-start.1
  36.2 0.4 collective-permute-start.8
  36.6 4.4 %stiff.1 = (f32[168,16,128]{2,1,0:T(8,128)S(1)}, f32[30,16,128]{2,1,0:T(8,128)S(1)}) custom-call(f32[3,81,16,128]{3,2,1,0:T(8,128)S(1)} %bitcast.4, s32[1,128]{1,0:T(1,128)S(1)} %copy-done.4, f32[81,4,81]{2,1,0:T(4,128)S(1)} %bitcast.6, f32[4,128]{1,0:T(4,128)S(1)} %copy-done.5), custom_call_target="tpu_custom_call" | custom-call | flops 1019215872 | bytes 3686400 | tf_op jit(solution)/shard_map/stiff/pallas_call | solution.py:360
  41.1 0.9 %collective-permute-done.3.refs_4_ = f32[4,200,128]{2,1,0:T(8,128)S(1)} collective-permute-done((f32[4,200,128]{2,1,0:T(8,128)S(1)}, f32[4,200,128]{2,1,0:T(8,128)S(1)}, u32[]{:S(2)}, u32[]{:S(2)}) %collective-permute-start.3) | collective-permute-done | bytes 409632 | tf_op jit(solution)/shard_map/ppermute | solution.py:93
  42.0 0.5 collective-permute-done.7.refs_7_
  42.5 3.6 %collective-permute-done.8.refs_8_ = f32[2,200,128]{2,1,0:T(8,128)S(1)} collective-permute-done((f32[2,200,128]{2,1,0:T(8,128)S(1)}, f32[2,200,128]{2,1,0:T(8,128)S(1)}, u32[]{:S(2)}, u32[]{:S(2)}) %collective-permute-start.8) | collective-permute-done | bytes 204832 | tf_op jit(solution)/shard_map/ppermute | solution.py:98
  46.1 1.1 %spanwise.1 = (f32[4,200,128]{2,1,0:T(8,128)S(1)}, f32[4,200,128]{2,1,0:T(8,128)S(1)}, f32[2,200,128]{2,1,0:T(8,128)S(1)}, f32[2,200,128]{2,1,0:T(8,128)S(1)}, f...) custom-call(f32[2,200,128]{2,1,0:T(8,128)S(1)} %copy-done.2, f32[2,200,128]{2,1,0:T(8,128)S(1)} %collective-permute-done.refs_1_, ...), custom_call_target="tpu_custom_call" | custom-call | flops 629145600 | bytes 3276800 | tf_op jit(solution)/shard_map/spanwise/pallas_call | solution.py:415
  47.2 0.1 collective-permute-start.13
  47.2 0.3 collective-permute-start.9
  47.5 1.5 %collective-permute-start.10 = (f32[2,200,128]{2,1,0:T(8,128)S(1)}, f32[2,200,128]{2,1,0:T(8,128)S(1)}, u32[]{:S(2)}, u32[]{:S(2)}) collective-permute-start(f32[2,200,128]{2,1,0:T(8,128)S(1)} %get-tuple-element.33), channel_id=1, source_target_pairs={{0,4},{2,6},{4,0},{6,2},{8,12},{10,14},{12,8},{14,10},{16,20},{18,... | collective-permute-start | bytes 614408 | tf_op jit(solution)/shard_map/ppermute | solution.py:98
  49.1 0.1 collective-permute-start.11
  49.2 1.9 %collective-permute-start.14 = (f32[4,200,128]{2,1,0:T(8,128)S(1)}, f32[4,200,128]{2,1,0:T(8,128)S(1)}, u32[]{:S(2)}, u32[]{:S(2)}) collective-permute-start(f32[4,200,128]{2,1,0:T(8,128)S(1)} %get-tuple-element.36), channel_id=1, source_target_pairs={{0,24},{2,26},{4,28},{6,30},{8,0},{10,2},{12,4},{14,6},{16,8},{18,... | collective-permute-start | bytes 1228808 | tf_op jit(solution)/shard_map/ppermute | solution.py:93
  51.2 4.3 %collective-permute-done.10.refs_2_ = f32[2,200,128]{2,1,0:T(8,128)S(1)} collective-permute-done((f32[2,200,128]{2,1,0:T(8,128)S(1)}, f32[2,200,128]{2,1,0:T(8,128)S(1)}, u32[]{:S(2)}, u32[]{:S(2)}) %collective-permute-start.10) | collective-permute-done | bytes 204832 | tf_op jit(solution)/shard_map/ppermute | solution.py:98
  55.4 3.1 %collective-permute-done.11.refs_3_ = f32[2,200,128]{2,1,0:T(8,128)S(1)} collective-permute-done((f32[2,200,128]{2,1,0:T(8,128)S(1)}, f32[2,200,128]{2,1,0:T(8,128)S(1)}, u32[]{:S(2)}, u32[]{:S(2)}) %collective-permute-start.11) | collective-permute-done | bytes 204832 | tf_op jit(solution)/shard_map/ppermute | solution.py:98
  58.6 0.1 collective-permute-start.12
  58.7 14.5 %collective-permute-done.13 = f32[4,200,128]{2,1,0:T(8,128)S(1)} collective-permute-done((f32[4,200,128]{2,1,0:T(8,128)S(1)}, f32[4,200,128]{2,1,0:T(8,128)S(1)}, u32[]{:S(2)}, u32[]{:S(2)}) %collective-permute-start.13) | collective-permute-done | bytes 409632 | tf_op jit(solution)/shard_map/ppermute | solution.py:93
  73.3 0.1 collective-permute-start.15
  73.4 1.6 %collective-permute-start.16 = (f32[2,200,128]{2,1,0:T(8,128)S(1)}, f32[2,200,128]{2,1,0:T(8,128)S(1)}, u32[]{:S(2)}, u32[]{:S(2)}) collective-permute-start(f32[2,200,128]{2,1,0:T(8,128)S(1)} %pad_maximum_fusion.8), channel_id=1, source_target_pairs={{0,4},{2,6},{4,0},{6,2},{8,12},{10,14},{12,8},{14,10},{16,20},{18,... | collective-permute-start | bytes 614408 | tf_op jit(solution)/shard_map/ppermute | solution.py:98
  75.0 0.4 collective-permute-start.17
  75.4 0.1 collective-permute-start.19
  75.5 0.0 collective-permute-done.15.refs_6_
  75.6 5.8 %collective-permute-done.16.refs_7_ = f32[2,200,128]{2,1,0:T(8,128)S(1)} collective-permute-done((f32[2,200,128]{2,1,0:T(8,128)S(1)}, f32[2,200,128]{2,1,0:T(8,128)S(1)}, u32[]{:S(2)}, u32[]{:S(2)}) %collective-permute-start.16) | collective-permute-done | bytes 204832 | tf_op jit(solution)/shard_map/ppermute | solution.py:98
  81.4 3.6 %collective-permute-done.17.refs_8_ = f32[2,200,128]{2,1,0:T(8,128)S(1)} collective-permute-done((f32[2,200,128]{2,1,0:T(8,128)S(1)}, f32[2,200,128]{2,1,0:T(8,128)S(1)}, u32[]{:S(2)}, u32[]{:S(2)}) %collective-permute-start.17) | collective-permute-done | bytes 204832 | tf_op jit(solution)/shard_map/ppermute | solution.py:98
  84.9 0.4 totals.1
  85.4 1.6 %collective-permute-start.18 = (f32[4,16,128]{2,1,0:T(8,128)S(1)}, f32[4,16,128]{2,1,0:T(8,128)S(1)}, u32[]{:S(2)}, u32[]{:S(2)}) collective-permute-start(f32[4,16,128]{2,1,0:T(8,128)S(1)} %get-tuple-element.38), channel_id=1, source_target_pairs={{0,1},{1,0},{2,3},{3,2},{4,5},{5,4},{6,7},{7,6},{8,9},{9,8},{10,11... | collective-permute-start | bytes 98312 | tf_op jit(solution)/shard_map/ppermute | solution.py:648
  86.9 1.3 %lower.1.refs_9_ = f32[3,81,16,128]{3,2,1,0:T(8,128)} custom-call(f32[168,16,128]{2,1,0:T(8,128)S(1)} %get-tuple-element.22.u_ref, f32[30,16,128]{2,1,0:T(8,128)S(1)} %get-tuple-element.37.t_ref, s32[1,128]{1,0:T(1,128)S(1)} %copy-done.4, f32[2,200,128]{2,1,0:T(8,128)S(1)} %get-tuple-element.31.refs_0_, f32[2,200,128]{2,1,0:T(8,128)S(1)} %collective-permute-done.9.refs_1_, ...), custom_call_target="tpu_custom_call" | custom-call | tf_op jit(solution)/shard_map/lower/pallas_call | solution.py:631
  88.2 0.0 collective-permute-done.19.refs_4_
  88.2 1.1 %collective-permute-done.18.before_ref.after_ref = f32[4,16,128]{2,1,0:T(8,128)S(1)} collective-permute-done((f32[4,16,128]{2,1,0:T(8,128)S(1)}, f32[4,16,128]{2,1,0:T(8,128)S(1)}, u32[]{:S(2)}, u32[]{:S(2)}) %collective-permute-start.18) | collective-permute-done | bytes 32800 | tf_op jit(solution)/shard_map/ppermute | solution.py:648
  89.3 1.6 %upper.1 = f32[3,81,16,128]{3,2,1,0:T(8,128)} custom-call(f32[168,16,128]{2,1,0:T(8,128)S(1)} %get-tuple-element.22.u_ref, f32[30,16,128]{2,1,0:T(8,128)S(1)} %get-tuple-element.37.t_ref, s32[1,128]{1,0:T(1,128)S(1)} %copy-done.4, f32[4,16,128]{2,1,0:T(8,128)S(1)} %collective-permute-done.18.before_ref.after_ref, ...), custom_call_target="tpu_custom_call", output_to_operand_aliasing={{}: (14, {})} | custom-call | tf_op jit(solution)/shard_map/upper/pallas_call | solution.py:631
  (37 shorter events, 0.5 us)
Async XLA Ops:
  5.4 29.0 %collective-permute-start.4 = (f32[4,200,128]{2,1,0:T(8,128)}, f32[4,200,128]{2,1,0:T(8,128)S(1)}, u32[]{:S(2)}, u32[]{:S(2)}) collective-permute-start(f32[4,200,128]{2,1,0:T(8,128)} %get-tuple-element.28), channel_id=1, source_target_pairs={{0,8},{2,10},{4,12},{6,14},{8,16},{10,18},{12,20},{14,22},{16,24},... | collective-permute-start | bytes 1228808 | tf_op jit(solution)/shard_map/ppermute | solution.py:93
  7.0 3.2 %collective-permute-start = (f32[2,200,128]{2,1,0:T(8,128)}, f32[2,200,128]{2,1,0:T(8,128)S(1)}, u32[]{:S(2)}, u32[]{:S(2)}) collective-permute-start(f32[2,200,128]{2,1,0:T(8,128)} %get-tuple-element.25), channel_id=1, source_target_pairs={{0,2},{2,0},{4,6},{6,4},{8,10},{10,8},{12,14},{14,12},{16,18},{18,... | collective-permute-start | bytes 614408 | tf_op jit(solution)/shard_map/ppermute | solution.py:98
  7.0 8.1 %collective-permute-start.1 = (f32[2,200,128]{2,1,0:T(8,128)}, f32[2,200,128]{2,1,0:T(8,128)S(1)}, u32[]{:S(2)}, u32[]{:S(2)}) collective-permute-start(f32[2,200,128]{2,1,0:T(8,128)} %get-tuple-element.26), channel_id=1, source_target_pairs={{0,4},{2,6},{4,0},{6,2},{8,12},{10,14},{12,8},{14,10},{16,20},{18,... | collective-permute-start | bytes 614408 | tf_op jit(solution)/shard_map/ppermute | solution.py:98
  8.5 10.2 %collective-permute-start.2 = (f32[2,200,128]{2,1,0:T(8,128)}, f32[2,200,128]{2,1,0:T(8,128)S(1)}, u32[]{:S(2)}, u32[]{:S(2)}) collective-permute-start(f32[2,200,128]{2,1,0:T(8,128)} %get-tuple-element.27), channel_id=1, source_target_pairs={{0,6},{2,4},{4,2},{6,0},{8,14},{10,12},{12,10},{14,8},{16,22},{18,... | collective-permute-start | bytes 614408 | tf_op jit(solution)/shard_map/ppermute | solution.py:98
  8.9 25.6 %collective-permute-start.5 = (f32[4,200,128]{2,1,0:T(8,128)}, f32[4,200,128]{2,1,0:T(8,128)S(1)}, u32[]{:S(2)}, u32[]{:S(2)}) collective-permute-start(f32[4,200,128]{2,1,0:T(8,128)} %get-tuple-element.29), channel_id=1, source_target_pairs={{0,24},{2,26},{4,28},{6,30},{8,0},{10,2},{12,4},{14,6},{16,8},{18,... | collective-permute-start | bytes 1228808 | tf_op jit(solution)/shard_map/ppermute | solution.py:93
  15.1 21.5 %copy-start = (f32[3,16,81,128]{3,1,2,0:T(8,128)S(1)}, f32[3,16,81,128]{3,1,2,0:T(8,128)}, u32[]{:S(2)}) copy-start(f32[3,16,81,128]{3,1,2,0:T(8,128)} %param.5) | copy-start | bytes 5971972
  15.1 21.5 %copy-start.3 = (f32[4,81,81]{2,0,1:T(4,128)S(1)}, f32[4,81,81]{2,0,1:T(4,128)}, u32[]{:S(2)}) copy-start(f32[4,81,81]{2,0,1:T(4,128)} %param.7) | copy-start | bytes 314932
  15.1 21.5 %copy-start.4 = (s32[1,128]{1,0:T(1,128)S(1)}, s32[1,128]{1,0:T(1,128)}, u32[]{:S(2)}) copy-start(s32[1,128]{1,0:T(1,128)} %slots_ref.3) | copy-start | bytes 1540
  15.1 21.5 %copy-start.5 = (f32[4,128]{1,0:T(4,128)S(1)}, f32[4,128]{1,0:T(4,128)}, u32[]{:S(2)}) copy-start(f32[4,128]{1,0:T(4,128)} %refs_3_.3) | copy-start | bytes 6148
  18.8 23.2 %collective-permute-start.3 = (f32[4,200,128]{2,1,0:T(8,128)S(1)}, f32[4,200,128]{2,1,0:T(8,128)S(1)}, u32[]{:S(2)}, u32[]{:S(2)}) collective-permute-start(f32[4,200,128]{2,1,0:T(8,128)S(1)} %pad_maximum_fusion), channel_id=1, source_target_pairs={{0,16},{2,18},{4,20},{6,22},{8,24},{10,26},{12,28},{14,30},{16,0},... | collective-permute-start | bytes 1228808 | tf_op jit(solution)/shard_map/ppermute | solution.py:93
  34.5 7.5 %collective-permute-start.6 = (f32[2,200,128]{2,1,0:T(8,128)S(1)}, f32[2,200,128]{2,1,0:T(8,128)S(1)}, u32[]{:S(2)}, u32[]{:S(2)}) collective-permute-start(f32[2,200,128]{2,1,0:T(8,128)S(1)} %pad_maximum_fusion.3), channel_id=1, source_target_pairs={{0,2},{2,0},{4,6},{6,4},{8,10},{10,8},{12,14},{14,12},{16,18},{18,... | collective-permute-start | bytes 614408 | tf_op jit(solution)/shard_map/ppermute | solution.py:98
  34.6 7.9 %collective-permute-start.7 = (f32[2,200,128]{2,1,0:T(8,128)S(1)}, f32[2,200,128]{2,1,0:T(8,128)S(1)}, u32[]{:S(2)}, u32[]{:S(2)}) collective-permute-start(f32[2,200,128]{2,1,0:T(8,128)S(1)} %pad_maximum_fusion.4), channel_id=1, source_target_pairs={{0,4},{2,6},{4,0},{6,2},{8,12},{10,14},{12,8},{14,10},{16,20},{18,... | collective-permute-start | bytes 614408 | tf_op jit(solution)/shard_map/ppermute | solution.py:98
  36.2 9.9 %copy-start.1 = (bf16[4,512,256]{2,1,0:T(8,128)(2,1)S(1)}, bf16[4,512,256]{2,1,0:T(8,128)(2,1)}, u32[]{:S(2)}) copy-start(bf16[4,512,256]{2,1,0:T(8,128)(2,1)} %constant.2.clone.refs_9_) | copy-start | bytes 3145732
  36.2 9.9 %copy-start.2 = (f32[2,200,128]{2,1,0:T(8,128)S(1)}, f32[2,200,128]{2,1,0:T(8,128)}, u32[]{:S(2)}) copy-start(f32[2,200,128]{2,1,0:T(8,128)} %get-tuple-element.24.refs_0_) | copy-start | bytes 614404
  36.2 9.9 %collective-permute-start.8 = (f32[2,200,128]{2,1,0:T(8,128)S(1)}, f32[2,200,128]{2,1,0:T(8,128)S(1)}, u32[]{:S(2)}, u32[]{:S(2)}) collective-permute-start(f32[2,200,128]{2,1,0:T(8,128)S(1)} %pad_maximum_fusion.5), channel_id=1, source_target_pairs={{0,6},{2,4},{4,2},{6,0},{8,14},{10,12},{12,10},{14,8},{16,22},{18,... | collective-permute-start | bytes 614408 | tf_op jit(solution)/shard_map/ppermute | solution.py:98
  47.2 26.0 %collective-permute-start.13 = (f32[4,200,128]{2,1,0:T(8,128)S(1)}, f32[4,200,128]{2,1,0:T(8,128)S(1)}, u32[]{:S(2)}, u32[]{:S(2)}) collective-permute-start(f32[4,200,128]{2,1,0:T(8,128)S(1)} %get-tuple-element.35), channel_id=1, source_target_pairs={{0,8},{2,10},{4,12},{6,14},{8,16},{10,18},{12,20},{14,22},{16,24},... | collective-permute-start | bytes 1228808 | tf_op jit(solution)/shard_map/ppermute | solution.py:93
  47.2 3.9 %collective-permute-start.9 = (f32[2,200,128]{2,1,0:T(8,128)S(1)}, f32[2,200,128]{2,1,0:T(8,128)S(1)}, u32[]{:S(2)}, u32[]{:S(2)}) collective-permute-start(f32[2,200,128]{2,1,0:T(8,128)S(1)} %get-tuple-element.32), channel_id=1, source_target_pairs={{0,2},{2,0},{4,6},{6,4},{8,10},{10,8},{12,14},{14,12},{16,18},{18,... | collective-permute-start | bytes 614408 | tf_op jit(solution)/shard_map/ppermute | solution.py:98
  47.5 7.9 %collective-permute-start.10 = (f32[2,200,128]{2,1,0:T(8,128)S(1)}, f32[2,200,128]{2,1,0:T(8,128)S(1)}, u32[]{:S(2)}, u32[]{:S(2)}) collective-permute-start(f32[2,200,128]{2,1,0:T(8,128)S(1)} %get-tuple-element.33), channel_id=1, source_target_pairs={{0,4},{2,6},{4,0},{6,2},{8,12},{10,14},{12,8},{14,10},{16,20},{18,... | collective-permute-start | bytes 614408 | tf_op jit(solution)/shard_map/ppermute | solution.py:98
  49.1 9.5 %collective-permute-start.11 = (f32[2,200,128]{2,1,0:T(8,128)S(1)}, f32[2,200,128]{2,1,0:T(8,128)S(1)}, u32[]{:S(2)}, u32[]{:S(2)}) collective-permute-start(f32[2,200,128]{2,1,0:T(8,128)S(1)} %get-tuple-element.34), channel_id=1, source_target_pairs={{0,6},{2,4},{4,2},{6,0},{8,14},{10,12},{12,10},{14,8},{16,22},{18,... | collective-permute-start | bytes 614408 | tf_op jit(solution)/shard_map/ppermute | solution.py:98
  49.2 24.1 %collective-permute-start.14 = (f32[4,200,128]{2,1,0:T(8,128)S(1)}, f32[4,200,128]{2,1,0:T(8,128)S(1)}, u32[]{:S(2)}, u32[]{:S(2)}) collective-permute-start(f32[4,200,128]{2,1,0:T(8,128)S(1)} %get-tuple-element.36), channel_id=1, source_target_pairs={{0,24},{2,26},{4,28},{6,30},{8,0},{10,2},{12,4},{14,6},{16,8},{18,... | collective-permute-start | bytes 1228808 | tf_op jit(solution)/shard_map/ppermute | solution.py:93
  58.6 17.0 %collective-permute-start.12 = (f32[4,112,128]{2,1,0:T(8,128)S(1)}, f32[4,112,128]{2,1,0:T(8,128)S(1)}, u32[]{:S(2)}, u32[]{:S(2)}) collective-permute-start(f32[4,112,128]{2,1,0:T(8,128)S(1)} %pad_maximum_fusion.1), channel_id=1, source_target_pairs={{0,16},{2,18},{4,20},{6,22},{8,24},{10,26},{12,28},{14,30},{16,0},... | collective-permute-start | bytes 688136 | tf_op jit(solution)/shard_map/ppermute | solution.py:93
  73.3 2.2 %collective-permute-start.15 = (f32[2,200,128]{2,1,0:T(8,128)S(1)}, f32[2,200,128]{2,1,0:T(8,128)S(1)}, u32[]{:S(2)}, u32[]{:S(2)}) collective-permute-start(f32[2,200,128]{2,1,0:T(8,128)S(1)} %pad_maximum_fusion.7), channel_id=1, source_target_pairs={{0,2},{2,0},{4,6},{6,4},{8,10},{10,8},{12,14},{14,12},{16,18},{18,... | collective-permute-start | bytes 614408 | tf_op jit(solution)/shard_map/ppermute | solution.py:98
  73.4 7.9 %collective-permute-start.16 = (f32[2,200,128]{2,1,0:T(8,128)S(1)}, f32[2,200,128]{2,1,0:T(8,128)S(1)}, u32[]{:S(2)}, u32[]{:S(2)}) collective-permute-start(f32[2,200,128]{2,1,0:T(8,128)S(1)} %pad_maximum_fusion.8), channel_id=1, source_target_pairs={{0,4},{2,6},{4,0},{6,2},{8,12},{10,14},{12,8},{14,10},{16,20},{18,... | collective-permute-start | bytes 614408 | tf_op jit(solution)/shard_map/ppermute | solution.py:98
  75.0 9.9 %collective-permute-start.17 = (f32[2,200,128]{2,1,0:T(8,128)S(1)}, f32[2,200,128]{2,1,0:T(8,128)S(1)}, u32[]{:S(2)}, u32[]{:S(2)}) collective-permute-start(f32[2,200,128]{2,1,0:T(8,128)S(1)} %pad_maximum_fusion.9), channel_id=1, source_target_pairs={{0,6},{2,4},{4,2},{6,0},{8,14},{10,12},{12,10},{14,8},{16,22},{18,... | collective-permute-start | bytes 614408 | tf_op jit(solution)/shard_map/ppermute | solution.py:98
  75.4 12.8 %collective-permute-start.19 = (f32[4,88,128]{2,1,0:T(8,128)S(1)}, f32[4,88,128]{2,1,0:T(8,128)S(1)}, u32[]{:S(2)}, u32[]{:S(2)}) collective-permute-start(f32[4,88,128]{2,1,0:T(8,128)S(1)} %pad_maximum_fusion.10), channel_id=1, source_target_pairs={{0,16},{2,18},{4,20},{6,22},{8,24},{10,26},{12,28},{14,30},{16,0},... | collective-permute-start | bytes 540680 | tf_op jit(solution)/shard_map/ppermute | solution.py:93
  85.4 4.0 %collective-permute-start.18 = (f32[4,16,128]{2,1,0:T(8,128)S(1)}, f32[4,16,128]{2,1,0:T(8,128)S(1)}, u32[]{:S(2)}, u32[]{:S(2)}) collective-permute-start(f32[4,16,128]{2,1,0:T(8,128)S(1)} %get-tuple-element.38), channel_id=1, source_target_pairs={{0,1},{1,0},{2,3},{3,2},{4,5},{5,4},{6,7},{7,6},{8,9},{9,8},{10,11... | collective-permute-start | bytes 98312 | tf_op jit(solution)/shard_map/ppermute | solution.py:648
